TPU v7x, 32 devices: a whole 2x2x4 slice. The times are simulated.
32 devices in a mesh: img: 8 (over y, x, core), blk: 4 (over z).
Axes of the slice: x: 2, y: 2, z: 4, core: 2. Of those that a mesh axis runs over, the one named last changes fastest.
Arguments:
- inputs: bfloat16 [16384, 1152], P(('img', 'blk')), may hold values from -6 to 6
- token_image: int32 [16384], P(('img', 'blk')), may hold values from 0 to 7, as said below
- image_time: int32 [64], replicated, may hold values from 0 to 999
- image_class: int32 [64], replicated, may hold values from 0 to 1000
- targets: bfloat16 [16384, 768], P(('img', 'blk')), may hold values from -6 to 6
- cotangent: bfloat16 [16384, 1152], P(('img', 'blk')), may hold values from -6 to 6
- class_table: bfloat16 [1001, 1152], P(None, 'img'), may hold values from -6 to 6
- modulate_weight: bfloat16 [1152, 6912], P('img'), may hold values from -0.1875 to 0.1875
- modulate_bias: bfloat16 [6912], replicated, may hold values from -4 to 4
- attend_weight: bfloat16 [1152, 3456], P('img'), may hold values from -0.1875 to 0.1875
- attend_bias: bfloat16 [2304], P('img'), may hold values from -3 to 3
- output_weight: bfloat16 [1152, 1152], P('img'), may hold values from -1.5 to 1.5
- output_bias: bfloat16 [1152], P('img'), may hold values from -3 to 3
- expand_weight: bfloat16 [1152, 4608], P('img'), may hold values from -0.1875 to 0.1875
- expand_bias: bfloat16 [4608], P('img'), may hold values from -3 to 3
- shrink_weight: bfloat16 [4608, 1152], P('img'), may hold values from -0.09375 to 0.09375
- shrink_bias: bfloat16 [1152], P('img'), may hold values from -3 to 3
- inner_weight: bfloat16 [1152, 2048], P('img'), may hold values from -0.1875 to 0.1875
- inner_bias: bfloat16 [2048], P('img'), may hold values from -3 to 3
- middle_weight: bfloat16 [2048, 2048], P('img'), may hold values from -0.125 to 0.125
- middle_bias: bfloat16 [2048], P('img'), may hold values from -3 to 3
- outer_weight: bfloat16 [2048, 768], P('img'), may hold values from -0.125 to 0.125
- outer_bias: bfloat16 [768], P('img'), may hold values from -4 to 4
Outputs:
- block_output: bfloat16 [16384, 1152], P(('img', 'blk'))
- input_gradient: bfloat16 [16384, 1152], P(('img', 'blk'))
- table_gradient: float32 [1001, 1152], P(None, 'img')
- modulate_weight_gradient: float32 [1152, 6912], P('img')
- modulate_bias_gradient: float32 [6912], replicated
- attend_weight_gradient: float32 [1152, 3456], P('img')
- attend_bias_gradient: float32 [2304], P('img')
- output_weight_gradient: float32 [1152, 1152], P('img')
- output_bias_gradient: float32 [1152], P('img')
- expand_weight_gradient: float32 [1152, 4608], P('img')
- expand_bias_gradient: float32 [4608], P('img')
- shrink_weight_gradient: float32 [4608, 1152], P('img')
- shrink_bias_gradient: float32 [1152], P('img')
- inner_weight_gradient: float32 [1152, 2048], P('img')
- inner_bias_gradient: float32 [2048], P('img')
- middle_weight_gradient: float32 [2048, 2048], P('img')
- middle_bias_gradient: float32 [2048], P('img')
- outer_weight_gradient: float32 [2048, 768], P('img')
- outer_bias_gradient: float32 [768], P('img')
Inputs may be any that keep to these rules, and one draw needn't show every extreme that they name: `token_image`: within an image group every device of blk holds the same layout: each of the group's images (of 1024 or 256 tokens) owns one run of consecutive rows, an equal share of its tokens on every device of the group; slots are numbered 0, 1, ... in row order, every row belongs to an image, and slots past a group's count of images are unused.
All inputs are finite; a program needn't handle non-finite values.
Results may differ from a plain program's by a relative error of at most 0.025.
Values may be sent and summed in bfloat16 or wider, within the bound.
A program may use at most 384 MiB of HBM per device.

v0:
```python
from functools import partial
import math

import jax
import jax.numpy as jnp
from jax import lax
from jax.sharding import PartitionSpec as P

HEADS = 16


EPSILON = 1e-06
HIGH = lax.Precision.HIGHEST
NEGATIVE = -1e30


def layer_norm(values):
    mean = jnp.mean(values, axis=-1, keepdims=True)
    centered = values - mean
    variance = jnp.mean(centered * centered, axis=-1, keepdims=True)
    inverse = lax.rsqrt(variance + EPSILON)
    return (centered * inverse, inverse)


def norm_back(grad, normal, inverse):
    mean_grad = jnp.mean(grad, axis=-1, keepdims=True)
    mean_cross = jnp.mean(grad * normal, axis=-1, keepdims=True)
    return inverse * (grad - mean_grad - normal * mean_cross)


def local_back(function, point, grad):
    return jax.vjp(function, point)[1](grad)[0]


def left_product(left, right):
    return jnp.einsum("ti,to->io", left, right, preferred_element_type=jnp.float32)


def right_product(grad, weight):
    return jnp.einsum("to,io->ti", grad, weight, preferred_element_type=jnp.float32)


def column_sum(values):
    return jnp.sum(values.astype(jnp.float32), axis=0)


def score_block(query_heads, key_block, query_labels, key_labels, scale):
    scores = (
        jnp.einsum("qhd,khd->hqk", query_heads, key_block, preferred_element_type=jnp.float32)
        * scale
    )
    mask = (query_labels[:, None] == key_labels[None, :])[None]
    return (scores, mask)


def attend_forward(query_heads, query_labels, key_blocks, value_blocks, label_blocks, scale):
    count, heads = (query_heads.shape[0], query_heads.shape[1])

    def stats_step(carry, block):
        top, total = carry
        scores, mask = score_block(query_heads, block[0], query_labels, block[1], scale)
        masked = jnp.where(mask, scores, NEGATIVE)
        new_top = jnp.maximum(top, jnp.max(masked, axis=2))
        fresh = jnp.where(mask, jnp.exp(masked - new_top[:, :, None]), 0.0)
        return ((new_top, total * jnp.exp(top - new_top) + jnp.sum(fresh, axis=2)), None)

    start = (
        jnp.full((heads, count), NEGATIVE, jnp.float32),
        jnp.zeros((heads, count), jnp.float32),
    )
    (top, total), unused = lax.scan(stats_step, start, (key_blocks, label_blocks))
    log_total = top + jnp.log(total)

    def value_step(running, block):
        scores, mask = score_block(query_heads, block[0], query_labels, block[2], scale)
        chance = jnp.where(mask, jnp.exp(scores - log_total[:, :, None]), 0.0).astype(jnp.bfloat16)
        return (
            running
            + jnp.einsum("hqk,khd->qhd", chance, block[1], preferred_element_type=jnp.float32),
            None,
        )

    attended, unused = lax.scan(
        value_step,
        jnp.zeros(query_heads.shape, jnp.float32),
        (key_blocks, value_blocks, label_blocks),
    )
    return (attended, log_total)


def attend_backward(
    query_heads,
    query_labels,
    grad_heads,
    offset,
    log_total,
    key_blocks,
    value_blocks,
    label_blocks,
    scale,
):

    def step(running, block):
        scores, mask = score_block(query_heads, block[0], query_labels, block[2], scale)
        chance = jnp.where(mask, jnp.exp(scores - log_total[:, :, None]), 0.0)
        value_grad = jnp.einsum(
            "hqk,qhd->khd",
            chance.astype(jnp.bfloat16),
            grad_heads,
            preferred_element_type=jnp.float32,
        )
        chance_grad = jnp.einsum(
            "qhd,khd->hqk", grad_heads, block[1], preferred_element_type=jnp.float32
        )
        score_grad = (chance * (chance_grad - offset[:, :, None])).astype(jnp.bfloat16)
        running = (
            running
            + jnp.einsum("hqk,khd->qhd", score_grad, block[0], preferred_element_type=jnp.float32)
            * scale
        )
        key_grad = (
            jnp.einsum("hqk,qhd->khd", score_grad, query_heads, preferred_element_type=jnp.float32)
            * scale
        )
        return (running, (key_grad, value_grad))

    query_grad, (key_grads, value_grads) = lax.scan(
        step, jnp.zeros(query_heads.shape, jnp.float32), (key_blocks, value_blocks, label_blocks)
    )
    return (query_grad, key_grads, value_grads)


def per_device(
    inputs,
    token_image,
    image_time,
    image_class,
    targets,
    cotangent,
    class_table,
    modulate_weight,
    modulate_bias,
    attend_weight,
    attend_bias,
    output_weight,
    output_bias,
    expand_weight,
    expand_bias,
    shrink_weight,
    shrink_bias,
    inner_weight,
    inner_bias,
    middle_weight,
    middle_bias,
    outer_weight,
    outer_bias,
):
    count, width = inputs.shape
    head_dim = width // HEADS
    scale = 1.0 / math.sqrt(head_dim)
    columns = class_table.shape[1]
    slots = image_class.shape[0] // lax.axis_size("img")
    parts = lax.axis_size("blk")
    group = count * parts
    block = math.gcd(group, 512)
    blocks = group // block
    half = width // 2
    class_hot = (image_class[:, None] == jnp.arange(class_table.shape[0])[None, :]).astype(
        jnp.bfloat16
    )
    column = lax.axis_index("img") * columns + jnp.arange(columns)
    frequency = jnp.exp(-math.log(10000.0) * (column % half).astype(jnp.float32) / half)
    angle = image_time.astype(jnp.float32)[:, None] * frequency[None, :]
    condition = jnp.dot(class_hot, class_table, preferred_element_type=jnp.float32) + jnp.where(
        column[None, :] < half, jnp.cos(angle), jnp.sin(angle)
    )
    silu_condition = jax.nn.silu(condition).astype(jnp.bfloat16)
    modulation = (
        lax.psum_scatter(
            jnp.dot(silu_condition, modulate_weight, preferred_element_type=jnp.float32),
            "img",
            scatter_dimension=0,
            tiled=True,
        )
        + modulate_bias.astype(jnp.float32)[None, :]
    )
    slot_hot = (token_image[:, None] == jnp.arange(slots)[None, :]).astype(jnp.float32)
    row_modulation = jnp.dot(slot_hot, modulation, precision=HIGH)
    shift_one, scale_one, gate_one, shift_two, scale_two, gate_two = jnp.split(
        row_modulation, 6, axis=1
    )
    (
        attend_full,
        attend_bias_full,
        output_full,
        output_bias_full,
        expand_full,
        expand_bias_full,
        shrink_full,
        shrink_bias_full,
        inner_full,
        inner_bias_full,
        middle_full,
        middle_bias_full,
        outer_full,
        outer_bias_full,
    ) = (
        lax.all_gather(attend_weight, "img", axis=0, tiled=True),
        lax.all_gather(attend_bias, "img", axis=0, tiled=True),
        lax.all_gather(output_weight, "img", axis=0, tiled=True),
        lax.all_gather(output_bias, "img", axis=0, tiled=True),
        lax.all_gather(expand_weight, "img", axis=0, tiled=True),
        lax.all_gather(expand_bias, "img", axis=0, tiled=True),
        lax.all_gather(shrink_weight, "img", axis=0, tiled=True),
        lax.all_gather(shrink_bias, "img", axis=0, tiled=True),
        lax.all_gather(inner_weight, "img", axis=0, tiled=True),
        lax.all_gather(inner_bias, "img", axis=0, tiled=True),
        lax.all_gather(middle_weight, "img", axis=0, tiled=True),
        lax.all_gather(middle_bias, "img", axis=0, tiled=True),
        lax.all_gather(outer_weight, "img", axis=0, tiled=True),
        lax.all_gather(outer_bias, "img", axis=0, tiled=True),
    )
    source = inputs.astype(jnp.float32)
    normal_one, inverse_one = layer_norm(source)
    modulated_one = (normal_one * (1.0 + scale_one) + shift_one).astype(jnp.bfloat16)
    projected = jnp.dot(modulated_one, attend_full, preferred_element_type=jnp.float32)
    query = (projected[:, :width] + attend_bias_full[:width]).astype(jnp.bfloat16)
    key = projected[:, width : 2 * width].astype(jnp.bfloat16)
    value = (projected[:, 2 * width :] + attend_bias_full[width:]).astype(jnp.bfloat16)
    gathered = (
        lax.all_gather(key, "blk", axis=0, tiled=True),
        lax.all_gather(value, "blk", axis=0, tiled=True),
        lax.all_gather(token_image, "blk", axis=0, tiled=True),
    )
    key_blocks = gathered[0].reshape(blocks, block, HEADS, head_dim)
    value_blocks = gathered[1].reshape(blocks, block, HEADS, head_dim)
    label_blocks = gathered[2].reshape(blocks, block)
    query_heads = query.reshape(count, HEADS, head_dim)
    attended, log_total = attend_forward(
        query_heads, token_image, key_blocks, value_blocks, label_blocks, scale
    )
    attended_low = attended.reshape(count, width).astype(jnp.bfloat16)
    branch_one = (
        jnp.dot(attended_low, output_full, preferred_element_type=jnp.float32) + output_bias_full
    )
    middle = source + gate_one * branch_one
    normal_two, inverse_two = layer_norm(middle)
    modulated_two = (normal_two * (1.0 + scale_two) + shift_two).astype(jnp.bfloat16)
    expanded = (
        jnp.dot(modulated_two, expand_full, preferred_element_type=jnp.float32) + expand_bias_full
    )
    gelu_tanh = partial(jax.nn.gelu, approximate=True)
    activated = gelu_tanh(expanded).astype(jnp.bfloat16)
    branch_two = (
        jnp.dot(activated, shrink_full, preferred_element_type=jnp.float32) + shrink_bias_full
    )
    whole = middle + gate_two * branch_two
    whole_low = whole.astype(jnp.bfloat16)
    pre_one = jnp.dot(whole_low, inner_full, preferred_element_type=jnp.float32) + inner_bias_full
    first = jax.nn.silu(pre_one).astype(jnp.bfloat16)
    pre_two = jnp.dot(first, middle_full, preferred_element_type=jnp.float32) + middle_bias_full
    second = jax.nn.silu(pre_two).astype(jnp.bfloat16)
    aligned = jnp.dot(second, outer_full, preferred_element_type=jnp.float32) + outer_bias_full
    target = targets.astype(jnp.float32)
    cross = jnp.sum(aligned * target, axis=1)
    aligned_inverse = lax.rsqrt(jnp.sum(aligned * aligned, axis=1) + EPSILON)
    target_inverse = lax.rsqrt(jnp.sum(target * target, axis=1) + EPSILON)
    cosine = cross * aligned_inverse * target_inverse
    grad_aligned = (
        -0.5
        * (
            target * (aligned_inverse * target_inverse)[:, None]
            - (cosine * aligned_inverse * aligned_inverse)[:, None] * aligned
        )
    ).astype(jnp.bfloat16)
    grad_outer = left_product(second, grad_aligned)
    grad_outer_bias = column_sum(grad_aligned)
    grad_pre_two = local_back(jax.nn.silu, pre_two, right_product(grad_aligned, outer_full)).astype(
        jnp.bfloat16
    )
    grad_middle_weight = left_product(first, grad_pre_two)
    grad_middle_bias = column_sum(grad_pre_two)
    grad_pre_one = local_back(
        jax.nn.silu, pre_one, right_product(grad_pre_two, middle_full)
    ).astype(jnp.bfloat16)
    grad_inner = left_product(whole_low, grad_pre_one)
    grad_inner_bias = column_sum(grad_pre_one)
    grad_whole = cotangent.astype(jnp.float32) + right_product(grad_pre_one, inner_full)
    grad_gate_two = grad_whole * branch_two
    grad_branch_two = (grad_whole * gate_two).astype(jnp.bfloat16)
    grad_shrink = left_product(activated, grad_branch_two)
    grad_shrink_bias = column_sum(grad_branch_two)
    grad_expanded = local_back(
        gelu_tanh, expanded, right_product(grad_branch_two, shrink_full)
    ).astype(jnp.bfloat16)
    grad_expand = left_product(modulated_two, grad_expanded)
    grad_expand_bias = column_sum(grad_expanded)
    grad_mod_two = right_product(grad_expanded, expand_full)
    grad_scale_two = grad_mod_two * normal_two
    grad_middle = grad_whole + norm_back(grad_mod_two * (1.0 + scale_two), normal_two, inverse_two)
    grad_gate_one = grad_middle * branch_one
    grad_branch_one = (grad_middle * gate_one).astype(jnp.bfloat16)
    grad_output = left_product(attended_low, grad_branch_one)
    grad_output_bias = column_sum(grad_branch_one)
    grad_attended = right_product(grad_branch_one, output_full).astype(jnp.bfloat16)
    grad_heads = grad_attended.reshape(count, HEADS, head_dim)
    offset = jnp.einsum("qhd,qhd->hq", grad_heads.astype(jnp.float32), attended)
    query_grad, key_grads, value_grads = attend_backward(
        query_heads,
        token_image,
        grad_heads,
        offset,
        log_total,
        key_blocks,
        value_blocks,
        label_blocks,
        scale,
    )
    key_mine, value_mine = (
        lax.psum_scatter(key_grads.reshape(group, width), "blk", scatter_dimension=0, tiled=True),
        lax.psum_scatter(value_grads.reshape(group, width), "blk", scatter_dimension=0, tiled=True),
    )
    grad_projected = jnp.concatenate(
        [query_grad.reshape(count, width), key_mine, value_mine], axis=1
    ).astype(jnp.bfloat16)
    grad_attend = left_product(modulated_one, grad_projected)
    grad_attend_bias = jnp.concatenate(
        [column_sum(grad_projected[:, :width]), column_sum(grad_projected[:, 2 * width :])]
    )
    grad_mod_one = right_product(grad_projected, attend_full)
    grad_scale_one = grad_mod_one * normal_one
    grad_source = grad_middle + norm_back(grad_mod_one * (1.0 + scale_one), normal_one, inverse_one)
    grad_rows = jnp.concatenate(
        [grad_mod_one, grad_scale_one, grad_gate_one, grad_mod_two, grad_scale_two, grad_gate_two],
        axis=1,
    )
    slot_grad = jnp.dot(slot_hot.T, grad_rows, precision=HIGH)
    (
        attend_sum,
        attend_bias_sum,
        output_sum,
        output_bias_sum,
        expand_sum,
        expand_bias_sum,
        shrink_sum,
        shrink_bias_sum,
        inner_sum,
        inner_bias_sum,
        middle_sum,
        middle_bias_sum,
        outer_sum,
        outer_bias_sum,
    ) = (
        lax.psum_scatter(grad_attend, "img", scatter_dimension=0, tiled=True),
        lax.psum_scatter(grad_attend_bias, "img", scatter_dimension=0, tiled=True),
        lax.psum_scatter(grad_output, "img", scatter_dimension=0, tiled=True),
        lax.psum_scatter(grad_output_bias, "img", scatter_dimension=0, tiled=True),
        lax.psum_scatter(grad_expand, "img", scatter_dimension=0, tiled=True),
        lax.psum_scatter(grad_expand_bias, "img", scatter_dimension=0, tiled=True),
        lax.psum_scatter(grad_shrink, "img", scatter_dimension=0, tiled=True),
        lax.psum_scatter(grad_shrink_bias, "img", scatter_dimension=0, tiled=True),
        lax.psum_scatter(grad_inner, "img", scatter_dimension=0, tiled=True),
        lax.psum_scatter(grad_inner_bias, "img", scatter_dimension=0, tiled=True),
        lax.psum_scatter(grad_middle_weight, "img", scatter_dimension=0, tiled=True),
        lax.psum_scatter(grad_middle_bias, "img", scatter_dimension=0, tiled=True),
        lax.psum_scatter(grad_outer, "img", scatter_dimension=0, tiled=True),
        lax.psum_scatter(grad_outer_bias, "img", scatter_dimension=0, tiled=True),
    )
    (
        slot_total,
        attend_sum,
        attend_bias_sum,
        output_sum,
        output_bias_sum,
        expand_sum,
        expand_bias_sum,
        shrink_sum,
        shrink_bias_sum,
        inner_sum,
        inner_bias_sum,
        middle_sum,
        middle_bias_sum,
        outer_sum,
        outer_bias_sum,
    ) = lax.psum(
        (
            slot_grad,
            attend_sum,
            attend_bias_sum,
            output_sum,
            output_bias_sum,
            expand_sum,
            expand_bias_sum,
            shrink_sum,
            shrink_bias_sum,
            inner_sum,
            inner_bias_sum,
            middle_sum,
            middle_bias_sum,
            outer_sum,
            outer_bias_sum,
        ),
        "blk",
    )
    modulation_grad = lax.all_gather(slot_total, "img", axis=0, tiled=True)
    modulate_sum = jnp.dot(silu_condition.astype(jnp.float32).T, modulation_grad, precision=HIGH)
    modulate_bias_sum = jnp.sum(modulation_grad, axis=0)
    silu_grad = jnp.dot(modulation_grad, modulate_weight.astype(jnp.float32).T, precision=HIGH)
    condition_grad = local_back(jax.nn.silu, condition, silu_grad)
    table_sum = jnp.dot(class_hot.astype(jnp.float32).T, condition_grad, precision=HIGH)
    return (
        whole_low,
        grad_source.astype(jnp.bfloat16),
        table_sum,
        modulate_sum,
        modulate_bias_sum,
        attend_sum,
        attend_bias_sum,
        output_sum,
        output_bias_sum,
        expand_sum,
        expand_bias_sum,
        shrink_sum,
        shrink_bias_sum,
        inner_sum,
        inner_bias_sum,
        middle_sum,
        middle_bias_sum,
        outer_sum,
        outer_bias_sum,
    )


def solution(mesh):
    in_specs = (
        P(("img", "blk"), None),
        P(("img", "blk")),
        P(),
        P(),
        P(("img", "blk"), None),
        P(("img", "blk"), None),
        P(None, "img"),
        P("img", None),
        P(),
        P("img", None),
        P("img"),
        P("img", None),
        P("img"),
        P("img", None),
        P("img"),
        P("img", None),
        P("img"),
        P("img", None),
        P("img"),
        P("img", None),
        P("img"),
        P("img", None),
        P("img"),
    )
    out_specs = (
        P(("img", "blk"), None),
        P(("img", "blk"), None),
        P(None, "img"),
        P("img", None),
        P(),
        P("img", None),
        P("img"),
        P("img", None),
        P("img"),
        P("img", None),
        P("img"),
        P("img", None),
        P("img"),
        P("img", None),
        P("img"),
        P("img", None),
        P("img"),
        P("img", None),
        P("img"),
    )
    return jax.shard_map(
        per_device, mesh=mesh, in_specs=in_specs, out_specs=out_specs, check_vma=False
    )
```

profile of v0, /device:TPU:9, one launch (start us, length us, event | category | flops | bytes accessed | tf_op | source)
XLA Modules:
  0.0 2806.7 jit_solution(14186170091453379769)
XLA Ops:
  13.3 39.3 %reduce-scatter.11.cloned.1.call-done = f32[8,6912]{1,0:T(8,128)} async-done(((f32[64,6912]{1,0:T(8,128)}), f32[8,6912]{1,0:T(8,128)}) %reduce-scatter.11.cloned.1.call-update) | async-done | bytes 221200 | tf_op jit(solution)/shard_map/reduce_scatter | solution.py:179
  66.6 40.9 %all-gather.14.cloned.1.call-done = bf16[1152,3456]{1,0:T(8,128)(2,1)} async-done(((bf16[144,3456]{1,0:T(8,128)(2,1)}), bf16[1152,3456]{1,0:T(8,128)(2,1)}) %all-gather.14.cloned.1.call-update) | async-done | bytes 7962640 | tf_op jit(solution)/shard_map/all_gather | solution.py:208
  123.9 21.3 all-reduce.15
  153.6 12.3 all-gather.2
  175.0 11.0 all-gather
  188.3 17.8 all-gather.18.cloned.1.call-done
  206.1 17.4 reshape.294
  223.5 13.1 copy.76
  236.6 34.4 %while.39 = (s32[]{:T(128)}, f32[16,512]{1,0:T(8,128)S(1)}, f32[16,512]{1,0:T(8,128)S(1)}, s32[512]{0:T(512)S(1)}, s32[4,512]{1,0:T(4,128)S(1)}, /*index=5*/bf16...) while((s32[]{:T(128)}, f32[16,512]{1,0:T(8,128)S(1)}, ...), condition=%wide.region_6.7_spmd.clone, body=%wide.region_3.6_spmd.clone.sunk | while | flops 637837312 | bytes 37134452 | solution.py:71
  271.1 24.9 all-gather.16.cloned.1.call-done
  296.0 17.4 reshape.293
  313.4 13.2 copy.75
  326.6 35.9 %while.40 = (s32[]{:T(128)}, f32[512,16,72]{0,2,1:T(8,128)}, bf16[4,512,16,72]{1,3,2,0:T(8,128)(2,1)}, s32[512]{0:T(512)S(1)}, s32[4,512]{1,0:T(4,128)S(1)}, /*i...) while((s32[]{:T(128)}, f32[512,16,72]{0,2,1:T(8,128)}, ...), condition=%wide.region_8.9_spmd.clone, body=%wide.region_7.8_spmd.clone.sunk | while | flops 1226178560 | bytes 8824442 | solution.py:83
  378.2 16.8 all-gather.22.cloned.1.call-done
  395.1 11.5 fusion.118
  406.5 54.3 %all-gather.24.cloned.1.call-done = bf16[4608,1152]{1,0:T(8,128)(2,1)} async-done(((bf16[576,1152]{1,0:T(8,128)(2,1)}), bf16[4608,1152]{1,0:T(8,128)(2,1)}) %all-gather.24.cloned.1.call-update) | async-done | bytes 10616848 | tf_op jit(solution)/shard_map/all_gather | solution.py:214
  460.8 15.4 add_convert_fusion
  476.2 25.4 all-gather.26.cloned.1.call-done
  509.2 48.8 %all-gather.28.cloned.1.call-done = bf16[2048,2048]{1,0:T(8,128)(2,1)} async-done(((bf16[256,2048]{1,0:T(8,128)(2,1)}), bf16[2048,2048]{1,0:T(8,128)(2,1)}) %all-gather.28.cloned.1.call-update) | async-done | bytes 8388624 | tf_op jit(solution)/shard_map/all_gather | solution.py:218
  558.0 11.2 fusion.108
  569.2 22.9 all-gather.30.cloned.1.call-done
  603.7 10.1 convert_reduce_fusion.2
  621.1 18.8 convert_reduce_fusion
  640.0 12.0 fusion.105
  666.3 585.6 %while.41 = (s32[]{:T(128)}, f32[512,16,72]{0,2,1:T(8,128)}, f32[4,512,16,72]{1,0,3,2:T(4,128)}, f32[4,512,16,72]{1,0,3,2:T(4,128)}, bf16[4,512,16,72]{1,3,2,0:T...) while((s32[]{:T(128)}, f32[512,16,72]{0,2,1:T(8,128)}, ...), condition=%wide.region_17.18_spmd.clone, body=%wide.region_16.17_spmd.clone.sunk | while | flops 3064463360 | bytes 131834088 | solution.py:127
  666.8 9.5 fusion.207
  676.3 10.7 fusion.209
  687.0 9.6 fusion.208
  711.8 50.5 %dynamic_update_slice.11 = f32[4,512,16,72]{1,0,3,2:T(4,128)} dynamic-update-slice(f32[4,512,16,72]{1,0,3,2:T(4,128)} %get-tuple-element.711, f32[1,512,16,72]{1,0,3,2:T(1,128)} %copy.130, s32[]{:T(128)S(6)} %copy.158, s32[]{:T(128)} %constant.104.clone.1..sunk.2, s32[]{:T(128)} %constant.104.clone.1..sunk.2, s32[]{:T(128)} %constant.104.clone.1..sunk.2) | dynamic-update-slice | bytes 4718596 | tf_op jit(solution)/shard_map/while/body/jit(dynamic_update_index_in_dim)/dynamic_update_slice | solution.py:127
  762.3 50.4 %dynamic_update_slice.12 = f32[4,512,16,72]{1,0,3,2:T(4,128)} dynamic-update-slice(f32[4,512,16,72]{1,0,3,2:T(4,128)} %get-tuple-element.712, f32[1,512,16,72]{1,0,3,2:T(1,128)} %copy.131, s32[]{:T(128)S(6)} %copy.158, s32[]{:T(128)} %constant.104.clone.1..sunk.2, s32[]{:T(128)} %constant.104.clone.1..sunk.2, s32[]{:T(128)} %constant.104.clone.1..sunk.2) | dynamic-update-slice | bytes 4718596 | tf_op jit(solution)/shard_map/while/body/jit(dynamic_update_index_in_dim)/dynamic_update_slice | solution.py:127
  813.0 9.5 fusion.207
  822.5 10.7 fusion.209
  833.2 9.6 fusion.208
  858.1 50.5 %dynamic_update_slice.11 = f32[4,512,16,72]{1,0,3,2:T(4,128)} dynamic-update-slice(f32[4,512,16,72]{1,0,3,2:T(4,128)} %get-tuple-element.711, f32[1,512,16,72]{1,0,3,2:T(1,128)} %copy.130, s32[]{:T(128)S(6)} %copy.158, s32[]{:T(128)} %constant.104.clone.1..sunk.2, s32[]{:T(128)} %constant.104.clone.1..sunk.2, s32[]{:T(128)} %constant.104.clone.1..sunk.2) | dynamic-update-slice | bytes 4718596 | tf_op jit(solution)/shard_map/while/body/jit(dynamic_update_index_in_dim)/dynamic_update_slice | solution.py:127
  908.6 50.4 %dynamic_update_slice.12 = f32[4,512,16,72]{1,0,3,2:T(4,128)} dynamic-update-slice(f32[4,512,16,72]{1,0,3,2:T(4,128)} %get-tuple-element.712, f32[1,512,16,72]{1,0,3,2:T(1,128)} %copy.131, s32[]{:T(128)S(6)} %copy.158, s32[]{:T(128)} %constant.104.clone.1..sunk.2, s32[]{:T(128)} %constant.104.clone.1..sunk.2, s32[]{:T(128)} %constant.104.clone.1..sunk.2) | dynamic-update-slice | bytes 4718596 | tf_op jit(solution)/shard_map/while/body/jit(dynamic_update_index_in_dim)/dynamic_update_slice | solution.py:127
  959.3 9.5 fusion.207
  968.8 10.7 fusion.209
  979.5 9.6 fusion.208
  1004.3 50.5 %dynamic_update_slice.11 = f32[4,512,16,72]{1,0,3,2:T(4,128)} dynamic-update-slice(f32[4,512,16,72]{1,0,3,2:T(4,128)} %get-tuple-element.711, f32[1,512,16,72]{1,0,3,2:T(1,128)} %copy.130, s32[]{:T(128)S(6)} %copy.158, s32[]{:T(128)} %constant.104.clone.1..sunk.2, s32[]{:T(128)} %constant.104.clone.1..sunk.2, s32[]{:T(128)} %constant.104.clone.1..sunk.2) | dynamic-update-slice | bytes 4718596 | tf_op jit(solution)/shard_map/while/body/jit(dynamic_update_index_in_dim)/dynamic_update_slice | solution.py:127
  1054.8 50.4 %dynamic_update_slice.12 = f32[4,512,16,72]{1,0,3,2:T(4,128)} dynamic-update-slice(f32[4,512,16,72]{1,0,3,2:T(4,128)} %get-tuple-element.712, f32[1,512,16,72]{1,0,3,2:T(1,128)} %copy.131, s32[]{:T(128)S(6)} %copy.158, s32[]{:T(128)} %constant.104.clone.1..sunk.2, s32[]{:T(128)} %constant.104.clone.1..sunk.2, s32[]{:T(128)} %constant.104.clone.1..sunk.2) | dynamic-update-slice | bytes 4718596 | tf_op jit(solution)/shard_map/while/body/jit(dynamic_update_index_in_dim)/dynamic_update_slice | solution.py:127
  1105.5 9.5 fusion.207
  1115.0 10.7 fusion.209
  1125.7 9.7 fusion.208
  1150.6 50.5 %dynamic_update_slice.11 = f32[4,512,16,72]{1,0,3,2:T(4,128)} dynamic-update-slice(f32[4,512,16,72]{1,0,3,2:T(4,128)} %get-tuple-element.711, f32[1,512,16,72]{1,0,3,2:T(1,128)} %copy.130, s32[]{:T(128)S(6)} %copy.158, s32[]{:T(128)} %constant.104.clone.1..sunk.2, s32[]{:T(128)} %constant.104.clone.1..sunk.2, s32[]{:T(128)} %constant.104.clone.1..sunk.2) | dynamic-update-slice | bytes 4718596 | tf_op jit(solution)/shard_map/while/body/jit(dynamic_update_index_in_dim)/dynamic_update_slice | solution.py:127
  1201.1 50.4 %dynamic_update_slice.12 = f32[4,512,16,72]{1,0,3,2:T(4,128)} dynamic-update-slice(f32[4,512,16,72]{1,0,3,2:T(4,128)} %get-tuple-element.712, f32[1,512,16,72]{1,0,3,2:T(1,128)} %copy.131, s32[]{:T(128)S(6)} %copy.158, s32[]{:T(128)} %constant.104.clone.1..sunk.2, s32[]{:T(128)} %constant.104.clone.1..sunk.2, s32[]{:T(128)} %constant.104.clone.1..sunk.2) | dynamic-update-slice | bytes 4718596 | tf_op jit(solution)/shard_map/while/body/jit(dynamic_update_index_in_dim)/dynamic_update_slice | solution.py:127
  1252.0 12.0 copy.124
  1264.0 11.8 copy.125
  1300.2 13.4 fusion.107
  1314.9 14.2 fusion.110
  1330.5 12.2 fusion.122
  1344.8 80.1 %reduce-scatter.13.cloned.1.call-done = f32[512,1152]{0,1:T(8,128)} async-done(((f32[2048,1152]{0,1:T(8,128)}), f32[512,1152]{0,1:T(8,128)}) %reduce-scatter.13.cloned.1.call-update) | async-done | bytes 2359312 | tf_op jit(solution)/shard_map/reduce_scatter | solution.py:320
  1427.7 161.5 %reduce-scatter.15.cloned.1.call-done = f32[512,1152]{0,1:T(8,128)} async-done(((f32[2048,1152]{0,1:T(8,128)}), f32[512,1152]{0,1:T(8,128)}) %reduce-scatter.15.cloned.1.call-update) | async-done | bytes 2359312 | tf_op jit(solution)/shard_map/reduce_scatter | solution.py:321
  1592.3 11.2 fusion.77
  1605.0 13.0 fusion.106
  1640.7 10.0 reduce-scatter.19.cloned.1.call-done
  1650.6 65.4 %reduce-scatter.29.cloned.1.call-done = f32[256,768]{1,0:T(8,128)} async-done(((f32[2048,768]{1,0:T(8,128)}), f32[256,768]{1,0:T(8,128)}) %reduce-scatter.29.cloned.1.call-update) | async-done | bytes 786448 | tf_op jit(solution)/shard_map/reduce_scatter | solution.py:366
  1716.0 79.9 %reduce-scatter.25.cloned.1.call-done = f32[144,2048]{1,0:T(8,128)} async-done(((f32[1152,2048]{1,0:T(8,128)}), f32[144,2048]{1,0:T(8,128)}) %reduce-scatter.25.cloned.1.call-update) | async-done | bytes 1179664 | tf_op jit(solution)/shard_map/reduce_scatter | solution.py:362
  1795.8 119.4 %reduce-scatter.27.cloned.1.call-done = f32[256,2048]{1,0:T(8,128)} async-done(((f32[2048,2048]{1,0:T(8,128)}), f32[256,2048]{1,0:T(8,128)}) %reduce-scatter.27.cloned.1.call-update) | async-done | bytes 2097168 | tf_op jit(solution)/shard_map/reduce_scatter | solution.py:364
  1915.2 140.7 %reduce-scatter.23.cloned.1.call-done = f32[576,1152]{1,0:T(8,128)} async-done(((f32[4608,1152]{1,0:T(8,128)}), f32[576,1152]{1,0:T(8,128)}) %reduce-scatter.23.cloned.1.call-update) | async-done | bytes 2654224 | tf_op jit(solution)/shard_map/reduce_scatter | solution.py:360
  2055.9 140.7 %reduce-scatter.21.cloned.1.call-done = f32[144,4608]{1,0:T(8,128)} async-done(((f32[1152,4608]{1,0:T(8,128)}), f32[144,4608]{1,0:T(8,128)}) %reduce-scatter.21.cloned.1.call-update) | async-done | bytes 2654224 | tf_op jit(solution)/shard_map/reduce_scatter | solution.py:358
  2196.6 116.6 %reduce-scatter.17.cloned.1.call-done = f32[144,3456]{1,0:T(8,128)} async-done(((f32[1152,3456]{1,0:T(8,128)}), f32[144,3456]{1,0:T(8,128)}) %reduce-scatter.17.cloned.1.call-update) | async-done | bytes 1990672 | tf_op jit(solution)/shard_map/reduce_scatter | solution.py:354
  2313.3 422.1 %all-reduce.18.cloned.1.call-done = (f32[8,6912]{1,0:T(8,128)}, f32[144,3456]{1,0:T(8,128)}, f32[144,1152]{1,0:T(8,128)}, f32[144,4608]{1,0:T(8,128)}, f32[576,1...) async-done(((f32[8,6912]{1,0:T(8,128)}, f32[144,3456]{1,0:T(8,128)}, f32[144,1152]{1,0:T(8,128)}, f32[144,4608]{1,0:T(8,128)}, ...) | async-done | bytes 12247056 | tf_op jit(solution)/shard_map/psum | solution.py:385
  2738.7 22.8 all-reduce.12
  2762.1 13.9 all-reduce.13
  (376 shorter events, 323.8 us)
Async XLA Ops:
  7.2 45.4 %reduce-scatter.11.cloned.1.call-start = ((), (), s32[]{:S(2)}) async-start(), calls=%async_computation.10 | async-start | bytes 1990656 | tf_op jit(solution)/shard_map/reduce_scatter | solution.py:179
  11.7 40.9 %copy-start.30 = (s32[512]{0:T(512)S(1)}, s32[512]{0:T(512)}, u32[]{:S(2)}) copy-start(s32[512]{0:T(512)} %param.30) | copy-start | bytes 6148
  11.7 95.8 %all-gather.14.cloned.1.call-start = ((), (), s32[]{:S(2)}) async-start(), calls=%async_computation.11 | async-start | bytes 8957952 | tf_op jit(solution)/shard_map/all_gather | solution.py:208
  12.5 193.6 %all-gather.18.cloned.1.call-start = ((), (), s32[]{:S(2)}) async-start(), calls=%async_computation.13 | async-start | bytes 5898240 | tf_op jit(solution)/shard_map/all_gather | solution.py:231
  12.8 46.4 %copy-start.40 = (f32[512]{0:T(512)}, f32[512]{0:T(512)S(1)}, u32[]{:S(2)}) copy-start(f32[512]{0:T(512)S(1)} %broadcast_multiply_fusion.5) | copy-start | bytes 6148
  13.3 46.0 %copy-start.50 = (f32[512]{0:T(512)}, f32[512]{0:T(512)S(1)}, u32[]{:S(2)}) copy-start(f32[512]{0:T(512)S(1)} %add_rsqrt_fusion.3) | copy-start | bytes 6148
  59.3 5.7 copy-start.3
  118.2 4.7 copy-start.69
  118.2 5.0 copy-start.70
  118.2 5.2 copy-start.64
  118.2 5.5 copy-start.63
  119.4 176.6 %all-gather.16.cloned.1.call-start = ((), (), s32[]{:S(2)}) async-start(), calls=%async_computation.12 | async-start | bytes 5898240 | tf_op jit(solution)/shard_map/all_gather | solution.py:232
  149.4 216.6 %all-gather.20.cloned.1.call-start = ((), (), s32[]{:S(2)}) async-start(), calls=%async_computation.14 | async-start | bytes 2985984 | tf_op jit(solution)/shard_map/all_gather | solution.py:210
  150.0 245.0 %all-gather.22.cloned.1.call-start = ((), (), s32[]{:S(2)}) async-start(), calls=%async_computation.15 | async-start | bytes 11943936 | tf_op jit(solution)/shard_map/all_gather | solution.py:212
  150.6 310.2 %all-gather.24.cloned.1.call-start = ((), (), s32[]{:S(2)}) async-start(), calls=%async_computation.16 | async-start | bytes 11943936 | tf_op jit(solution)/shard_map/all_gather | solution.py:214
  151.4 350.3 %all-gather.26.cloned.1.call-start = ((), (), s32[]{:S(2)}) async-start(), calls=%async_computation.17 | async-start | bytes 5308416 | tf_op jit(solution)/shard_map/all_gather | solution.py:216
  152.1 405.8 %all-gather.28.cloned.1.call-start = ((), (), s32[]{:S(2)}) async-start(), calls=%async_computation.18 | async-start | bytes 9437184 | tf_op jit(solution)/shard_map/all_gather | solution.py:218
  152.8 439.2 %all-gather.30.cloned.1.call-start = ((), (), s32[]{:S(2)}) async-start(), calls=%async_computation.19 | async-start | bytes 3538944 | tf_op jit(solution)/shard_map/all_gather | solution.py:220
  153.4 1271.4 %reduce-scatter.13.cloned.1.call-start = ((), (), s32[]{:S(2)}) async-start(), calls=%async_computation.20 | async-start | bytes 11796480 | tf_op jit(solution)/shard_map/reduce_scatter | solution.py:320
  186.7 434.5 %copy-start.47 = (f32[4608]{0:T(1024)}, f32[4608]{0:T(1024)S(1)}, u32[]{:S(2)}) copy-start(f32[4608]{0:T(1024)S(1)} %convert_element_type.158) | copy-start | bytes 55300
  362.5 10.3 copy-start.45
  372.8 279.2 %copy-start.38 = (f32[512]{0:T(512)}, f32[512]{0:T(512)S(1)}, u32[]{:S(2)}) copy-start(f32[512]{0:T(512)S(1)} %broadcast_multiply_fusion.4) | copy-start | bytes 6148
  374.2 277.8 %copy-start.42 = (f32[512]{0:T(512)}, f32[512]{0:T(512)S(1)}, u32[]{:S(2)}) copy-start(f32[512]{0:T(512)S(1)} %add_rsqrt_fusion.2) | copy-start | bytes 6148
  501.6 56.3 %copy-start.57 = (f32[8,1,256]{2,1,0:T(1,128)S(1)}, f32[8,1,256]{2,1,0:T(1,128)}, u32[]{:S(2)}) copy-start(f32[8,1,256]{2,1,0:T(1,128)} %convert_element_type.185) | copy-start | bytes 24580
  558.0 34.1 %copy-start.59 = (f32[8,1,256]{2,1,0:T(1,128)S(1)}, f32[8,1,256]{2,1,0:T(1,128)}, u32[]{:S(2)}) copy-start(f32[8,1,256]{2,1,0:T(1,128)} %convert_element_type.186) | copy-start | bytes 24580
  558.0 34.1 %copy-start.61 = (f32[768]{0:T(1024)S(1)}, f32[768]{0:T(1024)}, u32[]{:S(2)}) copy-start(f32[768]{0:T(1024)} %convert_element_type.168) | copy-start | bytes 9220
  592.0 6.1 copy-start.32
  592.0 7.1 copy-start.76
  598.1 5.5 slice-start
  599.1 4.5 copy-start.33
  603.6 10.1 copy-start.77
  603.7 10.1 copy-start.67
  621.1 18.9 copy-start.74
  621.1 31.0 %copy-start.14 = (f32[512,1152]{1,0:T(8,128)}, f32[512,1152]{1,0:T(8,128)S(1)}, u32[]{:S(2)}) copy-start(f32[512,1152]{1,0:T(8,128)S(1)} %get-tuple-element.464) | copy-start | bytes 7077892
  621.1 18.9 copy-start.5
  652.0 5.5 copy-start.10
  652.1 6.5 copy-start.19
  661.5 4.9 copy-start.46
  696.6 5.8 copy-start.1
  842.9 5.8 copy-start.1
  989.1 5.8 copy-start.1
  1135.4 5.8 copy-start.1
  1264.0 325.2 %reduce-scatter.15.cloned.1.call-start = ((), (), s32[]{:S(2)}) async-start(), calls=%async_computation.21 | async-start | bytes 11796480 | tf_op jit(solution)/shard_map/reduce_scatter | solution.py:321
  1275.9 374.7 %reduce-scatter.19.cloned.1.call-start = ((), (), s32[]{:S(2)}) async-start(), calls=%async_computation.24 | async-start | bytes 5971968 | tf_op jit(solution)/shard_map/reduce_scatter | solution.py:356
  1282.5 433.5 %reduce-scatter.29.cloned.1.call-start = ((), (), s32[]{:S(2)}) async-start(), calls=%async_computation.29 | async-start | bytes 7077888 | tf_op jit(solution)/shard_map/reduce_scatter | solution.py:366
  1290.4 505.5 %reduce-scatter.25.cloned.1.call-start = ((), (), s32[]{:S(2)}) async-start(), calls=%async_computation.27 | async-start | bytes 10616832 | tf_op jit(solution)/shard_map/reduce_scatter | solution.py:362
  1299.5 615.7 %reduce-scatter.27.cloned.1.call-start = ((), (), s32[]{:S(2)}) async-start(), calls=%async_computation.28 | async-start | bytes 18874368 | tf_op jit(solution)/shard_map/reduce_scatter | solution.py:364
  1313.6 742.3 %reduce-scatter.23.cloned.1.call-start = ((), (), s32[]{:S(2)}) async-start(), calls=%async_computation.26 | async-start | bytes 23887872 | tf_op jit(solution)/shard_map/reduce_scatter | solution.py:360
  1329.2 867.4 %reduce-scatter.21.cloned.1.call-start = ((), (), s32[]{:S(2)}) async-start(), calls=%async_computation.25 | async-start | bytes 23887872 | tf_op jit(solution)/shard_map/reduce_scatter | solution.py:358
  1342.8 970.4 %reduce-scatter.17.cloned.1.call-start = ((), (), s32[]{:S(2)}) async-start(), calls=%async_computation.23 | async-start | bytes 17915904 | tf_op jit(solution)/shard_map/reduce_scatter | solution.py:354
  1344.8 246.5 %copy-start.25 = (bf16[512,16,72]{0,2,1:T(8,128)(2,1)}, bf16[512,16,72]{0,2,1:T(8,128)(2,1)S(1)}, u32[]{:S(2)}) copy-start(bf16[512,16,72]{0,2,1:T(8,128)(2,1)S(1)} %get-tuple-element.442) | copy-start | bytes 3538948
  1603.6 1131.8 %all-reduce.18.cloned.1.call-start = ((), (), s32[]{:S(2)}) async-start(), calls=%async_computation.30 | async-start | bytes 24494080 | tf_op jit(solution)/shard_map/psum | solution.py:385
  1605.0 13.1 copy-start.9
  2313.2 425.5 %copy-start.44 = (f32[1152]{0:T(1024)S(1)}, f32[1152]{0:T(1024)}, u32[]{:S(2)}) copy-start(f32[1152]{0:T(1024)} %get-tuple-element.438) | copy-start | bytes 13828
  2313.2 425.5 %copy-start.49 = (f32[4608]{0:T(1024)S(1)}, f32[4608]{0:T(1024)}, u32[]{:S(2)}) copy-start(f32[4608]{0:T(1024)} %get-tuple-element.436) | copy-start | bytes 55300
  2313.2 425.5 %copy-start.52 = (f32[768]{0:T(1024)S(1)}, f32[768]{0:T(1024)}, u32[]{:S(2)}) copy-start(f32[768]{0:T(1024)} %get-tuple-element.428) | copy-start | bytes 9220
  2313.2 425.5 %copy-start.54 = (f32[2048]{0:T(1024)S(1)}, f32[2048]{0:T(1024)}, u32[]{:S(2)}) copy-start(f32[2048]{0:T(1024)} %get-tuple-element.430) | copy-start | bytes 24580
  2313.2 425.5 %copy-start.55 = (f32[2048]{0:T(1024)S(1)}, f32[2048]{0:T(1024)}, u32[]{:S(2)}) copy-start(f32[2048]{0:T(1024)} %get-tuple-element.432) | copy-start | bytes 24580
  2313.2 425.5 %copy-start.56 = (f32[1152]{0:T(1024)S(1)}, f32[1152]{0:T(1024)}, u32[]{:S(2)}) copy-start(f32[1152]{0:T(1024)} %get-tuple-element.434) | copy-start | bytes 13828
  2313.2 466.5 %copy-start.37 = (f32[64,144]{1,0:T(8,128)S(1)}, f32[64,144]{1,0:T(8,128)}, u32[]{:S(2)}) copy-start(f32[64,144]{1,0:T(8,128)} %copy-done.36) | copy-start | bytes 110596
  2313.2 466.5 %copy-start.65 = (s32[64]{0:T(128)S(1)}, s32[64]{0:T(128)}, u32[]{:S(2)}) copy-start(s32[64]{0:T(128)} %param.32) | copy-start | bytes 772
  2313.2 462.8 %all-gather.32.cloned.1.call-start = ((), (), s32[]{:S(2)}) async-start(), calls=%async_computation.22 | async-start | bytes 1990656 | tf_op jit(solution)/shard_map/all_gather | solution.py:405
  2776.0 5.0 copy-start.12
  2784.7 5.4 copy-start.35
  (43 other events, 97.8 us)
Sparse Core Ops, SparseCore 0:
  12.0 40.5 reduce-scatter.10
  54.5 53.0 all-gather.13
  119.5 86.5 all-gather.17
  208.1 87.8 all-gather.15
  297.7 31.7 all-gather.19
  331.2 63.8 all-gather.21
  397.0 63.8 all-gather.23
  462.7 38.9 all-gather.25
  503.5 54.3 all-gather.27
  559.7 32.3 all-gather.29
  1264.1 160.7 reduce-scatter.12
  1427.1 162.0 reduce-scatter.14
  1592.6 57.9 reduce-scatter.18
  1654.2 61.7 reduce-scatter.28
  1719.3 76.4 reduce-scatter.24
  1799.3 115.9 reduce-scatter.26
  1918.7 137.1 reduce-scatter.22
  2059.4 137.1 reduce-scatter.20
  2200.2 112.9 reduce-scatter.16
  2317.5 417.8 all-reduce.17
  2737.4 28.5 all-gather.31
where the time goes:
time: 2840 us; the launch traced here: 2810 us
  waiting for transfers between devices  1630 us (57%)
  local copies, waits for them, and re-layouts  573 us (20%)
  matrix products  426 us (15%)
  blocking collectives  89.4 us (3%)
  other arithmetic  63 us (2%)
    dynamic_update_slice x16, local copies, waits for them, and re-layouts, attend_backward(): lax.scan(step, jnp.zeros(query_heads.shape, jnp.float32), (key_blocks, va...  442 us
    psum x1, waiting for transfers between devices, per_device(): lax.psum((slot_grad, attend_sum, attend_bias_sum, output_sum, output_bias...  422 us
    reduce_scatter x1, waiting for transfers between devices, per_device(): lax.psum_scatter(value_grads.reshape(group, width), 'blk', scatter_dimens...  162 us
    reduce_scatter x1, waiting for transfers between devices, per_device(): lax.psum_scatter(grad_shrink, 'img', scatter_dimension=0, tiled=True)  141 us
    reduce_scatter x1, waiting for transfers between devices, per_device(): lax.psum_scatter(grad_expand, 'img', scatter_dimension=0, tiled=True)  141 us
    reduce_scatter x1, waiting for transfers between devices, per_device(): lax.psum_scatter(grad_middle_weight, 'img', scatter_dimension=0, tiled=True)  119 us
    reduce_scatter x1, waiting for transfers between devices, per_device(): lax.psum_scatter(grad_attend, 'img', scatter_dimension=0, tiled=True)  117 us
    unnamed x189, local copies, waits for them, and re-layouts  90.3 us
  transfers between devices with their start and end apart: 21, of which 19 were waited for; matrix products, arithmetic and copies ran while one was open for 12% of the time, Pallas kernels for 0%

commit v1 on v0

v1 whole, which is shorter than its diff:
```python
from functools import partial
import math

import jax
import jax.numpy as jnp
from jax import lax
from jax.experimental import pallas as pl
from jax.experimental.pallas import tpu as pltpu
from jax.sharding import PartitionSpec as P

HEADS = 16
SHORT = 256
RATIO = 4
LANES = 128

EPSILON = 1e-06
HIGH = lax.Precision.HIGHEST
BF = jnp.bfloat16
F32 = jnp.float32


def layer_norm(values):
    mean = jnp.mean(values, axis=-1, keepdims=True)
    centered = values - mean
    variance = jnp.mean(centered * centered, axis=-1, keepdims=True)
    inverse = lax.rsqrt(variance + EPSILON)
    return (centered * inverse, inverse)


def norm_back(grad, normal, inverse):
    mean_grad = jnp.mean(grad, axis=-1, keepdims=True)
    mean_cross = jnp.mean(grad * normal, axis=-1, keepdims=True)
    return inverse * (grad - mean_grad - normal * mean_cross)


def local_back(function, point, grad):
    return jax.vjp(function, point)[1](grad)[0]


def left_product(left, right):
    return jnp.einsum("ti,to->io", left, right, preferred_element_type=F32).astype(BF)


def right_product(grad, weight):
    return jnp.einsum("to,io->ti", grad, weight, preferred_element_type=F32)


def column_sum(values):
    return jnp.sum(values.astype(F32), axis=0)


def dot(left, right):
    return jnp.dot(left, right, preferred_element_type=F32)


def dot_general(left, right, contract):
    return lax.dot_general(left, right, ((contract[:1], contract[1:]), ((), ())), preferred_element_type=F32)


def softmax_keys(keys, queries, scale):
    scores = dot_general(keys, queries, (1, 1)) * scale
    raised = jnp.exp(scores - jnp.max(scores, axis=0, keepdims=True))
    return raised * (1.0 / jnp.sum(raised, axis=0, keepdims=True))


def attend_forward_kernel(heads, scale, start_ref, length_ref, qkv_ref, pick_ref, out_ref):
    parts, _, unit, _ = qkv_ref.shape
    u = pl.program_id(0)
    first = start_ref[u]

    def work(span):
        outs = []
        for h in range(heads):

            def head(which, lo, n):
                at = (which * heads + h) * LANES
                return qkv_ref[:, pl.ds(lo, n), :, at : at + LANES].reshape(parts * n * unit, LANES)

            chance = softmax_keys(head(1, first, span), head(0, u, 1), scale).astype(BF)
            outs.append(dot_general(chance, head(2, first, span), (0, 0)).astype(BF))
        packed = dot(jnp.concatenate(outs, axis=1), pick_ref[...]).astype(BF)
        out_ref[...] = packed.reshape(out_ref.shape)

    pl.when(length_ref[u] == 1)(lambda: work(1))
    pl.when(length_ref[u] != 1)(lambda: work(RATIO))


def attend_backward_kernel(
    heads, scale, start_ref, length_ref, qkv_ref, grad_ref, spread_ref, pick_ref, out_ref, dq, dk, dv
):
    parts, units, unit, _ = qkv_ref.shape
    u = pl.program_id(0)
    first = start_ref[u]

    @pl.when(u == 0)
    def _():
        dk[...] = jnp.zeros_like(dk)
        dv[...] = jnp.zeros_like(dv)

    def work(span):
        grads = dot(grad_ref[...].reshape(parts * unit, -1), spread_ref[...]).astype(BF)
        for h in range(heads):

            def head(which, lo, n):
                at = (which * heads + h) * LANES
                return qkv_ref[:, pl.ds(lo, n), :, at : at + LANES].reshape(parts * n * unit, LANES)

            at = slice(h * LANES, (h + 1) * LANES)
            grad = grads[:, at]
            query, key, value = head(0, u, 1), head(1, first, span), head(2, first, span)
            chance = softmax_keys(key, query, scale)
            chance_grad = dot_general(value, grad, (1, 1))
            offset = jnp.sum(chance * chance_grad, axis=0, keepdims=True)
            score_grad = (chance * (chance_grad - offset)).astype(BF)
            into = (parts, span, unit, LANES)
            dv[:, pl.ds(first, span), :, at] += dot(chance.astype(BF), grad).reshape(into)
            dk[:, pl.ds(first, span), :, at] += (dot(score_grad, query) * scale).reshape(into)
            dq[:, pl.ds(u, 1), :, at] = (
                (dot_general(score_grad, key, (0, 0)) * scale).astype(BF).reshape(parts, 1, unit, LANES)
            )

    pl.when(length_ref[u] == 1)(lambda: work(1))
    pl.when(length_ref[u] != 1)(lambda: work(RATIO))

    @pl.when(u == units - 1)
    def _():
        def pack(i, carry):
            rows = [ref[:, pl.ds(i, 1)].astype(BF).reshape(parts * unit, -1) for ref in (dq, dk, dv)]
            packed = dot(jnp.concatenate(rows, axis=1), pick_ref[...]).astype(BF)
            out_ref[:, pl.ds(i, 1)] = packed.reshape(parts, 1, unit, -1)
            return carry

        lax.fori_loop(0, units, pack, 0)


def picker(heads, head_dim, dtype):
    row = jnp.arange(heads * LANES)[:, None]
    col = jnp.arange(heads * head_dim)[None, :]
    return ((row // LANES == col // head_dim) & (row % LANES == col % head_dim)).astype(dtype)


def attend_forward(start, length, qkv, heads, head_dim):
    parts, units, unit, lanes = qkv.shape
    width = heads * head_dim
    whole = lambda *shape: pl.BlockSpec(shape, lambda u, *_: (0,) * len(shape))
    return pl.pallas_call(
        partial(attend_forward_kernel, heads, 1.0 / math.sqrt(head_dim)),
        grid_spec=pltpu.PrefetchScalarGridSpec(
            num_scalar_prefetch=2,
            grid=(units,),
            in_specs=[whole(parts, units, unit, lanes), whole(heads * LANES, width)],
            out_specs=pl.BlockSpec((parts, 1, unit, width), lambda u, *_: (0, u, 0, 0)),
        ),
        out_shape=jax.ShapeDtypeStruct((parts, units, unit, width), BF),
        compiler_params=pltpu.CompilerParams(vmem_limit_bytes=48 * 2**20),
        cost_estimate=pl.CostEstimate(flops=10 * 2**30, bytes_accessed=16 * 2**20, transcendentals=2**23),
        name="attend_forward",
    )(start, length, qkv, picker(heads, head_dim, BF))


def attend_backward(start, length, qkv, grad, heads, head_dim):
    parts, units, unit, lanes = qkv.shape
    width = heads * head_dim
    whole = lambda *shape: pl.BlockSpec(shape, lambda u, *_: (0,) * len(shape))
    pick = picker(heads, head_dim, BF)
    return pl.pallas_call(
        partial(attend_backward_kernel, heads, 1.0 / math.sqrt(head_dim)),
        grid_spec=pltpu.PrefetchScalarGridSpec(
            num_scalar_prefetch=2,
            grid=(units,),
            in_specs=[
                whole(parts, units, unit, lanes),
                pl.BlockSpec((parts, 1, unit, width), lambda u, *_: (0, u, 0, 0)),
                whole(width, heads * LANES),
                whole(3 * heads * LANES, 3 * width),
            ],
            out_specs=whole(parts, units, unit, 3 * width),
            scratch_shapes=[
                pltpu.VMEM((parts, units, unit, heads * LANES), BF),
                pltpu.VMEM((parts, units, unit, heads * LANES), F32),
                pltpu.VMEM((parts, units, unit, heads * LANES), F32),
            ],
        ),
        out_shape=jax.ShapeDtypeStruct((parts, units, unit, 3 * width), BF),
        compiler_params=pltpu.CompilerParams(vmem_limit_bytes=56 * 2**20),
        cost_estimate=pl.CostEstimate(flops=40 * 2**30, bytes_accessed=16 * 2**20, transcendentals=2**23),
        name="attend_backward",
    )(start, length, qkv, grad, pick.T, picker(3 * heads, head_dim, BF))


def flips(n, bit):
    return [(i, i ^ bit) for i in range(n)]


def scatter_steps(left, right):
    devices = lax.axis_size("img")
    place = lax.axis_index("img")
    count, depth = left.shape
    columns = right.shape[1]
    blocks = left.reshape(count, devices, depth // devices)

    def of(*masks):
        picked = [lax.dynamic_index_in_dim(blocks, place ^ m, axis=1, keepdims=False) for m in masks]
        return jnp.concatenate(picked, axis=1)

    rows = depth // devices
    sent = left_product(of(1, 3, 5, 7), right)
    got = lax.ppermute(sent, "img", flips(devices, 1))
    own = jnp.einsum("ti,to->io", of(0, 2, 4, 6), right, preferred_element_type=F32) + got.astype(F32)
    own = own.astype(BF).reshape(4, rows, columns)
    half = columns // 2 // LANES * LANES
    one, two = own[:, :, :half], own[:, :, half:]
    got_x = lax.ppermute(jnp.stack([one[1], one[3]]), "img", flips(devices, 2)).astype(F32)
    got_y = lax.ppermute(jnp.stack([two[2], two[3]]), "img", flips(devices, 4)).astype(F32)
    next_y = (one[2].astype(F32) + got_x[1]).astype(BF)
    next_x = (two[1].astype(F32) + got_y[1]).astype(BF)
    got_y2 = lax.ppermute(next_y, "img", flips(devices, 4)).astype(F32)
    got_x2 = lax.ppermute(next_x, "img", flips(devices, 2)).astype(F32)
    first = one[0].astype(F32) + got_x[0] + got_y2
    second = two[0].astype(F32) + got_y[0] + got_x2
    return jnp.concatenate([first, second], axis=1).astype(BF)


def line_sum(values):
    place = lax.axis_index("blk")
    inner = (place == 1) | (place == 2)
    values = (values.astype(F32) + lax.ppermute(values, "blk", [(0, 1), (3, 2)]).astype(F32)).astype(BF)
    total = (values.astype(F32) + lax.ppermute(values, "blk", [(1, 2), (2, 1)]).astype(F32)).astype(BF)
    back = lax.ppermute(total, "blk", [(1, 0), (2, 3)])
    return jnp.where(inner, total, back)


def per_device(
    inputs,
    token_image,
    image_time,
    image_class,
    targets,
    cotangent,
    class_table,
    modulate_weight,
    modulate_bias,
    attend_weight,
    attend_bias,
    output_weight,
    output_bias,
    expand_weight,
    expand_bias,
    shrink_weight,
    shrink_bias,
    inner_weight,
    inner_bias,
    middle_weight,
    middle_bias,
    outer_weight,
    outer_bias,
):
    count, width = inputs.shape
    head_dim = width // HEADS
    columns = class_table.shape[1]
    devices, parts = lax.axis_size("img"), lax.axis_size("blk")
    place_img, place_blk = lax.axis_index("img"), lax.axis_index("blk")
    slots = image_class.shape[0] // devices
    unit = SHORT // parts
    units = count // unit
    heads = HEADS // parts
    mine = heads * head_dim
    half = width // 2

    class_hot = (image_class[:, None] == jnp.arange(class_table.shape[0])[None, :]).astype(BF)
    column = place_img * columns + jnp.arange(columns)
    frequency = jnp.exp(-math.log(10000.0) * (column % half).astype(F32) / half)
    angle = image_time.astype(F32)[:, None] * frequency[None, :]
    condition = dot(class_hot, class_table) + jnp.where(column[None, :] < half, jnp.cos(angle), jnp.sin(angle))
    silu_condition = jax.nn.silu(condition).astype(BF)
    shares = dot(silu_condition, modulate_weight)
    biases = (attend_bias, output_bias, expand_bias, shrink_bias, inner_bias, middle_bias, outer_bias)
    bias_row = jnp.concatenate(biases).astype(F32)
    wide = shares.shape[1]
    tail = jnp.broadcast_to(jnp.pad(bias_row, (0, wide - bias_row.shape[0])), (devices, 1, wide))
    sent = jnp.concatenate([shares.reshape(devices, slots, wide), tail], axis=1)
    got = lax.all_to_all(sent, "img", split_axis=0, concat_axis=0, tiled=True)
    modulation = jnp.sum(got[:, :slots], axis=0) + modulate_bias.astype(F32)[None, :]
    full_biases = []
    at = 0
    for bias in biases:
        full_biases.append(got[:, slots, at : at + bias.shape[0]].reshape(-1))
        at += bias.shape[0]
    (
        attend_bias_full,
        output_bias_full,
        expand_bias_full,
        shrink_bias_full,
        inner_bias_full,
        middle_bias_full,
        outer_bias_full,
    ) = full_biases

    labels = token_image[::unit]
    same = labels[:, None] == labels[None, :]
    start = jnp.argmax(same, axis=1).astype(jnp.int32)
    length = jnp.sum(same, axis=1).astype(jnp.int32)
    unit_hot = (labels[:, None] == jnp.arange(slots)[None, :]).astype(F32)
    unit_modulation = jnp.dot(unit_hot, modulation, precision=HIGH)
    shift_one, scale_one, gate_one, shift_two, scale_two, gate_two = (
        block[:, None, :] for block in jnp.split(unit_modulation, 6, axis=1)
    )

    def by_unit(values):
        return values.reshape(units, unit, width)

    def by_row(values):
        return values.reshape(count, width)

    attend_mine = lax.dynamic_slice_in_dim(
        attend_weight.reshape(-1, 3, parts, mine), place_blk, 1, axis=2
    ).reshape(-1, 3 * mine)
    attend_full = lax.all_gather(attend_mine, "img", axis=0, tiled=True)
    output_full = lax.all_gather(output_weight, "img", axis=0, tiled=True)
    expand_full = lax.all_gather(expand_weight, "img", axis=0, tiled=True)
    shrink_full = lax.all_gather(shrink_weight, "img", axis=0, tiled=True)
    inner_full = lax.all_gather(inner_weight, "img", axis=0, tiled=True)
    middle_full = lax.all_gather(middle_weight, "img", axis=0, tiled=True)
    outer_full = lax.all_gather(outer_weight, "img", axis=0, tiled=True)

    source = by_unit(inputs.astype(F32))
    normal_one, inverse_one = layer_norm(source)
    modulated_one = by_row((normal_one * (1.0 + scale_one) + shift_one).astype(BF))
    modulated_group = lax.all_to_all(
        jnp.broadcast_to(modulated_one, (parts, count, width)), "blk", split_axis=0, concat_axis=0, tiled=True
    ).reshape(parts * count, width)

    def pad_heads(values):
        lead = values.shape[:-1]
        values = values.reshape(*lead, 3 * heads, head_dim)
        values = jnp.pad(values, ((0, 0),) * len(lead) + ((0, 0), (0, LANES - head_dim)))
        return values.reshape(*lead, 3 * heads * LANES)

    bias_mine = lax.dynamic_slice_in_dim(attend_bias_full.reshape(2, parts, mine), place_blk, 1, axis=1)
    bias_mine = jnp.concatenate([bias_mine[0, 0], jnp.zeros((mine,), F32), bias_mine[1, 0]])
    projected = dot(modulated_group, pad_heads(attend_full)) + pad_heads(bias_mine)[None, :]
    qkv = projected.astype(BF).reshape(parts, units, unit, 3 * heads * LANES)
    attended_heads = attend_forward(start, length, qkv, heads, head_dim)
    attended = lax.all_to_all(
        attended_heads.reshape(parts, count, mine), "blk", split_axis=0, concat_axis=0, tiled=True
    )
    output_heads = output_full.reshape(parts, mine, width)
    branch_one = by_unit(
        jnp.einsum("pti,pio->to", attended, output_heads, preferred_element_type=F32) + output_bias_full
    )
    middle = source + gate_one * branch_one
    normal_two, inverse_two = layer_norm(middle)
    modulated_two = by_row((normal_two * (1.0 + scale_two) + shift_two).astype(BF))
    expanded = dot(modulated_two, expand_full) + expand_bias_full
    gelu_tanh = partial(jax.nn.gelu, approximate=True)
    activated = gelu_tanh(expanded).astype(BF)
    branch_two = by_unit(dot(activated, shrink_full) + shrink_bias_full)
    whole = middle + gate_two * branch_two
    whole_low = by_row(whole.astype(BF))
    pre_one = dot(whole_low, inner_full) + inner_bias_full
    first = jax.nn.silu(pre_one).astype(BF)
    pre_two = dot(first, middle_full) + middle_bias_full
    second = jax.nn.silu(pre_two).astype(BF)
    aligned = dot(second, outer_full) + outer_bias_full
    target = targets.astype(F32)
    cross = jnp.sum(aligned * target, axis=1)
    aligned_inverse = lax.rsqrt(jnp.sum(aligned * aligned, axis=1) + EPSILON)
    target_inverse = lax.rsqrt(jnp.sum(target * target, axis=1) + EPSILON)
    cosine = cross * aligned_inverse * target_inverse
    grad_aligned = (
        -0.5
        * (
            target * (aligned_inverse * target_inverse)[:, None]
            - (cosine * aligned_inverse * aligned_inverse)[:, None] * aligned
        )
    ).astype(BF)

    def scatter(left, right):
        if devices == 8:
            return scatter_steps(left, right)
        return lax.psum_scatter(left_product(left, right), "img", scatter_dimension=0, tiled=True)

    def total(part):
        return line_sum(part) if parts == 4 else lax.psum(part, "blk")

    outer_sum = total(scatter(second, grad_aligned))
    grad_outer_bias = column_sum(grad_aligned)
    grad_pre_two = local_back(jax.nn.silu, pre_two, right_product(grad_aligned, outer_full)).astype(BF)
    middle_sum = total(scatter(first, grad_pre_two))
    grad_middle_bias = column_sum(grad_pre_two)
    grad_pre_one = local_back(jax.nn.silu, pre_one, right_product(grad_pre_two, middle_full)).astype(BF)
    inner_sum = total(scatter(whole_low, grad_pre_one))
    grad_inner_bias = column_sum(grad_pre_one)
    grad_whole = by_unit(cotangent.astype(F32)) + by_unit(right_product(grad_pre_one, inner_full))
    grad_gate_two = grad_whole * branch_two
    grad_branch_two = by_row((grad_whole * gate_two).astype(BF))
    shrink_sum = total(scatter(activated, grad_branch_two))
    grad_shrink_bias = column_sum(grad_branch_two)
    grad_expanded = local_back(gelu_tanh, expanded, right_product(grad_branch_two, shrink_full)).astype(BF)
    expand_sum = total(scatter(modulated_two, grad_expanded))
    grad_expand_bias = column_sum(grad_expanded)
    grad_mod_two = by_unit(right_product(grad_expanded, expand_full))
    grad_scale_two = grad_mod_two * normal_two
    grad_middle = grad_whole + norm_back(grad_mod_two * (1.0 + scale_two), normal_two, inverse_two)
    grad_gate_one = grad_middle * branch_one
    grad_branch_one = by_row((grad_middle * gate_one).astype(BF))
    attended_rows = jnp.transpose(attended, (1, 0, 2)).reshape(count, width)
    output_sum = total(scatter(attended_rows, grad_branch_one))
    grad_output_bias = column_sum(grad_branch_one)
    grad_attended = jnp.einsum("to,pio->pti", grad_branch_one, output_heads, preferred_element_type=F32)
    grad_heads = lax.all_to_all(grad_attended.astype(BF), "blk", split_axis=0, concat_axis=0, tiled=True)
    grad_qkv = attend_backward(
        start, length, qkv, grad_heads.reshape(parts, units, unit, mine), heads, head_dim
    ).reshape(parts * count, 3 * mine)
    attend_part = scatter(modulated_group, grad_qkv)
    attend_parts = lax.all_gather(attend_part, "blk", axis=0, tiled=False)
    attend_sum = jnp.transpose(attend_parts.reshape(parts, -1, 3, mine), (1, 2, 0, 3)).reshape(
        attend_part.shape[0], 3 * width
    )
    partial_mod_one = right_product(grad_qkv, attend_full).astype(BF)
    grad_mod_one = by_unit(
        lax.psum_scatter(partial_mod_one, "blk", scatter_dimension=0, tiled=True).astype(F32)
    )
    grad_scale_one = grad_mod_one * normal_one
    grad_source = grad_middle + norm_back(grad_mod_one * (1.0 + scale_one), normal_one, inverse_one)

    def slot_sum(*values):
        rows = jnp.concatenate([jnp.sum(v, axis=1) for v in values], axis=1)
        return jnp.dot(unit_hot.T, rows, precision=HIGH)

    early_biases = (
        grad_output_bias,
        grad_expand_bias,
        grad_shrink_bias,
        grad_inner_bias,
        grad_middle_bias,
        grad_outer_bias,
    )
    early_sizes = [b.shape[0] // devices for b in early_biases]
    early_bias_rows = jnp.concatenate([b.reshape(devices, -1) for b in early_biases], axis=1)
    early_bias = lax.psum_scatter(early_bias_rows, "img", scatter_dimension=0, tiled=True)
    early_slots = slot_sum(grad_gate_one, grad_mod_two, grad_scale_two, grad_gate_two)
    early_slots, early_bias = lax.psum((early_slots, early_bias), "blk")
    early_grad = lax.all_gather(early_slots, "img", axis=0, tiled=True)
    early_bias = early_bias.reshape(-1)
    (
        output_bias_sum,
        expand_bias_sum,
        shrink_bias_sum,
        inner_bias_sum,
        middle_bias_sum,
        outer_bias_sum,
    ) = (early_bias[sum(early_sizes[:i]) : sum(early_sizes[: i + 1])] for i in range(len(early_sizes)))

    qkv_bias = column_sum(grad_qkv).reshape(3, mine)
    late_slots = slot_sum(grad_mod_one, grad_scale_one)
    late_rows = jnp.concatenate(
        [late_slots, jnp.pad(qkv_bias, ((0, slots - 3), (0, 2 * width - mine)))], axis=0
    )
    late = lax.all_gather(late_rows, ("img", "blk"), axis=0, tiled=False)
    late = late.reshape(devices, parts, 2 * slots, 2 * width)
    late_grad = jnp.sum(late[:, :, :slots], axis=1).reshape(devices * slots, 2 * width)
    bias_all = jnp.sum(late[:, :, slots : slots + 3, :mine], axis=0)
    attend_bias_whole = jnp.concatenate([bias_all[:, 0].reshape(-1), bias_all[:, 2].reshape(-1)])
    attend_bias_sum = lax.dynamic_slice_in_dim(
        attend_bias_whole, place_img * attend_bias.shape[0], attend_bias.shape[0]
    )
    modulation_grad = jnp.concatenate([late_grad, early_grad], axis=1)
    modulate_sum = jnp.dot(silu_condition.astype(F32).T, modulation_grad, precision=HIGH)
    modulate_bias_sum = jnp.sum(modulation_grad, axis=0)
    silu_grad = jnp.dot(modulation_grad, modulate_weight.astype(F32).T, precision=HIGH)
    condition_grad = local_back(jax.nn.silu, condition, silu_grad)
    table_sum = jnp.dot(class_hot.astype(F32).T, condition_grad, precision=HIGH)
    return (
        whole_low,
        by_row(grad_source.astype(BF)),
        table_sum,
        modulate_sum,
        modulate_bias_sum,
        attend_sum.astype(F32),
        attend_bias_sum,
        output_sum.astype(F32),
        output_bias_sum,
        expand_sum.astype(F32),
        expand_bias_sum,
        shrink_sum.astype(F32),
        shrink_bias_sum,
        inner_sum.astype(F32),
        inner_bias_sum,
        middle_sum.astype(F32),
        middle_bias_sum,
        outer_sum.astype(F32),
        outer_bias_sum,
    )


def solution(mesh):
    in_specs = (
        P(("img", "blk"), None),
        P(("img", "blk")),
        P(),
        P(),
        P(("img", "blk"), None),
        P(("img", "blk"), None),
        P(None, "img"),
        P("img", None),
        P(),
        P("img", None),
        P("img"),
        P("img", None),
        P("img"),
        P("img", None),
        P("img"),
        P("img", None),
        P("img"),
        P("img", None),
        P("img"),
        P("img", None),
        P("img"),
        P("img", None),
        P("img"),
    )
    out_specs = (
        P(("img", "blk"), None),
        P(("img", "blk"), None),
        P(None, "img"),
        P("img", None),
        P(),
        P("img", None),
        P("img"),
        P("img", None),
        P("img"),
        P("img", None),
        P("img"),
        P("img", None),
        P("img"),
        P("img", None),
        P("img"),
        P("img", None),
        P("img"),
        P("img", None),
        P("img"),
    )
    return jax.shard_map(
        per_device, mesh=mesh, in_specs=in_specs, out_specs=out_specs, check_vma=False
    )
```

time: 2840 us -> 1110 us (0.39)
  waiting for transfers between devices: 1630 us -> 338 us
  local copies, waits for them, and re-layouts: 573 us -> 191 us
  matrix products: 426 us -> 203 us
  starting transfers between devices: 1.48 us -> 134 us
  Pallas kernels: 0 us -> 64.9 us
  blocking collectives: 89.4 us -> 54.9 us
  other arithmetic: 63 us -> 91.4 us
    reduce_scatter x10 -> x1, waiting for transfers between devices: 953 us -> 0.01 us  [per_device(): lax.psum_scatter(partial_mod_one, 'blk', scatter_dimension=0, tiled=True)]
    dynamic_update_slice x16 -> x0, local copies, waits for them, and re-layouts: 442 us -> none  [attend_backward(): lax.scan(step, jnp.zeros(query_heads.shape, jnp.float32), (key_blocks, va...]
    psum x1, waiting for transfers between devices: 422 us -> 0.01 us  [per_device(): early_slots, early_bias = lax.psum((early_slots, early_bias), 'blk')]
    all_gather x10 -> x9, waiting for transfers between devices: 252 us -> 0.04 us  [the longest x1 0.02 us: per_device(): middle_full = lax.all_gather(middle_weight, 'img', axis=0, tiled=True)]
    dot_general x56 -> x36, matrix products: 426 us -> 203 us  [the longest x8 65.8 us: dot(): return jnp.dot(left, right, preferred_element_type=F32)]
    ppermute x0 -> x53, waiting for transfers between devices: none -> 209 us  [the longest x6 69.3 us: line_sum(): lax.ppermute(values, 'blk', [(0, 1), (3, 2)]).astype(F32)]
    all_to_all x0 -> x4, waiting for transfers between devices: none -> 125 us  [the longest x1 82.7 us: per_device(): lax.all_to_all(jnp.broadcast_to(modulated_one, (parts, count, width)), 'b...]
    ppermute x0 -> x53, starting transfers between devices: none -> 104 us  [the longest x6 27.7 us: line_sum(): lax.ppermute(values, 'blk', [(1, 2), (2, 1)]).astype(F32)]
  transfers between devices with their start and end apart: 21 -> 68, of which waited for: 19 -> 23; matrix products, arithmetic and copies ran while one was open for 12% -> 35% of each run, Pallas kernels for 0% -> 6%
where the time goes in v1:
time: 1110 us; the launch traced here: 1090 us
  waiting for transfers between devices  338 us (30%)
  matrix products  203 us (18%)
  local copies, waits for them, and re-layouts  191 us (17%)
  starting transfers between devices  134 us (12%)
  other arithmetic  91.4 us (8%)
  Pallas kernels  64.9 us (6%)
  blocking collectives  54.9 us (5%)
  between operations  16.5 us (1%)
    all_to_all x1, waiting for transfers between devices, per_device(): lax.all_to_all(jnp.broadcast_to(modulated_one, (parts, count, width)), 'b...  82.7 us
    ppermute x6, waiting for transfers between devices, line_sum(): lax.ppermute(values, 'blk', [(0, 1), (3, 2)]).astype(F32)  69.3 us
    dot_general x8, matrix products, dot(): return jnp.dot(left, right, preferred_element_type=F32)  65.8 us
    dot_general x6, matrix products, right_product(): return jnp.einsum('to,io->ti', grad, weight, preferred_element_type=F32)  57.6 us
    ppermute x6, waiting for transfers between devices, line_sum(): lax.ppermute(values, 'blk', [(1, 2), (2, 1)]).astype(F32)  52.8 us
    pallas_call x1, Pallas kernels, attend_backward(): pl.pallas_call(partial(attend_backward_kernel, heads, 1.0 / math.sqrt(hea...  44.3 us
    all_to_all x1, waiting for transfers between devices, per_device(): got = lax.all_to_all(sent, 'img', split_axis=0, concat_axis=0, tiled=True)  42.6 us
    ppermute x6, waiting for transfers between devices, line_sum(): back = lax.ppermute(total, 'blk', [(1, 0), (2, 3)])  35 us
  transfers between devices with their start and end apart: 68, of which 23 were waited for; matrix products, arithmetic and copies ran while one was open for 35% of the time, Pallas kernels for 6%

profile of v1, /device:TPU:9, one launch (start us, length us, event | category | flops | bytes accessed | tf_op | source)
XLA Modules:
  0.0 1094.3 jit_solution(1247132544789493182)
XLA Ops:
  21.6 5.2 all-to-all-start
  28.3 42.6 %all-to-all-done = f32[8,9,6912]{2,1,0:T(8,128)} async-done(((f32[8,9,6912]{2,1,0:T(8,128)}), f32[8,9,6912]{2,1,0:T(8,128)}, u32[]{:S(2)}, u32[]{:S(2)}) %all-to-all-start) | async-done | bytes 1990688 | tf_op jit(solution)/shard_map/all_to_all | solution.py:282
  81.2 5.0 all-to-all-start.1
  101.2 82.7 %all-to-all-done.1 = bf16[4,512,1152]{1,2,0:T(8,128)(2,1)} async-done(((bf16[4,512,1152]{1,2,0:T(8,128)(2,1)}), bf16[4,512,1152]{1,2,0:T(8,128)(2,1)}, u32[]{:S(2)}, u32[]{:S(2)}) %all-to-all-start.1) | async-done | bytes 4718624 | tf_op jit(solution)/shard_map/all_to_all | solution.py:329
  183.9 6.8 copy.168
  190.7 13.2 %add_convert_fusion = bf16[2048,1536]{1,0:T(8,128)(2,1)} fusion(bf16[2048,1152]{1,0:T(8,128)(2,1)} %bitcast.454, bf16[1152,1536]{0,1:T(8,128)(2,1)} %bitcast.462, f32[1536]{0:T(1024)S(1)} %pad_bitcast_fusion), kind=kOutput, calls=%fused_computation.2 | convolution fusion | flops 7254048768 | bytes 14555136 | tf_op jit(solution)/shard_map/dot_general | solution.py:53
  203.9 20.6 %attend_forward.1 = bf16[4,8,64,288]{3,2,1,0:T(8,128)(2,1)S(1)} custom-call(s32[8]{0:T(128)S(1)} %get-tuple-element.20.start_ref, s32[8]{0:T(128)S(1)} %fusion.275.length_ref, bf16[4,8,64,1536]{3,2,1,0:T(8,128)(2,1)} %bitcast.514, bf16[512,288]{1,0:T(8,128)(2,1)S(1)} %and_convert_fusion.1.pick_ref), custom_call_target="tpu_custom_call" | custom-call | flops 10737418240 | bytes 16777216 | tf_op jit(solution)/shard_map/attend_forward/pallas_call | solution.py:146
  228.1 12.0 %all-to-all-start.2 = ((bf16[4,512,288]{1,2,0:T(8,128)(2,1)}), bf16[4,512,288]{1,2,0:T(8,128)(2,1)}, u32[]{:S(2)}, u32[]{:S(2)}) async-start(bf16[4,512,288]{1,2,0:T(8,128)(2,1)} %copy.171), calls=%async_computation.2 | async-start | bytes 2359296 | tf_op jit(solution)/shard_map/all_to_all | solution.py:344
  248.1 5.6 mul.495
  253.7 5.2 copy.182
  260.4 5.6 mul.489
  266.0 4.9 copy.177
  272.5 5.6 add.750
  278.2 5.1 copy.179
  284.8 5.6 mul.493
  290.5 5.0 copy.178
  296.3 17.8 %copy.173 = bf16[4,512,1152]{1,0,2:T(4,128)(2,1)} copy(bf16[4,512,1152]{1,2,0:T(8,128)(2,1)} %all-to-all-done.1) | data formatting | bytes 9437184 | tf_op jit(solution)/shard_map/all_to_all | solution.py:329
  314.1 9.2 reshape_reshape.8
  323.3 4.8 dynamic-slice_bitcast_fusion.15
  328.1 5.6 fusion.329
  342.4 14.8 %multiply_convert_fusion = (bf16[512,4608]{1,0:T(8,128)(2,1)}, f32[512,4608]{1,0:T(8,128)}) fusion(f32[4608]{0:T(1024)S(1)} %add.690, bf16[512,1152]{1,0:T(8,128)(2,1)S(1)} %fusion.22, bf16[1152,4608]{1,0:T(8,128)(2,1)} %all-gather.15.cloned.1.call-done), kind=kOutput, calls=%fused_computation.14 | convolution fusion | flops 5459410944 | bytes 25970688 | tf_op jit(solution)/shard_map/dot_general | solution.py:53
  357.2 6.7 copy.180
  363.9 12.6 %fusion.19 = (bf16[512,1152]{1,0:T(8,128)(2,1)S(1)}, f32[512,1152]{1,0:T(8,128)}) fusion(f32[512,1152]{1,0:T(8,128)} %copy-done.7, f32[8,1152]{1,0:T(8,128)S(1)} %get-tuple-element.149, f32[1152]{0:T(1024)S(1)} %add.695, bf16[512,4608]{1,0:T(8,128)(2,1)} %get-tuple-element.162, bf16[4608,1152]{1,0:T(8,128)(2,1)} %all-gather.17.cloned.1.call-done), kind=kOutput, calls=%fused_computation.66 | convolution fusion | flops 5438177280 | bytes 21275136 | tf_op jit(solution)/shard_map/dot_general | solution.py:53
  376.5 8.1 multiply_convert_fusion.2
  384.6 11.6 %multiply_convert_fusion.1 = (bf16[512,2048]{1,0:T(8,128)(2,1)}, f32[512,2048]{1,0:T(8,128)}) fusion(f32[2048]{0:T(1024)S(1)} %bitcast.508, bf16[512,2048]{1,0:T(8,128)(2,1)} %get-tuple-element.166, bf16[2048,2048]{1,0:T(8,128)(2,1)} %all-gather.21.cloned.1.call-done), kind=kOutput, calls=%fused_computation.32 | convolution fusion | flops 4301258752 | bytes 16785408 | tf_op jit(solution)/shard_map/dot_general | solution.py:53
  396.3 4.7 multiply_reduce_fusion.5
  406.3 10.6 convert_reduce_fusion.3
  417.0 4.5 convert_reduce_fusion.4
  421.4 15.9 %convert_reduce_fusion = (f32[4608]{0:T(1024)S(1)}, bf16[512,4608]{1,0:T(8,128)(2,1)S(1)}) fusion(f32[512,4608]{1,0:T(8,128)} %get-tuple-element.163, f32[4608]{0:T(1024)S(1)} %add.690, bf16[512,1152]{1,0:T(8,128)(2,1)S(1)} %get-tuple-element.51, bf16[4608,1152]{1,0:T(8,128)(2,1)} %all-gather.17.cloned.1.call-done), kind=kOutput, calls=%fused_computation.13 | convolution fusion | flops 5490077184 | bytes 25989120 | tf_op jit(solution)/shard_map/to,io->ti/dot_general | solution.py:45
  437.4 13.6 %fusion.66 = (f32[512]{0:T(512)S(1)}, f32[512]{0:T(512)S(1)}, f32[512,1152]{1,0:T(8,128)}) fusion(f32[8,1152]{1,0:T(8,128)S(1)} %get-tuple-element.151, f32[512]{0:T(512)S(1)} %add_rsqrt_fusion.2, f32[512,1152]{1,0:T(8,128)S(1)} %copy-done.8, f32[512]{0:T(512)S(1)} %broadcast_multiply_fusion.4, bf16[512,4608]{1,0:T(8,128)(2,1)S(1)} %get-tuple-element.53, ...), kind=kOutput, calls=%fused_computation.133 | convolution fusion | flops 5439355904 | bytes 20099072 | tf_op jit(solution)/shard_map/to,io->ti/dot_general | solution.py:45
  452.3 4.6 convert_reduce_fusion.5
  457.4 29.5 %all-reduce.4 = f32[8,1472]{1,0:T(8,128)S(1)} all-reduce(f32[8,1472]{1,0:T(8,128)S(1)} %concatenate.131), channel_id=4, replica_groups=mesh['img'=8,'blk'=4] {'img'}, use_global_device_ids=true, to_apply=%region_32.33.clone | all-reduce | flops 11776 | bytes 94208
  487.6 7.0 psum.15
  496.4 4.5 fusion.79
  500.9 6.6 all-to-all-start.3
  518.6 8.1 add_convert_fusion.11
  527.6 7.7 convolution_convert_fusion.1
  540.6 4.4 constant_dynamic-slice_fusion.16
  548.9 4.6 constant_dynamic-slice_fusion.8
  557.2 4.3 convolution_convert_fusion.3
  564.2 7.6 convolution_convert_fusion
  589.6 44.3 %attend_backward.1 = bf16[4,8,64,864]{3,2,1,0:T(8,128)(2,1)} custom-call(s32[8]{0:T(128)} %copy-done.2, s32[8]{0:T(128)} %copy-done.3, bf16[4,8,64,1536]{3,2,1,0:T(8,128)(2,1)} %bitcast.515, bf16[4,8,64,288]{3,2,1,0:T(8,128)(2,1)} %bitcast.475, bf16[288,512]{1,0:T(8,128)(2,1)} %and_convert_fusion.2.spread_ref, bf16[1536,864]{1,0:T(8,128)(2,1)} %and_convert_fusion.pick_ref), custom_call_target="tpu_custom_call" | custom-call | flops 42949672960 | bytes 16777216 | tf_op jit(solution)/shard_map/attend_backward/pallas_call | solution.py:166
  633.9 10.0 convolution_convert_fusion.2
  645.1 6.1 fusion.72
  652.0 13.6 %collective-permute-start.9 = (bf16[144,640]{1,0:T(8,128)(2,1)S(1)}, bf16[144,640]{1,0:T(8,128)(2,1)S(1)}, u32[]{:S(2)}, u32[]{:S(2)}) collective-permute-start(bf16[144,640]{1,0:T(8,128)(2,1)S(1)} %fusion.234), channel_id=1, source_target_pairs={{0,8},{4,12},{8,0},{12,4},{16,24},{20,28},{24,16},{28,20},{1,9},{5... | collective-permute-start | bytes 552968 | tf_op jit(solution)/shard_map/ppermute | solution.py:218
  684.2 17.0 %collective-permute-done.10 = bf16[144,1152]{1,0:T(8,128)(2,1)S(1)} collective-permute-done((bf16[144,1152]{1,0:T(8,128)(2,1)S(1)}, bf16[144,1152]{1,0:T(8,128)(2,1)S(1)}, u32[]{:S(2)}, u32[]{:S(2)}) %collective-permute-start.10) | collective-permute-done | bytes 331808 | tf_op jit(solution)/shard_map/ppermute | solution.py:227
  709.1 16.9 %collective-permute-done.11 = bf16[144,1152]{1,0:T(8,128)(2,1)S(1)} collective-permute-done((bf16[144,1152]{1,0:T(8,128)(2,1)S(1)}, bf16[144,1152]{1,0:T(8,128)(2,1)S(1)}, u32[]{:S(2)}, u32[]{:S(2)}) %collective-permute-start.11) | collective-permute-done | bytes 331808 | tf_op jit(solution)/shard_map/ppermute | solution.py:228
  732.7 12.7 %collective-permute-done.12 = bf16[144,1152]{1,0:T(8,128)(2,1)S(1)} collective-permute-done((bf16[144,1152]{1,0:T(8,128)(2,1)S(1)}, bf16[144,1152]{1,0:T(8,128)(2,1)S(1)}, u32[]{:S(2)}, u32[]{:S(2)}) %collective-permute-start.12) | collective-permute-done | bytes 331808 | tf_op jit(solution)/shard_map/ppermute | solution.py:229
  745.3 10.2 collective-permute-start.51
  781.1 7.9 collective-permute-done.34
  799.2 18.5 %all_gather.44 = bf16[4,144,864]{2,1,0:T(8,128)(2,1)S(1)} all-gather(bf16[1,144,864]{2,1,0:T(8,128)(2,1)S(1)} %pad_maximum_fusion.16), channel_id=1, replica_groups=mesh['img'=8,'blk'=4] {'blk'}, dimensions={0}, use_global_device_ids=true | all-gather | bytes 1244160 | tf_op jit(solution)/shard_map/all_gather | solution.py:416
  820.9 5.2 copy.174
  841.5 7.0 add_convert_fusion.2
  850.4 6.8 add_convert_fusion.1
  865.2 11.8 %collective-permute-done.14 = bf16[2,144,2304]{2,1,0:T(8,128)(2,1)S(1)} collective-permute-done((bf16[2,144,2304]{2,1,0:T(8,128)(2,1)S(1)}, bf16[2,144,2304]{2,1,0:T(8,128)(2,1)S(1)}, u32[]{:S(2)}, u32[]{:S(2)}) %collective-permute-start.14) | collective-permute-done | bytes 1327136 | tf_op jit(solution)/shard_map/ppermute | solution.py:213
  883.7 6.0 bitcast_reduce_fusion.1
  893.1 9.3 collective-permute-done.22
  915.0 9.2 collective-permute-done.15
  929.4 5.1 collective-permute-start.43
  941.0 14.5 %collective-permute-done.18 = bf16[144,4608]{1,0:T(8,128)(2,1)S(1)} collective-permute-done((bf16[144,4608]{1,0:T(8,128)(2,1)S(1)}, bf16[144,4608]{1,0:T(8,128)(2,1)S(1)}, u32[]{:S(2)}, u32[]{:S(2)}) %collective-permute-start.18) | collective-permute-done | bytes 1327136 | tf_op jit(solution)/shard_map/ppermute | solution.py:227
  963.4 30.0 %collective-permute-done.26 = bf16[576,1152]{1,0:T(8,128)(2,1)S(1)} collective-permute-done((bf16[576,1152]{1,0:T(8,128)(2,1)S(1)}, bf16[576,1152]{1,0:T(8,128)(2,1)S(1)}, u32[]{:S(2)}, u32[]{:S(2)}) %collective-permute-start.26) | collective-permute-done | bytes 1327136 | tf_op jit(solution)/shard_map/ppermute | solution.py:227
  1002.7 34.8 %collective-permute-done.27 = bf16[576,1152]{1,0:T(8,128)(2,1)S(1)} collective-permute-done((bf16[576,1152]{1,0:T(8,128)(2,1)S(1)}, bf16[576,1152]{1,0:T(8,128)(2,1)S(1)}, u32[]{:S(2)}, u32[]{:S(2)}) %collective-permute-start.27) | collective-permute-done | bytes 1327136 | tf_op jit(solution)/shard_map/ppermute | solution.py:228
  1047.1 22.4 %collective-permute-done.28 = bf16[576,1152]{1,0:T(8,128)(2,1)} collective-permute-done((bf16[576,1152]{1,0:T(8,128)(2,1)}, bf16[576,1152]{1,0:T(8,128)(2,1)}, u32[]{:S(2)}, u32[]{:S(2)}) %collective-permute-start.28) | collective-permute-done | bytes 1327136 | tf_op jit(solution)/shard_map/ppermute | solution.py:229
  1082.0 4.8 fusion.94
  (582 shorter events, 293.8 us)
Async XLA Ops:
  7.2 86.1 %all-gather.11.cloned.1.call-start = ((), (), s32[]{:S(2)}) async-start(), calls=%async_computation.5 | async-start | bytes 2322432 | tf_op jit(solution)/shard_map/all_gather | solution.py:318
  14.5 313.5 %all-gather.13.cloned.1.call-start = ((), (), s32[]{:S(2)}) async-start(), calls=%async_computation.6 | async-start | bytes 2985984 | tf_op jit(solution)/shard_map/all_gather | solution.py:319
  15.3 327.1 %all-gather.15.cloned.1.call-start = ((), (), s32[]{:S(2)}) async-start(), calls=%async_computation.7 | async-start | bytes 11943936 | tf_op jit(solution)/shard_map/all_gather | solution.py:320
  16.0 347.9 %all-gather.17.cloned.1.call-start = ((), (), s32[]{:S(2)}) async-start(), calls=%async_computation.8 | async-start | bytes 11943936 | tf_op jit(solution)/shard_map/all_gather | solution.py:321
  16.6 359.9 %all-gather.19.cloned.1.call-start = ((), (), s32[]{:S(2)}) async-start(), calls=%async_computation.9 | async-start | bytes 5308416 | tf_op jit(solution)/shard_map/all_gather | solution.py:322
  17.2 367.4 %all-gather.21.cloned.1.call-start = ((), (), s32[]{:S(2)}) async-start(), calls=%async_computation.10 | async-start | bytes 9437184 | tf_op jit(solution)/shard_map/all_gather | solution.py:323
  21.6 49.3 %all-to-all-start = ((f32[8,9,6912]{2,1,0:T(8,128)}), f32[8,9,6912]{2,1,0:T(8,128)}, u32[]{:S(2)}, u32[]{:S(2)}) async-start(f32[8,9,6912]{2,1,0:T(8,128)} %pad_maximum_fusion), calls=%async_computation | async-start | bytes 7077888 | tf_op jit(solution)/shard_map/all_to_all | solution.py:282
  81.2 102.7 %all-to-all-start.1 = ((bf16[4,512,1152]{1,2,0:T(8,128)(2,1)}), bf16[4,512,1152]{1,2,0:T(8,128)(2,1)}, u32[]{:S(2)}, u32[]{:S(2)}) async-start(bf16[4,512,1152]{1,2,0:T(8,128)(2,1)} %broadcast_in_dim.16), calls=%async_computation.1 | async-start | bytes 9437184 | tf_op jit(solution)/shard_map/all_to_all | solution.py:329
  86.3 310.0 %all-gather.23.cloned.1.call-start = ((), (), s32[]{:S(2)}) async-start(), calls=%async_computation.11 | async-start | bytes 3538944 | tf_op jit(solution)/shard_map/all_gather | solution.py:324
  228.1 99.9 %all-to-all-start.2 = ((bf16[4,512,288]{1,2,0:T(8,128)(2,1)}), bf16[4,512,288]{1,2,0:T(8,128)(2,1)}, u32[]{:S(2)}, u32[]{:S(2)}) async-start(bf16[4,512,288]{1,2,0:T(8,128)(2,1)} %copy.171), calls=%async_computation.2 | async-start | bytes 2359296 | tf_op jit(solution)/shard_map/all_to_all | solution.py:344
  500.9 87.2 %all-to-all-start.3 = ((bf16[4,512,288]{1,2,0:T(8,128)(2,1)}), bf16[4,512,288]{1,2,0:T(8,128)(2,1)S(1)}, u32[]{:S(2)}, u32[]{:S(2)}) async-start(bf16[4,512,288]{1,2,0:T(8,128)(2,1)} %fusion.79), calls=%async_computation.3 | async-start | bytes 2359296 | tf_op jit(solution)/shard_map/all_to_all | solution.py:411
  507.5 376.1 %reduce-scatter.2.cloned.1.call-start = ((), (), s32[]{:S(2)}) async-start(), calls=%async_computation.12 | async-start | bytes 5898240 | tf_op jit(solution)/shard_map/reduce_scatter | solution.py:422
  511.0 60.8 %collective-permute-start.5 = (bf16[576,1152]{1,0:T(8,128)(2,1)}, bf16[576,1152]{1,0:T(8,128)(2,1)}, u32[]{:S(2)}, u32[]{:S(2)}) collective-permute-start(bf16[576,1152]{1,0:T(8,128)(2,1)} %convolution_convert_fusion.5), channel_id=1, source_target_pairs={{0,4},{4,0},{8,12},{12,8},{16,20},{20,16},{24,28},{28,24},{1,5},{5... | collective-permute-start | bytes 3981320 | tf_op jit(solution)/shard_map/ppermute | solution.py:208
  535.3 306.1 %collective-permute-start.13 = (bf16[576,4608]{1,0:T(8,128)(2,1)}, bf16[576,4608]{1,0:T(8,128)(2,1)}, u32[]{:S(2)}, u32[]{:S(2)}) collective-permute-start(bf16[576,4608]{1,0:T(8,128)(2,1)} %convolution_convert_fusion.1), channel_id=1, source_target_pairs={{0,4},{4,0},{8,12},{12,8},{16,20},{20,16},{24,28},{28,24},{1,5},{5... | collective-permute-start | bytes 15925256 | tf_op jit(solution)/shard_map/ppermute | solution.py:208
  539.9 162.7 %collective-permute-start.29 = (bf16[576,2048]{1,0:T(8,128)(2,1)}, bf16[576,2048]{1,0:T(8,128)(2,1)}, u32[]{:S(2)}, u32[]{:S(2)}) collective-permute-start(bf16[576,2048]{1,0:T(8,128)(2,1)} %convolution_convert_fusion.4), channel_id=1, source_target_pairs={{0,4},{4,0},{8,12},{12,8},{16,20},{20,16},{24,28},{28,24},{1,5},{5... | collective-permute-start | bytes 7077896 | tf_op jit(solution)/shard_map/ppermute | solution.py:208
  555.6 21.3 %collective-permute-start.45 = (bf16[1024,768]{1,0:T(8,128)(2,1)S(1)}, bf16[1024,768]{1,0:T(8,128)(2,1)S(1)}, u32[]{:S(2)}, u32[]{:S(2)}) collective-permute-start(bf16[1024,768]{1,0:T(8,128)(2,1)S(1)} %convolution_convert_fusion.6), channel_id=1, source_target_pairs={{0,4},{4,0},{8,12},{12,8},{16,20},{20,16},{24,28},{28,24},{1,5},{5... | collective-permute-start | bytes 4718600 | tf_op jit(solution)/shard_map/ppermute | solution.py:208
  574.2 11.7 %collective-permute-start.8 = (bf16[2,144,640]{2,1,0:T(8,128)(2,1)S(1)}, bf16[2,144,640]{2,1,0:T(8,128)(2,1)S(1)}, u32[]{:S(2)}, u32[]{:S(2)}) collective-permute-start(bf16[2,144,640]{2,1,0:T(8,128)(2,1)S(1)} %stack.57), channel_id=1, source_target_pairs={{0,16},{4,20},{8,24},{12,28},{16,0},{20,4},{24,8},{28,12},{1,17},{... | collective-permute-start | bytes 1105928 | tf_op jit(solution)/shard_map/ppermute | solution.py:214
  576.9 7.8 collective-permute-start.6
  579.7 90.2 %collective-permute-start.46 = (bf16[2,256,384]{2,1,0:T(8,128)(2,1)}, bf16[2,256,384]{2,1,0:T(8,128)(2,1)}, u32[]{:S(2)}, u32[]{:S(2)}) collective-permute-start(bf16[2,256,384]{2,1,0:T(8,128)(2,1)} %pad_maximum_fusion.12), channel_id=1, source_target_pairs={{0,8},{4,12},{8,0},{12,4},{16,24},{20,28},{24,16},{28,20},{1,9},{5... | collective-permute-start | bytes 1179656 | tf_op jit(solution)/shard_map/ppermute | solution.py:213
  584.7 86.4 %collective-permute-start.48 = (bf16[2,256,384]{2,1,0:T(8,128)(2,1)}, bf16[2,256,384]{2,1,0:T(8,128)(2,1)}, u32[]{:S(2)}, u32[]{:S(2)}) collective-permute-start(bf16[2,256,384]{2,1,0:T(8,128)(2,1)} %stack.62), channel_id=1, source_target_pairs={{0,16},{4,20},{8,24},{12,28},{16,0},{20,4},{24,8},{28,12},{1,17},{... | collective-permute-start | bytes 1179656 | tf_op jit(solution)/shard_map/ppermute | solution.py:214
  585.9 66.1 %collective-permute-start.7 = (bf16[144,512]{1,0:T(8,128)(2,1)}, bf16[144,512]{1,0:T(8,128)(2,1)}, u32[]{:S(2)}, u32[]{:S(2)}) collective-permute-start(bf16[144,512]{1,0:T(8,128)(2,1)} %fusion.237), channel_id=1, source_target_pairs={{0,16},{4,20},{8,24},{12,28},{16,0},{20,4},{24,8},{28,12},{1,17},{... | collective-permute-start | bytes 442376 | tf_op jit(solution)/shard_map/ppermute | solution.py:217
  643.9 400.2 %all-reduce.7.cloned.1.call-start = ((), (), s32[]{:S(2)}) async-start(), calls=%async_computation.13 | async-start | bytes 294912 | tf_op jit(solution)/shard_map/psum | solution.py:443
  652.0 16.9 %collective-permute-start.9 = (bf16[144,640]{1,0:T(8,128)(2,1)S(1)}, bf16[144,640]{1,0:T(8,128)(2,1)S(1)}, u32[]{:S(2)}, u32[]{:S(2)}) collective-permute-start(bf16[144,640]{1,0:T(8,128)(2,1)S(1)} %fusion.234), channel_id=1, source_target_pairs={{0,8},{4,12},{8,0},{12,4},{16,24},{20,28},{24,16},{28,20},{1,9},{5... | collective-permute-start | bytes 552968 | tf_op jit(solution)/shard_map/ppermute | solution.py:218
  668.9 123.0 %collective-permute-start.37 = (bf16[1024,2048]{1,0:T(8,128)(2,1)}, bf16[1024,2048]{1,0:T(8,128)(2,1)S(1)}, u32[]{:S(2)}, u32[]{:S(2)}) collective-permute-start(bf16[1024,2048]{1,0:T(8,128)(2,1)} %convolution_convert_fusion.3), channel_id=1, source_target_pairs={{0,4},{4,0},{8,12},{12,8},{16,20},{20,16},{24,28},{28,24},{1,5},{5... | collective-permute-start | bytes 12582920 | tf_op jit(solution)/shard_map/ppermute | solution.py:208
  672.3 8.9 collective-permute-start.47
  681.2 47.4 %collective-permute-start = (bf16[576,864]{1,0:T(8,128)(2,1)S(1)}, bf16[576,864]{1,0:T(8,128)(2,1)S(1)}, u32[]{:S(2)}, u32[]{:S(2)}) collective-permute-start(bf16[576,864]{1,0:T(8,128)(2,1)S(1)} %copy-done.103), channel_id=1, source_target_pairs={{0,4},{4,0},{8,12},{12,8},{16,20},{20,16},{24,28},{28,24},{1,5},{5... | collective-permute-start | bytes 2985992 | tf_op jit(solution)/shard_map/ppermute | solution.py:208
  682.7 18.5 %collective-permute-start.10 = (bf16[144,1152]{1,0:T(8,128)(2,1)S(1)}, bf16[144,1152]{1,0:T(8,128)(2,1)S(1)}, u32[]{:S(2)}, u32[]{:S(2)}) collective-permute-start(bf16[144,1152]{1,0:T(8,128)(2,1)S(1)} %pad_maximum_fusion.14), channel_id=1, source_target_pairs={{0,1},{3,2},{4,5},{7,6},{8,9},{11,10},{12,13},{15,14},{16,17},{19,... | collective-permute-start | bytes 995336 | tf_op jit(solution)/shard_map/ppermute | solution.py:227
  701.2 26.0 %collective-permute-start.50 = (bf16[256,768]{1,0:T(8,128)(2,1)S(1)}, bf16[256,768]{1,0:T(8,128)(2,1)S(1)}, u32[]{:S(2)}, u32[]{:S(2)}) collective-permute-start(bf16[256,768]{1,0:T(8,128)(2,1)S(1)} %pad_maximum_fusion.13), channel_id=1, source_target_pairs={{0,1},{3,2},{4,5},{7,6},{8,9},{11,10},{12,13},{15,14},{16,17},{19,... | collective-permute-start | bytes 1179656 | tf_op jit(solution)/shard_map/ppermute | solution.py:227
  702.6 23.5 %collective-permute-start.11 = (bf16[144,1152]{1,0:T(8,128)(2,1)S(1)}, bf16[144,1152]{1,0:T(8,128)(2,1)S(1)}, u32[]{:S(2)}, u32[]{:S(2)}) collective-permute-start(bf16[144,1152]{1,0:T(8,128)(2,1)S(1)} %add_convert_fusion.21), channel_id=1, source_target_pairs={{1,2},{2,1},{5,6},{6,5},{9,10},{10,9},{13,14},{14,13},{17,18},{18,... | collective-permute-start | bytes 995336 | tf_op jit(solution)/shard_map/ppermute | solution.py:228
  726.1 30.4 %collective-permute-start.30 = (bf16[2,144,1024]{2,1,0:T(8,128)(2,1)S(1)}, bf16[2,144,1024]{2,1,0:T(8,128)(2,1)S(1)}, u32[]{:S(2)}, u32[]{:S(2)}) collective-permute-start(bf16[2,144,1024]{2,1,0:T(8,128)(2,1)S(1)} %pad_maximum_fusion.10), channel_id=1, source_target_pairs={{0,8},{4,12},{8,0},{12,4},{16,24},{20,28},{24,16},{28,20},{1,9},{5... | collective-permute-start | bytes 1769480 | tf_op jit(solution)/shard_map/ppermute | solution.py:213
  727.2 30.6 %collective-permute-start.32 = (bf16[2,144,1024]{2,1,0:T(8,128)(2,1)S(1)}, bf16[2,144,1024]{2,1,0:T(8,128)(2,1)S(1)}, u32[]{:S(2)}, u32[]{:S(2)}) collective-permute-start(bf16[2,144,1024]{2,1,0:T(8,128)(2,1)S(1)} %stack.60), channel_id=1, source_target_pairs={{0,16},{4,20},{8,24},{12,28},{16,0},{20,4},{24,8},{28,12},{1,17},{... | collective-permute-start | bytes 1769480 | tf_op jit(solution)/shard_map/ppermute | solution.py:214
  728.6 16.8 %collective-permute-start.12 = (bf16[144,1152]{1,0:T(8,128)(2,1)S(1)}, bf16[144,1152]{1,0:T(8,128)(2,1)S(1)}, u32[]{:S(2)}, u32[]{:S(2)}) collective-permute-start(bf16[144,1152]{1,0:T(8,128)(2,1)S(1)} %add_convert_fusion.20), channel_id=1, source_target_pairs={{1,0},{2,3},{5,4},{6,7},{9,8},{10,11},{13,12},{14,15},{17,16},{18,... | collective-permute-start | bytes 995336 | tf_op jit(solution)/shard_map/ppermute | solution.py:229
  745.3 15.4 %collective-permute-start.51 = (bf16[256,768]{1,0:T(8,128)(2,1)S(1)}, bf16[256,768]{1,0:T(8,128)(2,1)S(1)}, u32[]{:S(2)}, u32[]{:S(2)}) collective-permute-start(bf16[256,768]{1,0:T(8,128)(2,1)S(1)} %add_convert_fusion.19), channel_id=1, source_target_pairs={{1,2},{2,1},{5,6},{6,5},{9,10},{10,9},{13,14},{14,13},{17,18},{18,... | collective-permute-start | bytes 1179656 | tf_op jit(solution)/shard_map/ppermute | solution.py:228
  756.5 10.4 collective-permute-start.3
  757.9 7.2 collective-permute-start.1
  760.7 11.3 %collective-permute-start.31 = (bf16[144,1024]{1,0:T(8,128)(2,1)S(1)}, bf16[144,1024]{1,0:T(8,128)(2,1)S(1)}, u32[]{:S(2)}, u32[]{:S(2)}) collective-permute-start(bf16[144,1024]{1,0:T(8,128)(2,1)S(1)} %get-tuple-element.95), channel_id=1, source_target_pairs={{0,16},{4,20},{8,24},{12,28},{16,0},{20,4},{24,8},{28,12},{1,17},{... | collective-permute-start | bytes 884744 | tf_op jit(solution)/shard_map/ppermute | solution.py:217
  766.8 82.7 %collective-permute-start.21 = (bf16[2304,1152]{1,0:T(8,128)(2,1)}, bf16[2304,1152]{1,0:T(8,128)(2,1)}, u32[]{:S(2)}, u32[]{:S(2)}) collective-permute-start(bf16[2304,1152]{1,0:T(8,128)(2,1)} %convolution_convert_fusion), channel_id=1, source_target_pairs={{0,4},{4,0},{8,12},{12,8},{16,20},{20,16},{24,28},{28,24},{1,5},{5... | collective-permute-start | bytes 15925256 | tf_op jit(solution)/shard_map/ppermute | solution.py:208
  775.6 13.4 %collective-permute-start.34 = (bf16[144,2048]{1,0:T(8,128)(2,1)S(1)}, bf16[144,2048]{1,0:T(8,128)(2,1)S(1)}, u32[]{:S(2)}, u32[]{:S(2)}) collective-permute-start(bf16[144,2048]{1,0:T(8,128)(2,1)S(1)} %pad_maximum_fusion.11), channel_id=1, source_target_pairs={{0,1},{3,2},{4,5},{7,6},{8,9},{11,10},{12,13},{15,14},{16,17},{19,... | collective-permute-start | bytes 1769480 | tf_op jit(solution)/shard_map/ppermute | solution.py:227
  776.9 20.7 %collective-permute-start.52 = (bf16[256,768]{1,0:T(8,128)(2,1)S(1)}, bf16[256,768]{1,0:T(8,128)(2,1)S(1)}, u32[]{:S(2)}, u32[]{:S(2)}) collective-permute-start(bf16[256,768]{1,0:T(8,128)(2,1)S(1)} %add_convert_fusion.18), channel_id=1, source_target_pairs={{1,0},{2,3},{5,4},{6,7},{9,8},{10,11},{13,12},{14,15},{17,16},{18,... | collective-permute-start | bytes 1179656 | tf_op jit(solution)/shard_map/ppermute | solution.py:229
  790.0 40.7 %collective-permute-start.35 = (bf16[144,2048]{1,0:T(8,128)(2,1)}, bf16[144,2048]{1,0:T(8,128)(2,1)}, u32[]{:S(2)}, u32[]{:S(2)}) collective-permute-start(bf16[144,2048]{1,0:T(8,128)(2,1)} %add_convert_fusion.17), channel_id=1, source_target_pairs={{1,2},{2,1},{5,6},{6,5},{9,10},{10,9},{13,14},{14,13},{17,18},{18,... | collective-permute-start | bytes 1769480 | tf_op jit(solution)/shard_map/ppermute | solution.py:228
  797.0 38.6 %collective-permute-start.38 = (bf16[2,256,1024]{2,1,0:T(8,128)(2,1)}, bf16[2,256,1024]{2,1,0:T(8,128)(2,1)}, u32[]{:S(2)}, u32[]{:S(2)}) collective-permute-start(bf16[2,256,1024]{2,1,0:T(8,128)(2,1)} %pad_maximum_fusion.8), channel_id=1, source_target_pairs={{0,8},{4,12},{8,0},{12,4},{16,24},{20,28},{24,16},{28,20},{1,9},{5... | collective-permute-start | bytes 3145736 | tf_op jit(solution)/shard_map/ppermute | solution.py:213
  798.4 38.7 %collective-permute-start.40 = (bf16[2,256,1024]{2,1,0:T(8,128)(2,1)}, bf16[2,256,1024]{2,1,0:T(8,128)(2,1)}, u32[]{:S(2)}, u32[]{:S(2)}) collective-permute-start(bf16[2,256,1024]{2,1,0:T(8,128)(2,1)} %stack.61), channel_id=1, source_target_pairs={{0,16},{4,20},{8,24},{12,28},{16,0},{20,4},{24,8},{28,12},{1,17},{... | collective-permute-start | bytes 3145736 | tf_op jit(solution)/shard_map/ppermute | solution.py:214
  832.9 126.7 %collective-permute-start.36 = (bf16[144,2048]{1,0:T(8,128)(2,1)}, bf16[144,2048]{1,0:T(8,128)(2,1)}, u32[]{:S(2)}, u32[]{:S(2)}) collective-permute-start(bf16[144,2048]{1,0:T(8,128)(2,1)} %add_convert_fusion.16), channel_id=1, source_target_pairs={{1,0},{2,3},{5,4},{6,7},{9,8},{10,11},{13,12},{14,15},{17,16},{18,... | collective-permute-start | bytes 1769480 | tf_op jit(solution)/shard_map/ppermute | solution.py:229
  840.0 21.1 %collective-permute-start.39 = (bf16[256,1024]{1,0:T(8,128)(2,1)}, bf16[256,1024]{1,0:T(8,128)(2,1)}, u32[]{:S(2)}, u32[]{:S(2)}) collective-permute-start(bf16[256,1024]{1,0:T(8,128)(2,1)} %get-tuple-element.87), channel_id=1, source_target_pairs={{0,16},{4,20},{8,24},{12,28},{16,0},{20,4},{24,8},{28,12},{1,17},{... | collective-permute-start | bytes 1572872 | tf_op jit(solution)/shard_map/ppermute | solution.py:217
  840.6 21.0 %collective-permute-start.41 = (bf16[256,1024]{1,0:T(8,128)(2,1)}, bf16[256,1024]{1,0:T(8,128)(2,1)}, u32[]{:S(2)}, u32[]{:S(2)}) collective-permute-start(bf16[256,1024]{1,0:T(8,128)(2,1)} %get-tuple-element.88), channel_id=1, source_target_pairs={{0,8},{4,12},{8,0},{12,4},{16,24},{20,28},{24,16},{28,20},{1,9},{5... | collective-permute-start | bytes 1572872 | tf_op jit(solution)/shard_map/ppermute | solution.py:218
  848.9 28.2 %collective-permute-start.14 = (bf16[2,144,2304]{2,1,0:T(8,128)(2,1)S(1)}, bf16[2,144,2304]{2,1,0:T(8,128)(2,1)S(1)}, u32[]{:S(2)}, u32[]{:S(2)}) collective-permute-start(bf16[2,144,2304]{2,1,0:T(8,128)(2,1)S(1)} %pad_maximum_fusion.2), channel_id=1, source_target_pairs={{0,8},{4,12},{8,0},{12,4},{16,24},{20,28},{24,16},{28,20},{1,9},{5... | collective-permute-start | bytes 3981320 | tf_op jit(solution)/shard_map/ppermute | solution.py:213
  849.6 28.8 %collective-permute-start.16 = (bf16[2,144,2304]{2,1,0:T(8,128)(2,1)S(1)}, bf16[2,144,2304]{2,1,0:T(8,128)(2,1)}, u32[]{:S(2)}, u32[]{:S(2)}) collective-permute-start(bf16[2,144,2304]{2,1,0:T(8,128)(2,1)S(1)} %stack.58), channel_id=1, source_target_pairs={{0,16},{4,20},{8,24},{12,28},{16,0},{20,4},{24,8},{28,12},{1,17},{... | collective-permute-start | bytes 3981320 | tf_op jit(solution)/shard_map/ppermute | solution.py:214
  861.0 49.0 %collective-permute-start.24 = (bf16[2,576,640]{2,1,0:T(8,128)(2,1)}, bf16[2,576,640]{2,1,0:T(8,128)(2,1)}, u32[]{:S(2)}, u32[]{:S(2)}) collective-permute-start(bf16[2,576,640]{2,1,0:T(8,128)(2,1)} %stack.59), channel_id=1, source_target_pairs={{0,16},{4,20},{8,24},{12,28},{16,0},{20,4},{24,8},{28,12},{1,17},{... | collective-permute-start | bytes 4423688 | tf_op jit(solution)/shard_map/ppermute | solution.py:214
  861.6 40.8 %collective-permute-start.22 = (bf16[2,576,512]{2,1,0:T(8,128)(2,1)}, bf16[2,576,512]{2,1,0:T(8,128)(2,1)}, u32[]{:S(2)}, u32[]{:S(2)}) collective-permute-start(bf16[2,576,512]{2,1,0:T(8,128)(2,1)} %pad_maximum_fusion.5), channel_id=1, source_target_pairs={{0,8},{4,12},{8,0},{12,4},{16,24},{20,28},{24,16},{28,20},{1,9},{5... | collective-permute-start | bytes 3538952 | tf_op jit(solution)/shard_map/ppermute | solution.py:213
  881.8 42.4 %collective-permute-start.15 = (bf16[144,2304]{1,0:T(8,128)(2,1)}, bf16[144,2304]{1,0:T(8,128)(2,1)}, u32[]{:S(2)}, u32[]{:S(2)}) collective-permute-start(bf16[144,2304]{1,0:T(8,128)(2,1)} %get-tuple-element.65), channel_id=1, source_target_pairs={{0,16},{4,20},{8,24},{12,28},{16,0},{20,4},{24,8},{28,12},{1,17},{... | collective-permute-start | bytes 1990664 | tf_op jit(solution)/shard_map/ppermute | solution.py:217
  883.6 41.6 %collective-permute-start.17 = (bf16[144,2304]{1,0:T(8,128)(2,1)}, bf16[144,2304]{1,0:T(8,128)(2,1)}, u32[]{:S(2)}, u32[]{:S(2)}) collective-permute-start(bf16[144,2304]{1,0:T(8,128)(2,1)} %get-tuple-element.66), channel_id=1, source_target_pairs={{0,8},{4,12},{8,0},{12,4},{16,24},{20,28},{24,16},{28,20},{1,9},{5... | collective-permute-start | bytes 1990664 | tf_op jit(solution)/shard_map/ppermute | solution.py:218
  890.7 181.8 %all-gather.27.cloned.1.call-start = ((), (), s32[]{:S(2)}) async-start(), calls=%async_computation.15 | async-start | bytes 4866048 | tf_op jit(solution)/shard_map/all_gather | solution.py:460
  891.8 184.4 %all-gather.25.cloned.1.call-start = ((), (), s32[]{:S(2)}) async-start(), calls=%async_computation.14 | async-start | bytes 1327104 | tf_op jit(solution)/shard_map/all_gather | solution.py:444
  902.4 26.6 %collective-permute-start.42 = (bf16[256,2048]{1,0:T(8,128)(2,1)S(1)}, bf16[256,2048]{1,0:T(8,128)(2,1)S(1)}, u32[]{:S(2)}, u32[]{:S(2)}) collective-permute-start(bf16[256,2048]{1,0:T(8,128)(2,1)S(1)} %pad_maximum_fusion.9), channel_id=1, source_target_pairs={{0,1},{3,2},{4,5},{7,6},{8,9},{11,10},{12,13},{15,14},{16,17},{19,... | collective-permute-start | bytes 3145736 | tf_op jit(solution)/shard_map/ppermute | solution.py:227
  910.0 26.9 %collective-permute-start.23 = (bf16[576,512]{1,0:T(8,128)(2,1)S(1)}, bf16[576,512]{1,0:T(8,128)(2,1)S(1)}, u32[]{:S(2)}, u32[]{:S(2)}) collective-permute-start(bf16[576,512]{1,0:T(8,128)(2,1)S(1)} %fusion.141), channel_id=1, source_target_pairs={{0,16},{4,20},{8,24},{12,28},{16,0},{20,4},{24,8},{28,12},{1,17},{... | collective-permute-start | bytes 1769480 | tf_op jit(solution)/shard_map/ppermute | solution.py:217
  924.2 14.0 %collective-permute-start.25 = (bf16[576,640]{1,0:T(8,128)(2,1)S(1)}, bf16[576,640]{1,0:T(8,128)(2,1)S(1)}, u32[]{:S(2)}, u32[]{:S(2)}) collective-permute-start(bf16[576,640]{1,0:T(8,128)(2,1)S(1)} %fusion.138), channel_id=1, source_target_pairs={{0,8},{4,12},{8,0},{12,4},{16,24},{20,28},{24,16},{28,20},{1,9},{5... | collective-permute-start | bytes 2211848 | tf_op jit(solution)/shard_map/ppermute | solution.py:218
  927.5 28.0 %collective-permute-start.18 = (bf16[144,4608]{1,0:T(8,128)(2,1)S(1)}, bf16[144,4608]{1,0:T(8,128)(2,1)S(1)}, u32[]{:S(2)}, u32[]{:S(2)}) collective-permute-start(bf16[144,4608]{1,0:T(8,128)(2,1)S(1)} %pad_maximum_fusion.3), channel_id=1, source_target_pairs={{0,1},{3,2},{4,5},{7,6},{8,9},{11,10},{12,13},{15,14},{16,17},{19,... | collective-permute-start | bytes 3981320 | tf_op jit(solution)/shard_map/ppermute | solution.py:227
  929.4 32.3 %collective-permute-start.43 = (bf16[256,2048]{1,0:T(8,128)(2,1)S(1)}, bf16[256,2048]{1,0:T(8,128)(2,1)S(1)}, u32[]{:S(2)}, u32[]{:S(2)}) collective-permute-start(bf16[256,2048]{1,0:T(8,128)(2,1)S(1)} %add_convert_fusion.14), channel_id=1, source_target_pairs={{1,2},{2,1},{5,6},{6,5},{9,10},{10,9},{13,14},{14,13},{17,18},{18,... | collective-permute-start | bytes 3145736 | tf_op jit(solution)/shard_map/ppermute | solution.py:228
  939.7 53.7 %collective-permute-start.26 = (bf16[576,1152]{1,0:T(8,128)(2,1)S(1)}, bf16[576,1152]{1,0:T(8,128)(2,1)S(1)}, u32[]{:S(2)}, u32[]{:S(2)}) collective-permute-start(bf16[576,1152]{1,0:T(8,128)(2,1)S(1)} %pad_maximum_fusion.4), channel_id=1, source_target_pairs={{0,1},{3,2},{4,5},{7,6},{8,9},{11,10},{12,13},{15,14},{16,17},{19,... | collective-permute-start | bytes 3981320 | tf_op jit(solution)/shard_map/ppermute | solution.py:227
  955.8 41.6 %collective-permute-start.19 = (bf16[144,4608]{1,0:T(8,128)(2,1)S(1)}, bf16[144,4608]{1,0:T(8,128)(2,1)S(1)}, u32[]{:S(2)}, u32[]{:S(2)}) collective-permute-start(bf16[144,4608]{1,0:T(8,128)(2,1)S(1)} %add_convert_fusion.9), channel_id=1, source_target_pairs={{1,2},{2,1},{5,6},{6,5},{9,10},{10,9},{13,14},{14,13},{17,18},{18,... | collective-permute-start | bytes 3981320 | tf_op jit(solution)/shard_map/ppermute | solution.py:228
  962.1 39.1 %collective-permute-start.44 = (bf16[256,2048]{1,0:T(8,128)(2,1)S(1)}, bf16[256,2048]{1,0:T(8,128)(2,1)S(1)}, u32[]{:S(2)}, u32[]{:S(2)}) collective-permute-start(bf16[256,2048]{1,0:T(8,128)(2,1)S(1)} %add_convert_fusion.13), channel_id=1, source_target_pairs={{1,0},{2,3},{5,4},{6,7},{9,8},{10,11},{13,12},{14,15},{17,16},{18,... | collective-permute-start | bytes 3145736 | tf_op jit(solution)/shard_map/ppermute | solution.py:229
  993.8 43.7 %collective-permute-start.27 = (bf16[576,1152]{1,0:T(8,128)(2,1)S(1)}, bf16[576,1152]{1,0:T(8,128)(2,1)S(1)}, u32[]{:S(2)}, u32[]{:S(2)}) collective-permute-start(bf16[576,1152]{1,0:T(8,128)(2,1)S(1)} %add_convert_fusion.7), channel_id=1, source_target_pairs={{1,2},{2,1},{5,6},{6,5},{9,10},{10,9},{13,14},{14,13},{17,18},{18,... | collective-permute-start | bytes 3981320 | tf_op jit(solution)/shard_map/ppermute | solution.py:228
  998.8 45.3 %collective-permute-start.20 = (bf16[144,4608]{1,0:T(8,128)(2,1)}, bf16[144,4608]{1,0:T(8,128)(2,1)}, u32[]{:S(2)}, u32[]{:S(2)}) collective-permute-start(bf16[144,4608]{1,0:T(8,128)(2,1)} %add_convert_fusion.8), channel_id=1, source_target_pairs={{1,0},{2,3},{5,4},{6,7},{9,8},{10,11},{13,12},{14,15},{17,16},{18,... | collective-permute-start | bytes 3981320 | tf_op jit(solution)/shard_map/ppermute | solution.py:229
  1038.9 30.6 %collective-permute-start.28 = (bf16[576,1152]{1,0:T(8,128)(2,1)}, bf16[576,1152]{1,0:T(8,128)(2,1)}, u32[]{:S(2)}, u32[]{:S(2)}) collective-permute-start(bf16[576,1152]{1,0:T(8,128)(2,1)} %add_convert_fusion.6), channel_id=1, source_target_pairs={{1,0},{2,3},{5,4},{6,7},{9,8},{10,11},{13,12},{14,15},{17,16},{18,... | collective-permute-start | bytes 3981320 | tf_op jit(solution)/shard_map/ppermute | solution.py:229
  (121 other events, 2346.4 us)
Sparse Core Ops, SparseCore 0:
  14.5 47.9 all-gather.10
  64.5 33.8 all-gather.12
  100.2 63.7 all-gather.14
  165.8 63.8 all-gather.16
  231.4 38.9 all-gather.18
  272.1 54.3 all-gather.20
  328.4 32.3 all-gather.22
  644.0 111.1 reduce-scatter.1
  890.8 51.0 all-reduce.6
  945.0 71.8 all-gather.26
  1044.2 30.4 all-gather.24

commit v2 on v1

--- a/solution.py
+++ b/solution.py
@@ -133,9 +133,13 @@
         lax.fori_loop(0, units, pack, 0)
 
 
-def picker(heads, head_dim, dtype):
+def whole_lanes(width):
+    return -(-width // LANES) * LANES
+
+
+def picker(heads, head_dim, dtype, width=None):
     row = jnp.arange(heads * LANES)[:, None]
-    col = jnp.arange(heads * head_dim)[None, :]
+    col = jnp.arange(heads * head_dim if width is None else width)[None, :]
     return ((row // LANES == col // head_dim) & (row % LANES == col % head_dim)).astype(dtype)
 
 
@@ -172,62 +176,528 @@
                 whole(parts, units, unit, lanes),
                 pl.BlockSpec((parts, 1, unit, width), lambda u, *_: (0, u, 0, 0)),
                 whole(width, heads * LANES),
-                whole(3 * heads * LANES, 3 * width),
+                whole(3 * heads * LANES, whole_lanes(3 * width)),
             ],
-            out_specs=whole(parts, units, unit, 3 * width),
+            out_specs=whole(parts, units, unit, whole_lanes(3 * width)),
             scratch_shapes=[
                 pltpu.VMEM((parts, units, unit, heads * LANES), BF),
                 pltpu.VMEM((parts, units, unit, heads * LANES), F32),
                 pltpu.VMEM((parts, units, unit, heads * LANES), F32),
             ],
         ),
-        out_shape=jax.ShapeDtypeStruct((parts, units, unit, 3 * width), BF),
+        out_shape=jax.ShapeDtypeStruct((parts, units, unit, whole_lanes(3 * width)), BF),
         compiler_params=pltpu.CompilerParams(vmem_limit_bytes=56 * 2**20),
         cost_estimate=pl.CostEstimate(flops=40 * 2**30, bytes_accessed=16 * 2**20, transcendentals=2**23),
         name="attend_backward",
-    )(start, length, qkv, grad, pick.T, picker(3 * heads, head_dim, BF))
-
-
-def flips(n, bit):
-    return [(i, i ^ bit) for i in range(n)]
-
-
-def scatter_steps(left, right):
-    devices = lax.axis_size("img")
-    place = lax.axis_index("img")
-    count, depth = left.shape
-    columns = right.shape[1]
-    blocks = left.reshape(count, devices, depth // devices)
-
-    def of(*masks):
-        picked = [lax.dynamic_index_in_dim(blocks, place ^ m, axis=1, keepdims=False) for m in masks]
-        return jnp.concatenate(picked, axis=1)
-
-    rows = depth // devices
-    sent = left_product(of(1, 3, 5, 7), right)
-    got = lax.ppermute(sent, "img", flips(devices, 1))
-    own = jnp.einsum("ti,to->io", of(0, 2, 4, 6), right, preferred_element_type=F32) + got.astype(F32)
-    own = own.astype(BF).reshape(4, rows, columns)
-    half = columns // 2 // LANES * LANES
-    one, two = own[:, :, :half], own[:, :, half:]
-    got_x = lax.ppermute(jnp.stack([one[1], one[3]]), "img", flips(devices, 2)).astype(F32)
-    got_y = lax.ppermute(jnp.stack([two[2], two[3]]), "img", flips(devices, 4)).astype(F32)
-    next_y = (one[2].astype(F32) + got_x[1]).astype(BF)
-    next_x = (two[1].astype(F32) + got_y[1]).astype(BF)
-    got_y2 = lax.ppermute(next_y, "img", flips(devices, 4)).astype(F32)
-    got_x2 = lax.ppermute(next_x, "img", flips(devices, 2)).astype(F32)
-    first = one[0].astype(F32) + got_x[0] + got_y2
-    second = two[0].astype(F32) + got_y[0] + got_x2
-    return jnp.concatenate([first, second], axis=1).astype(BF)
-
-
-def line_sum(values):
-    place = lax.axis_index("blk")
-    inner = (place == 1) | (place == 2)
-    values = (values.astype(F32) + lax.ppermute(values, "blk", [(0, 1), (3, 2)]).astype(F32)).astype(BF)
-    total = (values.astype(F32) + lax.ppermute(values, "blk", [(1, 2), (2, 1)]).astype(F32)).astype(BF)
-    back = lax.ppermute(total, "blk", [(1, 0), (2, 3)])
-    return jnp.where(inner, total, back)
+    )(start, length, qkv, grad, pick.T, picker(3 * heads, head_dim, BF, whole_lanes(3 * width)))
+
+
+MESH = pl.DeviceIdType.MESH
+
+
+def add_into(ref, at, other):
+    ref[at] = (ref[at].astype(F32) + other.astype(F32)).astype(BF)
+
+
+def cut_rows(rows, k):
+    up = (rows // 2 + 15) // 16 * 16
+    return up if k % 2 == 0 else rows - up
+
+
+def reduce_kernel(chunks, tensors, *refs):
+    grads, outs, scratch = refs[:tensors], refs[tensors : 2 * tensors], list(refs[2 * tensors :])
+    own, local_sem, send_sem, recv_sem = scratch[:4]
+    bufs = scratch[4:]
+    per = 8
+    place, z = lax.axis_index("img"), lax.axis_index("blk")
+    y, x, c = lax.div(place, 4), lax.rem(lax.div(place, 2), 2), lax.rem(place, 2)
+    pair, beside, across = place + 1 - 2 * c, place + 2 - 4 * x, place + 4 - 8 * y
+    near, far = z + 1 - 2 * lax.rem(z, 2), 3 - z
+    inside = (z == 1) | (z == 2)
+    outside = (z == 0) | (z == 3)
+
+    barrier = pltpu.get_barrier_semaphore()
+    for other in (pair, beside, across):
+        pl.semaphore_signal(barrier, inc=1, device_id={"img": other}, device_id_type=MESH)
+    for step in (1, 2, 3):
+        pl.semaphore_signal(barrier, inc=1, device_id={"blk": lax.rem(z + step, 4)}, device_id_type=MESH)
+    pl.semaphore_wait(barrier, 6)
+
+    def send(k, which, source, target, where):
+        return pltpu.make_async_remote_copy(
+            src_ref=source,
+            dst_ref=target,
+            send_sem=send_sem.at[k, which],
+            recv_sem=recv_sem.at[k, which],
+            device_id=where,
+            device_id_type=MESH,
+        )
+
+    def parts_of(k):
+        t, row, rows, col, cols, gather = chunks[k]
+        return grads[t], outs[t], row, rows, col, cols, gather
+
+    def cut(k):
+        return cut_rows(chunks[k][2], k)
+
+    copies = {}
+
+    def begin(k, which, source, target, where):
+        copies[k, which] = send(k, which, source, target, where)
+        copies[k, which].start()
+
+    def load(k):
+        grad, _, row, rows, col, cols, _ = parts_of(k)
+        return pltpu.make_async_copy(
+            grad.at[:, :, c, pl.ds(row, rows), pl.ds(col, cols)],
+            own.at[k % 2, :, :, pl.ds(0, rows), pl.ds(0, cols)],
+            local_sem.at[k % 2],
+        )
+
+    count = len(chunks)
+    for k in range(count):
+        grad, _, row, rows, col, cols, _ = parts_of(k)
+        begin(k, 0, grad.at[:, :, 1 - c, pl.ds(row, rows), pl.ds(col, cols)], bufs[per * k], {"img": pair})
+    for k in range(min(2, count)):
+        load(k).start()
+
+    def stage_one(k):
+        _, _, _, rows, _, cols, _ = parts_of(k)
+        acc, rx, ry = bufs[per * k : per * k + 3]
+        load(k).wait()
+        copies[k, 0].wait_recv()
+        for i in range(2):
+            for j in range(2):
+                add_into(acc, (i, j), own[k % 2, i, j, :rows, :cols])
+        if k + 2 < count:
+            load(k + 2).start()
+        first = cut(k)
+        begin(k, 1, acc.at[:, 1 - x, pl.ds(0, first)], rx, {"img": beside})
+        begin(k, 2, acc.at[1 - y, :, pl.ds(first, rows - first)], ry, {"img": across})
+
+    def stage_two(k):
+        rows = chunks[k][2]
+        acc, rx, ry, rx2, ry2 = bufs[per * k : per * k + 5]
+        first = cut(k)
+        copies[k, 1].wait_recv()
+        copies[k, 2].wait_recv()
+        copies[k, 1].wait_send()
+        copies[k, 2].wait_send()
+        for i in range(2):
+            add_into(acc, (i, x, slice(0, first)), rx[i])
+            add_into(acc, (y, i, slice(first, rows)), ry[i])
+        begin(k, 3, acc.at[y, 1 - x, pl.ds(first, rows - first)], rx2, {"img": beside})
+        begin(k, 4, acc.at[1 - y, x, pl.ds(0, first)], ry2, {"img": across})
+
+    def stage_three(k):
+        _, out, row, rows, col, cols, gather = parts_of(k)
+        acc, _, _, rx2, ry2, from_near, from_far, total = bufs[per * k : per * (k + 1)]
+        first = cut(k)
+        copies[k, 3].wait_recv()
+        copies[k, 4].wait_recv()
+        low = (acc[y, x, 0:first].astype(F32) + ry2[...].astype(F32)).astype(BF)
+        high = (acc[y, x, first:rows].astype(F32) + rx2[...].astype(F32)).astype(BF)
+        if gather:
+            total[z, 0:first] = low
+            total[z, first:rows] = high
+            for step in (1, 2, 3):
+                begin(k, 4 + step, total.at[z], total.at[z], {"blk": lax.rem(z + step, 4)})
+            return
+        from_far[0, 0:first] = low
+        from_far[0, first:rows] = high
+        copies[k, 5] = send(k, 5, from_far.at[0], from_near, {"blk": near})
+        pl.when(outside)(copies[k, 5].start)
+
+    def stage_four(k):
+        if chunks[k][5]:
+            return
+        from_near, from_far, total = bufs[per * k + 5 : per * k + 8]
+        copies[k, 6] = send(k, 6, from_far.at[0], from_far.at[1], {"blk": far})
+
+        @pl.when(inside)
+        def _():
+            copies[k, 5].wait_recv()
+            add_into(from_far, 0, from_near[...])
+            copies[k, 6].start()
+
+    def stage_five(k):
+        if chunks[k][5]:
+            return
+        from_near, from_far, total = bufs[per * k + 5 : per * k + 8]
+        copies[k, 7] = send(k, 7, total, total, {"blk": near})
+
+        @pl.when(inside)
+        def _():
+            copies[k, 6].wait_recv()
+            total[...] = (from_far[0].astype(F32) + from_far[1].astype(F32)).astype(BF)
+            copies[k, 7].start()
+
+    def stage_six(k):
+        _, out, row, rows, col, cols, gather = parts_of(k)
+        total = bufs[per * k + 7]
+        if gather:
+            for step in (1, 2, 3):
+                copies[k, 4 + step].wait()
+            out[:, row : row + rows, col : col + cols] = total[...]
+            return
+        pl.when(outside)(copies[k, 7].wait_recv)
+        out[row : row + rows, col : col + cols] = total[...]
+
+    stages = ((stage_one, 0), (stage_two, 2), (stage_three, 4), (stage_four, 5), (stage_five, 6), (stage_six, 7))
+    for step in range(count + 7):
+        for stage, behind in stages:
+            if 0 <= step - behind < count:
+                stage(step - behind)
+    for k in range(count):
+        copies[k, 0].wait_send()
+        copies[k, 3].wait_send()
+        copies[k, 4].wait_send()
+        if not chunks[k][5]:
+            pl.when(outside)(copies[k, 5].wait_send)
+            pl.when(inside)(copies[k, 6].wait_send)
+            pl.when(inside)(copies[k, 7].wait_send)
+
+
+def reduce_call(grads, gathered, depth, width, collective_id):
+    chunks, shapes = [], []
+    for t, grad in enumerate(grads):
+        rows, cols = grad.shape[0] // 8, grad.shape[1]
+        for row in range(0, rows, depth):
+            for col in range(0, cols, width):
+                chunks.append((t, row, min(depth, rows - row), col, min(width, cols - col), gathered[t]))
+        shapes.append(jax.ShapeDtypeStruct((4, rows, cols) if gathered[t] else (rows, cols), BF))
+    scratch = [
+        pltpu.VMEM((2, 2, 2, depth, width), BF),
+        pltpu.SemaphoreType.DMA((2,)),
+        pltpu.SemaphoreType.DMA((len(chunks), 8)),
+        pltpu.SemaphoreType.DMA((len(chunks), 8)),
+    ]
+    for k, (_, _, rows, _, cols, gather) in enumerate(chunks):
+        first = cut_rows(rows, k)
+        for shape in (
+            (2, 2, rows, cols),
+            (2, first, cols),
+            (2, rows - first, cols),
+            (rows - first, cols),
+            (first, cols),
+            (16, cols) if gather else (rows, cols),
+            (1, 16, cols) if gather else (2, rows, cols),
+            (4, rows, cols) if gather else (rows, cols),
+        ):
+            scratch.append(pltpu.VMEM(shape, BF))
+    return pl.pallas_call(
+        partial(reduce_kernel, chunks, len(grads)),
+        out_shape=shapes,
+        in_specs=[pl.BlockSpec(memory_space=pl.ANY)] * len(grads),
+        out_specs=[pl.BlockSpec(memory_space=pltpu.VMEM)] * len(grads),
+        scratch_shapes=scratch,
+        compiler_params=pltpu.CompilerParams(
+            collective_id=collective_id, has_side_effects=True, vmem_limit_bytes=56 * 2**20
+        ),
+        cost_estimate=pl.CostEstimate(flops=0, bytes_accessed=500 * 2**20, transcendentals=0),
+        name=f"reduce_{collective_id}",
+    )(*(g.reshape(2, 2, 2, g.shape[0] // 8, g.shape[1]) for g in grads))
+
+
+def gather_kernel(chunks, tensors, early, hot_ref, x_ref, share_ref, bias_ref, start_ref, *refs):
+    shards, refs = refs[:tensors], refs[tensors:]
+    fulls, refs = refs[:tensors], refs[tensors:]
+    rows_ref, modulation_ref, bias_out = refs[:3]
+    share_got, own_sem, first_send, first_recv, rest_send, rest_recv, bias_send, bias_recv = refs[3:11]
+    send_sem, recv_sem, line_send, line_recv, spread_send, spread_recv = refs[11:]
+    place, z = lax.axis_index("img"), lax.axis_index("blk")
+    y, x, c = lax.div(place, 4), lax.rem(lax.div(place, 2), 2), lax.rem(place, 2)
+    step_x, step_y = 2 - 4 * x, 4 - 8 * y
+    pair, beside, across = place + 1 - 2 * c, place + step_x, place + step_y
+    diagonal = place + step_x + step_y
+    devices = share_got.shape[0]
+    units, slots = hot_ref.shape
+    unit = x_ref.shape[0] // units
+    wide = x_ref.shape[1]
+
+    barrier = pltpu.get_barrier_semaphore()
+    for step in range(1, devices):
+        pl.semaphore_signal(barrier, inc=1, device_id={"img": lax.rem(place + step, devices)}, device_id_type=MESH)
+    for step in (1, 2, 3):
+        pl.semaphore_signal(barrier, inc=1, device_id={"blk": lax.rem(z + step, 4)}, device_id_type=MESH)
+    pl.semaphore_wait(barrier, devices + 2)
+
+    def remote(source, target, send, recv, where):
+        return pltpu.make_async_remote_copy(
+            src_ref=source,
+            dst_ref=target,
+            send_sem=send,
+            recv_sem=recv,
+            device_id=where,
+            device_id_type=MESH,
+        )
+
+    part = (share_ref.shape[2] - early) // 4
+    part_at = pl.multiple_of(early + z * part, LANES)
+    first, rest, biases = [], [], []
+    for step in range(1, devices):
+        to = lax.rem(place + step, devices)
+        for copies, lo, size, send, recv in (
+            (first, 0, early, first_send, first_recv),
+            (rest, part_at, part, rest_send, rest_recv),
+        ):
+            copies.append(
+                remote(
+                    share_ref.at[to, :, pl.ds(lo, size)],
+                    share_got.at[place, :, pl.ds(lo, size)],
+                    send.at[step],
+                    recv.at[step],
+                    {"img": to},
+                )
+            )
+        biases.append(remote(bias_ref, bias_out.at[place], bias_send.at[step], bias_recv.at[step], {"img": to}))
+    for copy in first:
+        copy.start()
+
+    copies = {}
+
+    def begin(k, which, block, rows, where):
+        t, row, count = chunks[k]
+        at = (block, pl.ds(row + rows[0], rows[1]))
+        copies[k, which] = remote(
+            fulls[t].at[at], fulls[t].at[at], send_sem.at[k, which], recv_sem.at[k, which], where
+        )
+        copies[k, which].start()
+
+    def begin_own(k, which, where):
+        t, row, count = chunks[k]
+        source = shards[t].at[pl.ds(row, count)]
+        copies[k, which] = remote(
+            source, fulls[t].at[place, pl.ds(row, count)], send_sem.at[k, which], recv_sem.at[k, which], where
+        )
+        copies[k, which].start()
+
+    own = [pltpu.make_async_copy(shards[t], fulls[t].at[place], own_sem.at[t]) for t in range(tensors)]
+    def ahead(k):
+        if k < len(chunks):
+            begin_own(k, 0, {"img": beside})
+            begin_own(k, 1, {"img": across})
+            begin_own(k, 2, {"img": pair})
+
+    ahead(0)
+    for copy in rest + biases:
+        copy.start()
+    for k in range(1, 3):
+        ahead(k)
+    for copy in own:
+        copy.start()
+
+    share_got[place] = share_ref[place]
+    bias_out[place] = bias_ref[...]
+    for copy in first:
+        copy.wait()
+
+    def modulation_of(lo, size):
+        at = pl.ds(lo, size)
+        total = share_got[0, :, at]
+        for i in range(1, devices):
+            total = total + share_got[i, :, at]
+        modulation_ref[:, at] = start_ref[:, at] + total
+
+    modulation_of(0, early)
+    for u in range(units):
+        chosen = hot_ref[u : u + 1, 0:1] * modulation_ref[0:1, 0:early]
+        for s in range(1, slots):
+            chosen = chosen + hot_ref[u : u + 1, s : s + 1] * modulation_ref[s : s + 1, 0:early]
+        at = pl.ds(u * unit, unit)
+        values = x_ref[at, :].astype(F32)
+        centered = values - jnp.mean(values, axis=1, keepdims=True)
+        inverse = lax.rsqrt(jnp.mean(centered * centered, axis=1, keepdims=True) + EPSILON)
+        rows_ref[z, at, :] = (centered * inverse * (1.0 + chosen[:, wide:]) + chosen[:, :wide]).astype(BF)
+
+    up = [
+        remote(block, block, line_send.at[0, s], line_recv.at[0, s], {"blk": lax.rem(z + 1, 4)})
+        for s, block in ((s, rows_ref.at[lax.rem(z - s + 4, 4)]) for s in range(3))
+    ]
+    down = [
+        remote(block, block, line_send.at[1, s], line_recv.at[1, s], {"blk": lax.rem(z + 3, 4)})
+        for s, block in ((s, rows_ref.at[lax.rem(z + s, 4)]) for s in range(3))
+    ]
+
+    def line_step(s):
+        if s > 0:
+            pl.when(z >= s)(up[s - 1].wait_recv)
+            pl.when(z + s < 4)(down[s - 1].wait_recv)
+        if s < 3:
+            pl.when((z >= s) & (z < 3))(up[s].start)
+            pl.when((z + s < 4) & (z > 0))(down[s].start)
+
+    def cut(k):
+        return cut_rows(chunks[k][2], k)
+
+    def relay(k):
+        count, half = chunks[k][2], cut(k)
+        copies[k, 0].wait_recv()
+        begin(k, 3, beside, (0, half), {"img": across})
+        begin(k, 5, beside, (0, count), {"img": pair})
+        copies[k, 1].wait_recv()
+        begin(k, 4, across, (half, count - half), {"img": beside})
+        begin(k, 6, across, (0, count), {"img": pair})
+
+    def last(k):
+        count, half = chunks[k][2], cut(k)
+        copies[k, 3].wait_recv()
+        begin(k, 7, diagonal, (0, half), {"img": pair})
+        copies[k, 4].wait_recv()
+        begin(k, 8, diagonal, (half, count - half), {"img": pair})
+
+    line_step(0)
+    for copy in rest:
+        copy.wait()
+    modulation_of(part_at, part)
+    own_part = modulation_ref.at[:, pl.ds(part_at, part)]
+    spread = [
+        remote(own_part, own_part, spread_send.at[step], spread_recv.at[step], {"blk": lax.rem(z + step, 4)})
+        for step in (1, 2, 3)
+    ]
+    for copy in spread:
+        copy.start()
+    n = len(chunks)
+    for k in range(n + 2):
+        if k < n:
+            relay(k)
+            ahead(k + 3)
+        if k >= 2:
+            last(k - 2)
+        for s in (1, 2):
+            if k == 2 * s - 1:
+                line_step(s)
+    for copy in biases:
+        copy.wait()
+    line_step(3)
+    for copy in spread:
+        copy.wait()
+    for copy in own:
+        copy.wait()
+    for k in range(n):
+        for which in (0, 1, 3, 4):
+            copies[k, which].wait_send()
+        copies[k, 2].wait()
+        for which in (5, 6, 7, 8):
+            copies[k, which].wait()
+    for s in range(3):
+        pl.when((z >= s) & (z < 3))(up[s].wait_send)
+        pl.when((z + s < 4) & (z > 0))(down[s].wait_send)
+
+
+def gather_call(shards, unit_hot, rows, shares, bias_row, modulate_bias, collective_id):
+    devices = shares.shape[0]
+    slots, wide = shares.shape[1:]
+    chunks = []
+    for t, shard in enumerate(shards):
+        depth = shard.shape[0]
+        for row in range(0, depth, 144):
+            chunks.append((t, row, min(144, depth - row)))
+    n = len(chunks)
+    vmem, anywhere = pl.BlockSpec(memory_space=pltpu.VMEM), pl.BlockSpec(memory_space=pl.ANY)
+    dma = pltpu.SemaphoreType.DMA
+    first_modulation = jnp.broadcast_to(modulate_bias.astype(F32)[None, :], (slots, wide))
+    return pl.pallas_call(
+        partial(gather_kernel, chunks, len(shards), 2 * rows.shape[1]),
+        out_shape=[jax.ShapeDtypeStruct((devices, *s.shape), BF) for s in shards]
+        + [
+            jax.ShapeDtypeStruct((4, *rows.shape), BF),
+            jax.ShapeDtypeStruct((slots, wide), F32),
+            jax.ShapeDtypeStruct((devices, *bias_row.shape), F32),
+        ],
+        in_specs=[vmem] * 5 + [anywhere] * len(shards),
+        out_specs=[anywhere] * len(shards) + [vmem] * 3,
+        scratch_shapes=[
+            pltpu.VMEM((devices, slots, wide), F32),
+            dma((len(shards),)),
+            dma((devices,)),
+            dma((devices,)),
+            dma((devices,)),
+            dma((devices,)),
+            dma((devices,)),
+            dma((devices,)),
+            dma((n, 9)),
+            dma((n, 9)),
+            dma((2, 3)),
+            dma((2, 3)),
+            dma((4,)),
+            dma((4,)),
+        ],
+        compiler_params=pltpu.CompilerParams(
+            collective_id=collective_id, has_side_effects=True, vmem_limit_bytes=48 * 2**20
+        ),
+        cost_estimate=pl.CostEstimate(flops=0, bytes_accessed=450 * 2**20, transcendentals=0),
+        name=f"gather_{collective_id}",
+    )(unit_hot, rows, shares, bias_row, first_modulation, *shards)
+
+
+def total_kernel(mine_ref, out_ref, lines, line_send, line_recv, send_sem, recv_sem):
+    place, z = lax.axis_index("img"), lax.axis_index("blk")
+    parts, devices = lines.shape[0], out_ref.shape[0]
+    barrier = pltpu.get_barrier_semaphore()
+    for step in range(1, parts):
+        pl.semaphore_signal(barrier, inc=1, device_id={"blk": lax.rem(z + step, parts)}, device_id_type=MESH)
+    for step in range(1, devices):
+        pl.semaphore_signal(barrier, inc=1, device_id={"img": lax.rem(place + step, devices)}, device_id_type=MESH)
+    pl.semaphore_wait(barrier, parts + devices - 2)
+
+    lines[z] = mine_ref[...]
+    copies = [
+        pltpu.make_async_remote_copy(
+            src_ref=lines.at[z],
+            dst_ref=lines.at[z],
+            send_sem=line_send.at[step],
+            recv_sem=line_recv.at[step],
+            device_id={"blk": lax.rem(z + step, parts)},
+            device_id_type=MESH,
+        )
+        for step in range(1, parts)
+    ]
+    for copy in copies:
+        copy.start()
+    for copy in copies:
+        copy.wait()
+    total = lines[0]
+    for step in range(1, parts):
+        total = total + lines[step]
+    out_ref[place] = total
+    copies = [
+        pltpu.make_async_remote_copy(
+            src_ref=out_ref.at[place],
+            dst_ref=out_ref.at[place],
+            send_sem=send_sem.at[step],
+            recv_sem=recv_sem.at[step],
+            device_id={"img": lax.rem(place + step, devices)},
+            device_id_type=MESH,
+        )
+        for step in range(1, devices)
+    ]
+    for copy in copies:
+        copy.start()
+    for copy in copies:
+        copy.wait()
+
+
+def total_call(mine, devices, parts, collective_id):
+    if (devices, parts) != (8, 4):
+        return lax.all_gather(lax.psum(mine, "blk"), "img", axis=0, tiled=False)
+    return pl.pallas_call(
+        total_kernel,
+        out_shape=jax.ShapeDtypeStruct((devices, *mine.shape), mine.dtype),
+        in_specs=[pl.BlockSpec(memory_space=pltpu.VMEM)],
+        out_specs=pl.BlockSpec(memory_space=pltpu.VMEM),
+        scratch_shapes=[
+            pltpu.VMEM((parts, *mine.shape), mine.dtype),
+            pltpu.SemaphoreType.DMA((parts,)),
+            pltpu.SemaphoreType.DMA((parts,)),
+            pltpu.SemaphoreType.DMA((devices,)),
+            pltpu.SemaphoreType.DMA((devices,)),
+        ],
+        compiler_params=pltpu.CompilerParams(
+            collective_id=collective_id, has_side_effects=True, vmem_limit_bytes=32 * 2**20
+        ),
+        name=f"total_{collective_id}",
+    )(mine)
 
 
 def per_device(
@@ -276,15 +746,55 @@
     shares = dot(silu_condition, modulate_weight)
     biases = (attend_bias, output_bias, expand_bias, shrink_bias, inner_bias, middle_bias, outer_bias)
     bias_row = jnp.concatenate(biases).astype(F32)
-    wide = shares.shape[1]
-    tail = jnp.broadcast_to(jnp.pad(bias_row, (0, wide - bias_row.shape[0])), (devices, 1, wide))
-    sent = jnp.concatenate([shares.reshape(devices, slots, wide), tail], axis=1)
-    got = lax.all_to_all(sent, "img", split_axis=0, concat_axis=0, tiled=True)
-    modulation = jnp.sum(got[:, :slots], axis=0) + modulate_bias.astype(F32)[None, :]
+    bias_row = jnp.pad(bias_row, (0, whole_lanes(bias_row.shape[0]) - bias_row.shape[0]))[None, :]
+    shares = shares.reshape(devices, slots, -1)
+
+    labels = token_image[::unit]
+    same = labels[:, None] == labels[None, :]
+    start = jnp.argmax(same, axis=1).astype(jnp.int32)
+    length = jnp.sum(same, axis=1).astype(jnp.int32)
+    unit_hot = (labels[:, None] == jnp.arange(slots)[None, :]).astype(F32)
+    def by_unit(values):
+        return values.reshape(units, unit, width)
+
+    def by_row(values):
+        return values.reshape(count, width)
+
+    attend_mine = lax.dynamic_slice_in_dim(
+        attend_weight.reshape(-1, 3, parts, mine), place_blk, 1, axis=2
+    ).reshape(-1, 3 * mine)
+    attend_mine = jnp.pad(attend_mine, ((0, 0), (0, whole_lanes(3 * mine) - 3 * mine)))
+
+    def gather(shard):
+        return lax.all_gather(shard, "img", axis=0, tiled=True)
+
+    source = by_unit(inputs.astype(F32))
+    normal_one, inverse_one = layer_norm(source)
+    first_weights = (attend_mine, output_weight, expand_weight, outer_weight, shrink_weight)
+    if (devices, parts) == (8, 4):
+        *fulls, rows_group, modulation, got_bias = gather_call(
+            first_weights, unit_hot, inputs, shares, bias_row, modulate_bias, 3
+        )
+        fulls = [full.reshape(-1, full.shape[2]) for full in fulls]
+        modulated_group = rows_group.reshape(parts * count, width)
+    else:
+        fulls = [gather(shard) for shard in first_weights]
+        modulation = modulate_bias.astype(F32)[None, :] + lax.psum_scatter(
+            shares.reshape(devices * slots, -1), "img", scatter_dimension=0, tiled=True
+        )
+        got_bias = lax.all_gather(bias_row, "img", axis=0, tiled=False)
+        chosen = jnp.dot(unit_hot, modulation, precision=HIGH)[:, None, : 2 * width]
+        modulated_one = normal_one * (1.0 + chosen[:, :, width:]) + chosen[:, :, :width]
+        modulated_group = lax.all_gather(by_row(modulated_one.astype(BF)), "blk", axis=0, tiled=True)
+    attend_full, output_full, expand_full, outer_full, shrink_full = fulls
+    inner_shard, middle_shard, modulated_group = lax.optimization_barrier(
+        (inner_weight, middle_weight, modulated_group)
+    )
+    inner_full, middle_full = gather(inner_shard), gather(middle_shard)
     full_biases = []
     at = 0
     for bias in biases:
-        full_biases.append(got[:, slots, at : at + bias.shape[0]].reshape(-1))
+        full_biases.append(got_bias[:, 0, at : at + bias.shape[0]].reshape(-1))
         at += bias.shape[0]
     (
         attend_bias_full,
@@ -295,40 +805,10 @@
         middle_bias_full,
         outer_bias_full,
     ) = full_biases
-
-    labels = token_image[::unit]
-    same = labels[:, None] == labels[None, :]
-    start = jnp.argmax(same, axis=1).astype(jnp.int32)
-    length = jnp.sum(same, axis=1).astype(jnp.int32)
-    unit_hot = (labels[:, None] == jnp.arange(slots)[None, :]).astype(F32)
     unit_modulation = jnp.dot(unit_hot, modulation, precision=HIGH)
     shift_one, scale_one, gate_one, shift_two, scale_two, gate_two = (
         block[:, None, :] for block in jnp.split(unit_modulation, 6, axis=1)
     )
-
-    def by_unit(values):
-        return values.reshape(units, unit, width)
-
-    def by_row(values):
-        return values.reshape(count, width)
-
-    attend_mine = lax.dynamic_slice_in_dim(
-        attend_weight.reshape(-1, 3, parts, mine), place_blk, 1, axis=2
-    ).reshape(-1, 3 * mine)
-    attend_full = lax.all_gather(attend_mine, "img", axis=0, tiled=True)
-    output_full = lax.all_gather(output_weight, "img", axis=0, tiled=True)
-    expand_full = lax.all_gather(expand_weight, "img", axis=0, tiled=True)
-    shrink_full = lax.all_gather(shrink_weight, "img", axis=0, tiled=True)
-    inner_full = lax.all_gather(inner_weight, "img", axis=0, tiled=True)
-    middle_full = lax.all_gather(middle_weight, "img", axis=0, tiled=True)
-    outer_full = lax.all_gather(outer_weight, "img", axis=0, tiled=True)
-
-    source = by_unit(inputs.astype(F32))
-    normal_one, inverse_one = layer_norm(source)
-    modulated_one = by_row((normal_one * (1.0 + scale_one) + shift_one).astype(BF))
-    modulated_group = lax.all_to_all(
-        jnp.broadcast_to(modulated_one, (parts, count, width)), "blk", split_axis=0, concat_axis=0, tiled=True
-    ).reshape(parts * count, width)
 
     def pad_heads(values):
         lead = values.shape[:-1]
@@ -338,7 +818,7 @@
 
     bias_mine = lax.dynamic_slice_in_dim(attend_bias_full.reshape(2, parts, mine), place_blk, 1, axis=1)
     bias_mine = jnp.concatenate([bias_mine[0, 0], jnp.zeros((mine,), F32), bias_mine[1, 0]])
-    projected = dot(modulated_group, pad_heads(attend_full)) + pad_heads(bias_mine)[None, :]
+    projected = dot(modulated_group, pad_heads(attend_full[:, : 3 * mine])) + pad_heads(bias_mine)[None, :]
     qkv = projected.astype(BF).reshape(parts, units, unit, 3 * heads * LANES)
     attended_heads = attend_forward(start, length, qkv, heads, head_dim)
     attended = lax.all_to_all(
@@ -375,60 +855,72 @@
         )
     ).astype(BF)
 
-    def scatter(left, right):
-        if devices == 8:
-            return scatter_steps(left, right)
-        return lax.psum_scatter(left_product(left, right), "img", scatter_dimension=0, tiled=True)
-
-    def total(part):
-        return line_sum(part) if parts == 4 else lax.psum(part, "blk")
-
-    outer_sum = total(scatter(second, grad_aligned))
+    def scatter(values):
+        return lax.psum_scatter(values, "img", scatter_dimension=0, tiled=True)
+
+    outer_part = scatter(left_product(second, grad_aligned))
     grad_outer_bias = column_sum(grad_aligned)
     grad_pre_two = local_back(jax.nn.silu, pre_two, right_product(grad_aligned, outer_full)).astype(BF)
-    middle_sum = total(scatter(first, grad_pre_two))
+    middle_part = scatter(left_product(first, grad_pre_two))
     grad_middle_bias = column_sum(grad_pre_two)
     grad_pre_one = local_back(jax.nn.silu, pre_one, right_product(grad_pre_two, middle_full)).astype(BF)
-    inner_sum = total(scatter(whole_low, grad_pre_one))
+    grad_inner = left_product(whole_low, grad_pre_one)
     grad_inner_bias = column_sum(grad_pre_one)
     grad_whole = by_unit(cotangent.astype(F32)) + by_unit(right_product(grad_pre_one, inner_full))
     grad_gate_two = grad_whole * branch_two
     grad_branch_two = by_row((grad_whole * gate_two).astype(BF))
-    shrink_sum = total(scatter(activated, grad_branch_two))
+    grad_shrink = left_product(activated, grad_branch_two)
     grad_shrink_bias = column_sum(grad_branch_two)
     grad_expanded = local_back(gelu_tanh, expanded, right_product(grad_branch_two, shrink_full)).astype(BF)
-    expand_sum = total(scatter(modulated_two, grad_expanded))
+    grad_expand = left_product(modulated_two, grad_expanded)
     grad_expand_bias = column_sum(grad_expanded)
     grad_mod_two = by_unit(right_product(grad_expanded, expand_full))
     grad_scale_two = grad_mod_two * normal_two
     grad_middle = grad_whole + norm_back(grad_mod_two * (1.0 + scale_two), normal_two, inverse_two)
     grad_gate_one = grad_middle * branch_one
     grad_branch_one = by_row((grad_middle * gate_one).astype(BF))
-    attended_rows = jnp.transpose(attended, (1, 0, 2)).reshape(count, width)
-    output_sum = total(scatter(attended_rows, grad_branch_one))
+    grad_output = jnp.einsum("pti,to->pio", attended, grad_branch_one, preferred_element_type=F32)
+    grad_output = grad_output.astype(BF).reshape(width, width)
     grad_output_bias = column_sum(grad_branch_one)
+    def slot_sum(*values):
+        rows = jnp.concatenate([jnp.sum(v, axis=1) for v in values], axis=1)
+        return jnp.dot(unit_hot.T, rows, precision=HIGH)
+
+    early_slots = lax.psum(slot_sum(grad_gate_one, grad_mod_two, grad_scale_two, grad_gate_two), "blk")
     grad_attended = jnp.einsum("to,pio->pti", grad_branch_one, output_heads, preferred_element_type=F32)
     grad_heads = lax.all_to_all(grad_attended.astype(BF), "blk", split_axis=0, concat_axis=0, tiled=True)
+    grad_heads, outer_part, early_slots = lax.optimization_barrier((grad_heads, outer_part, early_slots))
+    early_grad = lax.all_gather(early_slots, "img", axis=0, tiled=True)
     grad_qkv = attend_backward(
         start, length, qkv, grad_heads.reshape(parts, units, unit, mine), heads, head_dim
-    ).reshape(parts * count, 3 * mine)
-    attend_part = scatter(modulated_group, grad_qkv)
-    attend_parts = lax.all_gather(attend_part, "blk", axis=0, tiled=False)
-    attend_sum = jnp.transpose(attend_parts.reshape(parts, -1, 3, mine), (1, 2, 0, 3)).reshape(
-        attend_part.shape[0], 3 * width
-    )
+    ).reshape(parts * count, -1)
+    grad_qkv, middle_part, early_grad = lax.optimization_barrier((grad_qkv, middle_part, early_grad))
+    outer_sum, middle_sum = lax.psum((outer_part, middle_part), "blk")
+    grad_attend = left_product(modulated_group, grad_qkv)
     partial_mod_one = right_product(grad_qkv, attend_full).astype(BF)
+    late_grads = (grad_inner, grad_shrink, grad_attend, grad_output, grad_expand)
+    if (devices, parts) == (8, 4):
+        inner_sum, shrink_sum, attend_parts, output_sum, expand_sum = reduce_call(
+            late_grads, (False, False, True, False, False), width // devices, 640, 1
+        )
+    else:
+        inner_sum, shrink_sum, attend_part, output_sum, expand_sum = (scatter(g) for g in late_grads)
+        sums = lax.psum((inner_sum, shrink_sum, output_sum, expand_sum), "blk")
+        inner_sum, shrink_sum, output_sum, expand_sum = sums
+        attend_parts = lax.all_gather(attend_part, "blk", axis=0, tiled=False)
+    attend_parts = attend_parts[:, :, : 3 * mine].reshape(parts, -1, 3, mine)
+    attend_sum = jnp.transpose(attend_parts, (1, 2, 0, 3)).reshape(-1, 3 * width)
     grad_mod_one = by_unit(
         lax.psum_scatter(partial_mod_one, "blk", scatter_dimension=0, tiled=True).astype(F32)
     )
     grad_scale_one = grad_mod_one * normal_one
     grad_source = grad_middle + norm_back(grad_mod_one * (1.0 + scale_one), normal_one, inverse_one)
 
-    def slot_sum(*values):
-        rows = jnp.concatenate([jnp.sum(v, axis=1) for v in values], axis=1)
-        return jnp.dot(unit_hot.T, rows, precision=HIGH)
-
-    early_biases = (
+    qkv_bias = column_sum(grad_qkv[:, : 3 * mine]).reshape(3, 1, mine)
+    spread = (jnp.arange(parts) == place_blk).astype(F32)[None, :, None]
+    attend_bias_rows = jnp.concatenate([qkv_bias[:1], qkv_bias[2:]]) * spread
+    bias_grads = (
+        attend_bias_rows,
         grad_output_bias,
         grad_expand_bias,
         grad_shrink_bias,
@@ -436,35 +928,28 @@
         grad_middle_bias,
         grad_outer_bias,
     )
-    early_sizes = [b.shape[0] // devices for b in early_biases]
-    early_bias_rows = jnp.concatenate([b.reshape(devices, -1) for b in early_biases], axis=1)
-    early_bias = lax.psum_scatter(early_bias_rows, "img", scatter_dimension=0, tiled=True)
-    early_slots = slot_sum(grad_gate_one, grad_mod_two, grad_scale_two, grad_gate_two)
-    early_slots, early_bias = lax.psum((early_slots, early_bias), "blk")
-    early_grad = lax.all_gather(early_slots, "img", axis=0, tiled=True)
-    early_bias = early_bias.reshape(-1)
+    bias_rows = jnp.concatenate([b.reshape(devices, -1) for b in bias_grads], axis=1)
+    late_slots = slot_sum(grad_mod_one, grad_scale_one)
+    late_rows = jnp.concatenate(
+        [late_slots, jnp.pad(bias_rows, ((0, 0), (0, late_slots.shape[1] - bias_rows.shape[1])))], axis=0
+    )
+    late = total_call(late_rows, devices, parts, 2)
+    late_grad = late[:, :slots].reshape(devices * slots, 2 * width)
+    bias_sum = jnp.sum(lax.dynamic_index_in_dim(late, slots + place_img, axis=1, keepdims=False), axis=0)
+    bias_sums = []
+    at = 0
+    for bias in biases:
+        bias_sums.append(bias_sum[at : at + bias.shape[0]])
+        at += bias.shape[0]
     (
+        attend_bias_sum,
         output_bias_sum,
         expand_bias_sum,
         shrink_bias_sum,
         inner_bias_sum,
         middle_bias_sum,
         outer_bias_sum,
-    ) = (early_bias[sum(early_sizes[:i]) : sum(early_sizes[: i + 1])] for i in range(len(early_sizes)))
-
-    qkv_bias = column_sum(grad_qkv).reshape(3, mine)
-    late_slots = slot_sum(grad_mod_one, grad_scale_one)
-    late_rows = jnp.concatenate(
-        [late_slots, jnp.pad(qkv_bias, ((0, slots - 3), (0, 2 * width - mine)))], axis=0
-    )
-    late = lax.all_gather(late_rows, ("img", "blk"), axis=0, tiled=False)
-    late = late.reshape(devices, parts, 2 * slots, 2 * width)
-    late_grad = jnp.sum(late[:, :, :slots], axis=1).reshape(devices * slots, 2 * width)
-    bias_all = jnp.sum(late[:, :, slots : slots + 3, :mine], axis=0)
-    attend_bias_whole = jnp.concatenate([bias_all[:, 0].reshape(-1), bias_all[:, 2].reshape(-1)])
-    attend_bias_sum = lax.dynamic_slice_in_dim(
-        attend_bias_whole, place_img * attend_bias.shape[0], attend_bias.shape[0]
-    )
+    ) = bias_sums
     modulation_grad = jnp.concatenate([late_grad, early_grad], axis=1)
     modulate_sum = jnp.dot(silu_condition.astype(F32).T, modulation_grad, precision=HIGH)
     modulate_bias_sum = jnp.sum(modulation_grad, axis=0)

time: 1110 us -> 925 us (0.83); the launches traced: 1090 us -> 921 us
  Pallas kernels: 64.9 us -> 476 us
  waiting for transfers between devices: 338 us -> 127 us
  local copies, waits for them, and re-layouts: 191 us -> 53 us
  starting transfers between devices: 134 us -> 14.1 us
  blocking collectives: 54.9 us -> 0 us
  other arithmetic: 91.4 us -> 41.1 us
    pallas_call x0 -> x3, Pallas kernels: none -> 392 us  [the longest x1 216 us: reduce_call(): pl.pallas_call(partial(reduce_kernel, chunks, len(grads)), out_shape=shap...]
    ppermute x53 -> x0, waiting for transfers between devices: 209 us -> none  [the longest x6 69.3 us: line_sum(): lax.ppermute(values, 'blk', [(0, 1), (3, 2)]).astype(F32)]
    all_to_all x2 -> x0, waiting for transfers between devices: 125 us -> none  [the longest x1 82.7 us: per_device(): lax.all_to_all(jnp.broadcast_to(modulated_one, (parts, count, width)), 'b...]
    ppermute x53 -> x0, starting transfers between devices: 104 us -> none  [the longest x6 27.7 us: line_sum(): lax.ppermute(values, 'blk', [(1, 2), (2, 1)]).astype(F32)]
    reduce_scatter x0 -> x2, waiting for transfers between devices: none -> 74.3 us  [scatter(): return lax.psum_scatter(values, 'img', scatter_dimension=0, tiled=True)]
    mul x9 -> x4, local copies, waits for them, and re-layouts: 36.6 us -> 0.61 us  [per_device(): attend_bias_rows = jnp.concatenate([qkv_bias[:1], qkv_bias[2:]]) * spread]
    convert_element_type x40 -> x3, other arithmetic: 36.4 us -> 2.74 us  [the longest x1 2.67 us: per_device(): attend_sum.astype(F32)]
    unnamed x1 -> x0, blocking collectives: 29.5 us -> none
  transfers between devices with their start and end apart: 68 -> 10, of which waited for: 23 -> 4; matrix products, arithmetic and copies ran while one was open for 35% -> 20% of each run, Pallas kernels for 6% -> 33%
where the time goes in v2:
time: 925 us; the launch traced here: 921 us
  Pallas kernels  476 us (51%)
  matrix products  195 us (21%)
  waiting for transfers between devices  127 us (14%)
  local copies, waits for them, and re-layouts  53 us (6%)
  other arithmetic  41.1 us (4%)
  between operations  15.2 us (2%)
  starting transfers between devices  14.1 us (2%)
    pallas_call x1, Pallas kernels, reduce_call(): pl.pallas_call(partial(reduce_kernel, chunks, len(grads)), out_shape=shap...  216 us
    pallas_call x1, Pallas kernels, gather_call(): pl.pallas_call(partial(gather_kernel, chunks, len(shards), 2 * rows.shape...  141 us
    reduce_scatter x2, waiting for transfers between devices, scatter(): return lax.psum_scatter(values, 'img', scatter_dimension=0, tiled=True)  74.3 us
    dot_general x8, matrix products, dot(): return jnp.dot(left, right, preferred_element_type=F32)  59.4 us
    dot_general x6, matrix products, right_product(): return jnp.einsum('to,io->ti', grad, weight, preferred_element_type=F32)  58.6 us
    pallas_call x1, Pallas kernels, attend_backward(): pl.pallas_call(partial(attend_backward_kernel, heads, 1.0 / math.sqrt(hea...  57.1 us
    dot_general x6, matrix products, left_product(): jnp.einsum('ti,to->io', left, right, preferred_element_type=F32).astype(BF)  52.3 us
    pallas_call x1, Pallas kernels, total_call(): pl.pallas_call(total_kernel, out_shape=jax.ShapeDtypeStruct((devices, *mi...  34.8 us
  transfers between devices with their start and end apart: 10, of which 4 were waited for; matrix products, arithmetic and copies ran while one was open for 20% of the time, Pallas kernels for 33%

profile of v2, /device:TPU:9, one launch (start us, length us, event | category | flops | bytes accessed | tf_op | source)
XLA Modules:
  0.0 920.8 jit_solution(7885121326218757259)
XLA Ops:
  7.3 0.9 slice.75
  9.0 4.8 concatenate.29
  13.8 2.8 reshape.496
  16.5 3.6 dynamic-slice_reduce_fusion
  21.5 1.6 convolution_bitcast_fusion.share_ref
  24.3 141.0 %gather_3.1 = (bf16[8,144,896]{2,1,0:T(8,128)(2,1)}, bf16[8,144,1152]{2,1,0:T(8,128)(2,1)}, bf16[8,144,4608]{2,1,0:T(8,128)(2,1)}, bf16[8,256,768]{2,1,0:T(8,128...) custom-call(f32[8,8]{1,0:T(8,128)S(1)} %fusion.76.hot_ref, ...), custom_call_target="tpu_custom_call" | custom-call | bytes 471859200 | tf_op jit(solution)/shard_map/gather_3/pallas_call | solution.py:600
  166.1 4.1 copy.57
  170.1 3.8 pad.23
  175.5 13.3 %add_convert_fusion = bf16[2048,1536]{1,0:T(8,128)(2,1)} fusion(bf16[2048,1152]{1,0:T(8,128)(2,1)} %bitcast.173, bf16[1152,1536]{0,1:T(8,128)(2,1)} %bitcast.154, f32[1536]{0:T(1024)S(1)} %pad_bitcast_fusion), kind=kOutput, calls=%fused_computation.4 | convolution fusion | flops 7254048768 | bytes 14555136 | tf_op jit(solution)/shard_map/dot_general | solution.py:53
  188.9 27.5 %attend_forward.1 = bf16[4,8,64,288]{3,2,1,0:T(8,128)(2,1)S(1)} custom-call(s32[8]{0:T(128)S(1)} %get-tuple-element.43.start_ref, s32[8]{0:T(128)S(1)} %fusion.65.length_ref, bf16[4,8,64,1536]{3,2,1,0:T(8,128)(2,1)} %bitcast.177, bf16[512,288]{1,0:T(8,128)(2,1)S(1)} %and_convert_fusion.1.pick_ref), custom_call_target="tpu_custom_call" | custom-call | flops 10737418240 | bytes 16777216 | tf_op jit(solution)/shard_map/attend_forward/pallas_call | solution.py:150
  216.4 1.1 copy-done.2
  217.6 2.5 copy.52
  220.0 5.6 all-to-all-start
  227.1 24.0 %all-to-all-done = bf16[4,512,288]{1,2,0:T(8,128)(2,1)} async-done(((bf16[4,512,288]{1,2,0:T(8,128)(2,1)}), bf16[4,512,288]{1,2,0:T(8,128)(2,1)}, u32[]{:S(2)}, u32[]{:S(2)}) %all-to-all-start) | async-done | bytes 1179680 | tf_op jit(solution)/shard_map/all_to_all | solution.py:824
  251.1 5.7 convert_reduce_fusion.6
  256.9 3.3 multiply_reduce_fusion.4
  260.4 2.4 fusion.17
  262.8 13.7 %fusion.107 = f32[512,4608]{1,0:T(8,128)} fusion(bf16[512,1152]{1,0:T(8,128)(2,1)S(1)} %fusion.17, bf16[1152,4608]{1,0:T(8,128)(2,1)} %bitcast.171), kind=kOutput, calls=%fused_computation.222 | convolution fusion | flops 5435817984 | bytes 21233664 | tf_op jit(solution)/shard_map/dot_general | solution.py:53
  276.5 11.4 %fusion.15 = (bf16[512,1152]{1,0:T(8,128)(2,1)}, f32[512,1152]{1,0:T(8,128)}) fusion(f32[8,1152]{1,0:T(8,128)S(1)} %get-tuple-element.104, f32[512,1152]{1,0:T(8,128)S(1)} %copy-done.9, f32[8,1152]{1,0:T(8,128)S(1)} %get-tuple-element.105, bf16[512,1152]{1,0:T(8,128)(2,1)S(1)} %copy-done.1, f32[1152]{0:T(1024)S(1)} %add.340, ...), kind=kOutput, calls=%fused_computation.47 | convolution fusion | flops 5463539712 | bytes 27228672 | tf_op jit(solution)/shard_map/dot_general | solution.py:53
  287.9 7.6 fusion.108
  295.4 8.8 fusion.97
  304.3 2.7 multiply_reduce_fusion.8
  306.9 1.0 convert_reduce_fusion.7
  308.0 4.0 convert_reduce_fusion.2
  312.0 9.7 %convert_reduce_fusion.3 = (f32[2048]{0:T(1024)S(1)}, bf16[512,2048]{1,0:T(8,128)(2,1)S(1)}) fusion(f32[512,2048]{1,0:T(8,128)S(1)} %copy-done.60, f32[2048]{0:T(1024)S(1)} %bitcast.166, bf16[512,2048]{1,0:T(8,128)(2,1)} %get-tuple-element.89, bf16[2048,2048]{1,0:T(8,128)(2,1)} %all-gather.6.cloned.1.call-done), kind=kOutput, calls=%fused_computation.29 | convolution fusion | flops 4308596736 | bytes 16793600 | tf_op jit(solution)/shard_map/to,io->ti/dot_general | solution.py:45
  321.8 4.4 convert_reduce_fusion.4
  326.3 17.6 %convert_reduce_fusion = (f32[4608]{0:T(1024)S(1)}, bf16[512,4608]{1,0:T(8,128)(2,1)}) fusion(f32[512,4608]{1,0:T(8,128)} %fusion.107, f32[4608]{0:T(1024)S(1)} %add.335, bf16[512,1152]{1,0:T(8,128)(2,1)S(1)} %get-tuple-element.93, bf16[4608,1152]{1,0:T(8,128)(2,1)} %bitcast.139), kind=kOutput, calls=%fused_computation.12 | convolution fusion | flops 5490077184 | bytes 25989120 | tf_op jit(solution)/shard_map/to,io->ti/dot_general | solution.py:45
  343.9 13.6 %multiply_reduce_fusion.2 = (f32[8,1152]{1,0:T(8,128)S(1)}, f32[8,64]{1,0:T(8,128)S(1)}, f32[8,64]{1,0:T(8,128)S(1)}, f32[8,1152]{1,0:T(8,128)S(1)}, f32[8,64,11...) fusion(f32[8,1152]{1,0:T(8,128)S(1)} %get-tuple-element.103, f32[8,64]{1,0:T(8,128)S(1)} %rsqrt.47, ...), kind=kOutput, calls=%fused_computation.64 | convolution fusion | flops 5442876416 | bytes 26107904 | tf_op jit(solution)/shard_map/to,io->ti/dot_general | solution.py:45
  357.5 2.8 multiply_reduce_fusion.1
  361.2 3.6 convert_reduce_fusion.5
  365.2 1.0 copy-done.11
  366.3 1.0 fusion.31
  367.6 6.0 convolution_convert_fusion.7
  373.6 4.8 fusion.26
  378.4 7.3 all-to-all-start.1
  385.8 27.6 %all-reduce.9.cloned.1.call-done = f32[8,4608]{1,0:T(8,128)} async-done(((f32[8,4608]{1,0:T(8,128)}), f32[8,4608]{1,0:T(8,128)}) %all-reduce.9.cloned.1.call-update) | async-done | bytes 147472 | tf_op jit(solution)/shard_map/psum | solution.py:889
  413.4 48.2 %reduce-scatter.4.cloned.1.call-done = bf16[256,768]{1,0:T(8,128)(2,1)} async-done(((bf16[2048,768]{1,0:T(8,128)(2,1)}), bf16[256,768]{1,0:T(8,128)(2,1)}) %reduce-scatter.4.cloned.1.call-update) | async-done | bytes 393232 | tf_op jit(solution)/shard_map/reduce_scatter | solution.py:859
  461.6 10.7 %convolution_convert_fusion.4 = bf16[2048,2048]{1,0:T(8,128)(2,1)} fusion(bf16[512,2048]{1,0:T(8,128)(2,1)} %get-tuple-element.89, f32[512,2048]{1,0:T(8,128)} %fusion.108, f32[2048]{0:T(1024)S(1)} %bitcast.167), kind=kOutput, calls=%fused_computation.17 | convolution fusion | flops 4305453056 | bytes 14688256 | tf_op jit(solution)/shard_map/ti,to->io/dot_general | solution.py:41
  473.9 2.3 and_convert_fusion.pick_ref
  476.2 2.5 copy.53
  478.8 57.1 %attend_backward.1 = bf16[4,8,64,896]{3,2,1,0:T(8,128)(2,1)} custom-call(s32[8]{0:T(128)} %copy-done.7, s32[8]{0:T(128)} %copy-done.8, bf16[4,8,64,1536]{3,2,1,0:T(8,128)(2,1)} %bitcast.178, bf16[4,8,64,288]{3,2,1,0:T(8,128)(2,1)} %bitcast.161, bf16[288,512]{1,0:T(8,128)(2,1)} %and_convert_fusion.2.spread_ref, bf16[1536,896]{1,0:T(8,128)(2,1)} %and_convert_fusion.pick_ref), custom_call_target="tpu_custom_call" | custom-call | flops 42949672960 | bytes 16777216 | tf_op jit(solution)/shard_map/attend_backward/pallas_call | solution.py:170
  535.9 26.2 %reduce-scatter.6.cloned.1.call-done = bf16[256,2048]{1,0:T(8,128)(2,1)} async-done(((bf16[2048,2048]{1,0:T(8,128)(2,1)}), bf16[256,2048]{1,0:T(8,128)(2,1)}) %reduce-scatter.6.cloned.1.call-update) | async-done | bytes 1048592 | tf_op jit(solution)/shard_map/reduce_scatter | solution.py:859
  562.3 9.3 %convolution_convert_fusion.2 = bf16[2048,1152]{1,0:T(8,128)(2,1)} fusion(bf16[2048,896]{1,0:T(8,128)(2,1)} %bitcast.151, bf16[1152,896]{1,0:T(8,128)(2,1)} %bitcast.160), kind=kOutput, calls=%fused_computation.15 | convolution fusion | flops 4230217728 | bytes 10452992 | tf_op jit(solution)/shard_map/to,io->ti/dot_general | solution.py:45
  575.6 5.0 convolution_convert_fusion.5
  580.7 4.3 convolution_convert_fusion.3
  585.0 10.5 %convolution_convert_fusion = bf16[1152,4608]{1,0:T(8,128)(2,1)} fusion(bf16[512,1152]{1,0:T(8,128)(2,1)S(1)} %copy-done.24, bf16[512,4608]{1,0:T(8,128)(2,1)} %get-tuple-element.95), kind=kOutput, calls=%fused_computation | convolution fusion | flops 5441126400 | bytes 16515072 | tf_op jit(solution)/shard_map/ti,to->io/dot_general | solution.py:41
  595.6 10.7 %convolution_convert_fusion.1 = bf16[4608,1152]{1,0:T(8,128)(2,1)} fusion(bf16[512,1152]{1,0:T(8,128)(2,1)S(1)} %copy-done.22, f32[512,4608]{1,0:T(8,128)S(1)} %bitcast.146, f32[4608]{0:T(1024)S(1)} %add.335), kind=kOutput, calls=%fused_computation.1 | convolution fusion | flops 5464719360 | bytes 21252096 | tf_op jit(solution)/shard_map/ti,to->io/dot_general | solution.py:41
  607.0 9.9 %convolution_convert_fusion.6 = bf16[1152,896]{1,0:T(8,128)(2,1)} fusion(bf16[2048,1152]{1,0:T(8,128)(2,1)} %bitcast.174, bf16[2048,896]{1,0:T(8,128)(2,1)} %bitcast.152), kind=kOutput, calls=%fused_computation.35 | convolution fusion | flops 4228890624 | bytes 10452992 | tf_op jit(solution)/shard_map/ti,to->io/dot_general | solution.py:41
  617.0 215.9 %reduce_1.1 = (bf16[144,2048]{1,0:T(8,128)(2,1)}, bf16[576,1152]{1,0:T(8,128)(2,1)}, bf16[4,144,896]{2,1,0:T(8,128)(2,1)}, bf16[144,1152]{1,0:T(8,128)(2,1)}, bf16[144,4608]{1,0:T(8,128)(2,1)}) custom-call(bf16[2,2,2,144,2048]{4,3,2,1,0:T(8,128)(2,1)} %bitcast.150, bf16[2,2,2,576,1152]{4,3,2,1,0:T(8,128)(2,1)} %bitcast.144, ...), custom_call_target="tpu_custom_call" | custom-call | bytes 524288000 | tf_op jit(solution)/shard_map/reduce_1/pallas_call | solution.py:388
  832.9 2.7 slice_convert_fusion
  835.5 5.2 reshape.528
  840.7 5.2 copy.54
  845.9 3.6 reshape.527
  850.5 3.1 convert_element_type.238
  853.6 1.7 convert_element_type.239
  855.3 1.1 convert_element_type.240
  856.7 2.8 convert_element_type.241
  859.5 0.9 convert_element_type.242
  860.4 2.1 fusion.20
  862.7 4.9 bitcast_reduce_fusion
  867.9 34.8 %total_2.1 = f32[8,16,2304]{2,1,0:T(8,128)S(1)} custom-call(f32[16,2304]{1,0:T(8,128)S(1)} %select_maximum_fusion.mine_ref), custom_call_target="tpu_custom_call" | custom-call | tf_op jit(solution)/shard_map/total_2/pallas_call | solution.py:684
  902.9 2.1 fusion.29
  905.0 3.7 fusion.28
  912.5 1.3 fusion.30
  (245 shorter events, 21.0 us)
Async XLA Ops:
  7.2 14.3 %copy-start = (bf16[144,6912]{1,0:T(8,128)(2,1)S(1)}, bf16[144,6912]{1,0:T(8,128)(2,1)}, u32[]{:S(2)}) copy-start(bf16[144,6912]{1,0:T(8,128)(2,1)} %param.30) | copy-start | bytes 5971972
  7.2 13.2 %copy-start.59 = (bf16[1001,144]{0,1:T(8,128)(2,1)S(1)}, bf16[1001,144]{0,1:T(8,128)(2,1)}, u32[]{:S(2)}) copy-start(bf16[1001,144]{0,1:T(8,128)(2,1)} %param.29) | copy-start | bytes 864868
  7.2 13.2 %copy-start.55 = (s32[64]{0:T(128)S(1)}, s32[64]{0:T(128)}, u32[]{:S(2)}) copy-start(s32[64]{0:T(128)} %param.26) | copy-start | bytes 772
  7.2 280.7 %all-gather.4.cloned.1.call-start = ((), (), s32[]{:S(2)}) async-start(), calls=%async_computation.5 | async-start | bytes 5308416 | tf_op jit(solution)/shard_map/all_gather | solution.py:769
  8.2 358.1 %copy-start.47 = (s32[8]{0:T(128)}, s32[8]{0:T(128)S(1)}, u32[]{:S(2)}) copy-start(s32[8]{0:T(128)S(1)} %slice.75) | copy-start | bytes 100
  21.5 2.9 copy-start.6
  165.3 130.1 %all-gather.6.cloned.1.call-start = ((), (), s32[]{:S(2)}) async-start(), calls=%async_computation.6 | async-start | bytes 9437184 | tf_op jit(solution)/shard_map/all_gather | solution.py:769
  174.3 14.6 %copy-start.37 = (s32[288]{0:T(512)}, s32[288]{0:T(512)S(1)}, u32[]{:S(2)}) copy-start(s32[288]{0:T(512)S(1)} %get-tuple-element.123) | copy-start | bytes 3460
  174.3 14.6 %copy-start.39 = (s32[288]{0:T(512)}, s32[288]{0:T(512)S(1)}, u32[]{:S(2)}) copy-start(s32[288]{0:T(512)S(1)} %get-tuple-element.124) | copy-start | bytes 3460
  174.3 14.5 %copy-start.41 = (s32[512]{0:T(512)}, s32[512]{0:T(512)S(1)}, u32[]{:S(2)}) copy-start(s32[512]{0:T(512)S(1)} %get-tuple-element.125) | copy-start | bytes 6148
  174.3 14.5 %copy-start.43 = (s32[512]{0:T(512)}, s32[512]{0:T(512)S(1)}, u32[]{:S(2)}) copy-start(s32[512]{0:T(512)S(1)} %get-tuple-element.126) | copy-start | bytes 6148
  174.6 14.3 %copy-start.8 = (s32[8]{0:T(128)}, s32[8]{0:T(128)S(1)}, u32[]{:S(2)}) copy-start(s32[8]{0:T(128)S(1)} %fusion.65.length_ref) | copy-start | bytes 100
  175.3 13.6 %copy-start.7 = (s32[8]{0:T(128)}, s32[8]{0:T(128)S(1)}, u32[]{:S(2)}) copy-start(s32[8]{0:T(128)S(1)} %get-tuple-element.43.start_ref) | copy-start | bytes 100
  220.0 31.1 %all-to-all-start = ((bf16[4,512,288]{1,2,0:T(8,128)(2,1)}), bf16[4,512,288]{1,2,0:T(8,128)(2,1)}, u32[]{:S(2)}, u32[]{:S(2)}) async-start(bf16[4,512,288]{1,2,0:T(8,128)(2,1)} %copy.52), calls=%async_computation | async-start | bytes 2359296 | tf_op jit(solution)/shard_map/all_to_all | solution.py:824
  225.6 187.8 %all-reduce.9.cloned.1.call-start = ((), (), s32[]{:S(2)}) async-start(), calls=%async_computation.8 | async-start | bytes 294912 | tf_op jit(solution)/shard_map/psum | solution.py:889
  256.9 5.8 copy-start.33
  262.7 13.7 %copy-start.23 = (bf16[512,1152]{1,0:T(8,128)(2,1)}, bf16[512,1152]{1,0:T(8,128)(2,1)S(1)}, u32[]{:S(2)}) copy-start(bf16[512,1152]{1,0:T(8,128)(2,1)S(1)} %fusion.17) | copy-start | bytes 3538948
  262.8 13.7 %slice-start = ((s8[10616832]{0:T(1024)(128)(4,1)}), s8[4194304]{0:T(1024)(128)(4,1)S(1)}, s32[]{:S(2)}) async-start(s8[10616832]{0:T(1024)(128)(4,1)} %bitcast.140), calls=%async_computation.13 | async-start | bytes 8388608
  262.8 13.7 %copy-start.9 = (f32[512,1152]{1,0:T(8,128)S(1)}, f32[512,1152]{1,0:T(8,128)}, u32[]{:S(2)}) copy-start(f32[512,1152]{1,0:T(8,128)} %get-tuple-element.117) | copy-start | bytes 7077892
  262.8 13.7 %slice-start.1 = ((s8[10616832]{0:T(1024)(128)(4,1)}), s8[4194304]{0:T(1024)(128)(4,1)S(1)}, s32[]{:S(2)}) async-start(s8[10616832]{0:T(1024)(128)(4,1)} %bitcast.140), calls=%async_computation.14 | async-start | bytes 8388608
  262.8 13.7 %slice-start.2 = ((s8[10616832]{0:T(1024)(128)(4,1)}), s8[2228224]{0:T(1024)(128)(4,1)S(1)}, s32[]{:S(2)}) async-start(s8[10616832]{0:T(1024)(128)(4,1)} %bitcast.140), calls=%async_computation.15 | async-start | bytes 4456448
  295.4 8.8 copy-start.25
  295.4 8.8 copy-start.58
  304.2 3.7 copy-start.61
  308.0 4.1 copy-start.26
  308.0 4.1 copy-start.60
  308.0 13.8 %slice-start.6 = ((s8[4718592]{0:T(1024)(128)(4,1)}), s8[4194304]{0:T(1024)(128)(4,1)S(1)}, s32[]{:S(2)}) async-start(s8[4718592]{0:T(1024)(128)(4,1)} %bitcast.148), calls=%async_computation.19 | async-start | bytes 8388608
  312.0 9.8 %slice-start.7 = ((s8[4718592]{0:T(1024)(128)(4,1)}), s8[524288]{0:T(1024)(128)(4,1)S(1)}, s32[]{:S(2)}) async-start(s8[4718592]{0:T(1024)(128)(4,1)} %bitcast.148), calls=%async_computation.20 | async-start | bytes 1048576
  312.0 9.8 %copy-start.19 = (bf16[512,1152]{1,0:T(8,128)(2,1)S(1)}, bf16[512,1152]{1,0:T(8,128)(2,1)}, u32[]{:S(2)}) copy-start(bf16[512,1152]{1,0:T(8,128)(2,1)} %param.28) | copy-start | bytes 3538948
  321.8 4.5 copy-start.16
  326.3 17.6 %copy-start.21 = (bf16[512,1152]{1,0:T(8,128)(2,1)}, bf16[512,1152]{1,0:T(8,128)(2,1)S(1)}, u32[]{:S(2)}) copy-start(bf16[512,1152]{1,0:T(8,128)(2,1)S(1)} %get-tuple-element.93) | copy-start | bytes 3538948
  326.3 17.6 %copy-start.10 = (f32[512,1152]{1,0:T(8,128)S(1)}, f32[512,1152]{1,0:T(8,128)}, u32[]{:S(2)}) copy-start(f32[512,1152]{1,0:T(8,128)} %get-tuple-element.117) | copy-start | bytes 7077892
  357.4 3.1 copy-start.12
  357.4 3.8 copy-start.15
  367.3 94.2 %reduce-scatter.4.cloned.1.call-start = ((), (), s32[]{:S(2)}) async-start(), calls=%async_computation.7 | async-start | bytes 3538944 | tf_op jit(solution)/shard_map/reduce_scatter | solution.py:859
  378.4 34.9 %all-to-all-start.1 = ((bf16[4,512,288]{1,2,0:T(8,128)(2,1)}), bf16[4,512,288]{1,2,0:T(8,128)(2,1)}, u32[]{:S(2)}, u32[]{:S(2)}) async-start(bf16[4,512,288]{1,2,0:T(8,128)(2,1)} %fusion.26), calls=%async_computation.1 | async-start | bytes 2359296 | tf_op jit(solution)/shard_map/all_to_all | solution.py:891
  385.8 150.1 %all-gather.8.cloned.1.call-start = ((), (), s32[]{:S(2)}) async-start(), calls=%async_computation.10 | async-start | bytes 1327104 | tf_op jit(solution)/shard_map/all_gather | solution.py:893
  461.6 100.5 %reduce-scatter.6.cloned.1.call-start = ((), (), s32[]{:S(2)}) async-start(), calls=%async_computation.9 | async-start | bytes 9437184 | tf_op jit(solution)/shard_map/reduce_scatter | solution.py:859
  472.4 384.3 %all-reduce.11.cloned.1.call-start = ((), (), s32[]{:S(2)}) async-start(), calls=%async_computation.12 | async-start | bytes 2883584 | tf_op jit(solution)/shard_map/psum | solution.py:898
  562.0 298.4 %reduce-scatter.8.cloned.1.call-start = ((), (), s32[]{:S(2)}) async-start(), calls=%async_computation.11 | async-start | bytes 5898240 | tf_op jit(solution)/shard_map/reduce_scatter | solution.py:914
  571.5 3.5 copy-start.49
  572.9 7.8 copy-start.45
  575.6 5.0 copy-start.17
  575.6 5.0 copy-start.20
  580.6 4.3 copy-start.24
  580.7 14.9 %slice-start.3 = ((s8[9437184]{0:T(1024)(128)(4,1)}), s8[4194304]{0:T(1024)(128)(4,1)S(1)}, s32[]{:S(2)}) async-start(s8[9437184]{0:T(1024)(128)(4,1)} %bitcast.145), calls=%async_computation.16 | async-start | bytes 8388608
  580.7 14.9 %slice-start.4 = ((s8[9437184]{0:T(1024)(128)(4,1)}), s8[4194304]{0:T(1024)(128)(4,1)S(1)}, s32[]{:S(2)}) async-start(s8[9437184]{0:T(1024)(128)(4,1)} %bitcast.145), calls=%async_computation.17 | async-start | bytes 8388608
  585.0 10.6 %slice-start.5 = ((s8[9437184]{0:T(1024)(128)(4,1)}), s8[1048576]{0:T(1024)(128)(4,1)S(1)}, s32[]{:S(2)}) async-start(s8[9437184]{0:T(1024)(128)(4,1)} %bitcast.145), calls=%async_computation.18 | async-start | bytes 2097152
  585.0 10.6 %copy-start.22 = (bf16[512,1152]{1,0:T(8,128)(2,1)S(1)}, bf16[512,1152]{1,0:T(8,128)(2,1)}, u32[]{:S(2)}) copy-start(bf16[512,1152]{1,0:T(8,128)(2,1)} %copy-done.21) | copy-start | bytes 3538948
  595.6 10.8 %copy-start.14 = (bf16[4,8,64,896]{3,2,1,0:T(8,128)(2,1)S(1)}, bf16[4,8,64,896]{3,2,1,0:T(8,128)(2,1)}, u32[]{:S(2)}) copy-start(bf16[4,8,64,896]{3,2,1,0:T(8,128)(2,1)} %attend_backward.1) | copy-start | bytes 11010052
  845.9 3.6 copy-start.32
  849.6 4.0 copy-start.18
  853.6 2.9 copy-start.57
  853.6 2.9 copy-start.35
  853.6 2.9 copy-start.36
  853.6 2.9 copy-start.52
  856.4 4.0 copy-start.31
  856.4 4.0 copy-start.46
  856.6 2.9 copy-start.30
  859.5 3.2 copy-start.50
  859.5 3.2 copy-start.51
  862.7 4.9 copy-start.48
  867.6 35.2 %copy-start.13 = (f32[64,4608]{1,0:T(8,128)S(1)}, f32[64,4608]{1,0:T(8,128)}, u32[]{:S(2)}) copy-start(f32[64,4608]{1,0:T(8,128)} %all-gather.8.cloned.1.call-done) | copy-start | bytes 3538948
  905.0 7.5 copy-start.56
  (16 other events, 24.1 us)
Sparse Core Ops, SparseCore 0:
  165.5 38.4 all-gather.3
  205.9 54.3 all-gather.5
  367.4 45.9 all-reduce.8
  417.6 43.9 reduce-scatter.3
  463.3 24.4 all-gather.7
  491.1 70.8 reduce-scatter.5
  564.6 64.2 all-reduce.10
  631.3 121.7 reduce-scatter.7

commit v3 on v2

--- a/solution.py
+++ b/solution.py
@@ -57,27 +57,39 @@
     return lax.dot_general(left, right, ((contract[:1], contract[1:]), ((), ())), preferred_element_type=F32)
 
 
-def softmax_keys(keys, queries, scale):
-    scores = dot_general(keys, queries, (1, 1)) * scale
-    raised = jnp.exp(scores - jnp.max(scores, axis=0, keepdims=True))
-    return raised * (1.0 / jnp.sum(raised, axis=0, keepdims=True))
-
-
-def attend_forward_kernel(heads, scale, start_ref, length_ref, qkv_ref, pick_ref, out_ref):
+def softmax_base(scale):
+    return scale * math.log2(math.e)
+
+
+def attend_forward_kernel(heads, scale, start_ref, length_ref, qkv_ref, pick_ref, out_ref, norm_ref):
     parts, _, unit, _ = qkv_ref.shape
+    base = softmax_base(scale)
     u = pl.program_id(0)
     first = start_ref[u]
 
+    def head(which, h, at):
+        lane = (which * heads + h) * LANES
+        return qkv_ref[:, pl.ds(at, 1), :, lane : lane + LANES].reshape(parts * unit, LANES)
+
     def work(span):
         outs = []
+        lane = lax.broadcasted_iota(jnp.int32, (parts * unit, LANES), 1)
+        norms = jnp.zeros((parts * unit, LANES), F32)
         for h in range(heads):
-
-            def head(which, lo, n):
-                at = (which * heads + h) * LANES
-                return qkv_ref[:, pl.ds(lo, n), :, at : at + LANES].reshape(parts * n * unit, LANES)
-
-            chance = softmax_keys(head(1, first, span), head(0, u, 1), scale).astype(BF)
-            outs.append(dot_general(chance, head(2, first, span), (0, 0)).astype(BF))
+            query = head(0, h, u)
+            scores = [dot_general(query, head(1, h, first + j), (1, 1)) for j in range(span)]
+            top = scores[0]
+            for block in scores[1:]:
+                top = jnp.maximum(top, block)
+            top = jnp.max(top, axis=1, keepdims=True) * base
+            attended = 0.0
+            for j in range(span):
+                raised = jnp.exp2(scores[j] * base - top).astype(BF)
+                attended = attended + dot(raised, head(2, h, first + j))
+            total = attended[:, LANES - 1 :]
+            norms = jnp.where(lane == h, top + jnp.log2(total), norms)
+            outs.append((attended * (1.0 / total)).astype(BF))
+        norm_ref[0] = jnp.transpose(norms)[:8]
         packed = dot(jnp.concatenate(outs, axis=1), pick_ref[...]).astype(BF)
         out_ref[...] = packed.reshape(out_ref.shape)
 
@@ -86,38 +98,67 @@
 
 
 def attend_backward_kernel(
-    heads, scale, start_ref, length_ref, qkv_ref, grad_ref, spread_ref, pick_ref, out_ref, dq, dk, dv
+    heads,
+    scale,
+    start_ref,
+    length_ref,
+    qkv_ref,
+    norm_ref,
+    attended_ref,
+    grad_ref,
+    spread_ref,
+    mark_ref,
+    pick_ref,
+    out_ref,
+    dq,
+    dk,
+    dv,
+    keys_across,
 ):
     parts, units, unit, _ = qkv_ref.shape
+    base = softmax_base(scale)
     u = pl.program_id(0)
     first = start_ref[u]
+
+    def head(which, h, at):
+        lane = (which * heads + h) * LANES
+        return qkv_ref[:, pl.ds(at, 1), :, lane : lane + LANES].reshape(parts * unit, LANES)
 
     @pl.when(u == 0)
     def _():
         dk[...] = jnp.zeros_like(dk)
         dv[...] = jnp.zeros_like(dv)
 
+        def turn(i, carry):
+            for h in range(heads):
+                keys_across[i, h] = jnp.transpose(head(1, h, i))
+            return carry
+
+        lax.fori_loop(0, units, turn, 0)
+
     def work(span):
-        grads = dot(grad_ref[...].reshape(parts * unit, -1), spread_ref[...]).astype(BF)
+        packed = grad_ref[...].reshape(parts * unit, -1)
+        grads = dot(packed, spread_ref[...]).astype(BF)
+        product = packed.astype(F32) * attended_ref[...].reshape(parts * unit, -1).astype(F32)
+        high = product.astype(BF)
+        low = (product - high.astype(F32)).astype(BF)
+        offsets = dot_general(mark_ref[...], high, (1, 1)) + dot_general(mark_ref[...], low, (1, 1))
+        into = (parts, 1, unit, LANES)
         for h in range(heads):
-
-            def head(which, lo, n):
-                at = (which * heads + h) * LANES
-                return qkv_ref[:, pl.ds(lo, n), :, at : at + LANES].reshape(parts * n * unit, LANES)
-
             at = slice(h * LANES, (h + 1) * LANES)
-            grad = grads[:, at]
-            query, key, value = head(0, u, 1), head(1, first, span), head(2, first, span)
-            chance = softmax_keys(key, query, scale)
-            chance_grad = dot_general(value, grad, (1, 1))
-            offset = jnp.sum(chance * chance_grad, axis=0, keepdims=True)
-            score_grad = (chance * (chance_grad - offset)).astype(BF)
-            into = (parts, span, unit, LANES)
-            dv[:, pl.ds(first, span), :, at] += dot(chance.astype(BF), grad).reshape(into)
-            dk[:, pl.ds(first, span), :, at] += (dot(score_grad, query) * scale).reshape(into)
-            dq[:, pl.ds(u, 1), :, at] = (
-                (dot_general(score_grad, key, (0, 0)) * scale).astype(BF).reshape(parts, 1, unit, LANES)
-            )
+            grad, query = grads[:, at], head(0, h, u)
+            norm, offset = norm_ref[0, h : h + 1, :], offsets[h : h + 1]
+            query_grad = 0.0
+            for j in range(span):
+                key, value = head(1, h, first + j), head(2, h, first + j)
+                chance = jnp.exp2(dot_general(key, query, (1, 1)) * base - norm)
+                chance_grad = dot_general(value, grad, (1, 1))
+                score_grad = (chance * (chance_grad - offset)).astype(BF)
+                block = pl.ds(first + j, 1)
+                dv[:, block, :, at] += dot(chance.astype(BF), grad).reshape(into)
+                dk[:, block, :, at] += dot(score_grad, query).reshape(into)
+                query_grad = query_grad + dot(keys_across[first + j, h], score_grad)
+            dq[:, pl.ds(u, 1), :, at] = jnp.transpose(query_grad * scale).astype(BF).reshape(into)
 
     pl.when(length_ref[u] == 1)(lambda: work(1))
     pl.when(length_ref[u] != 1)(lambda: work(RATIO))
@@ -125,9 +166,11 @@
     @pl.when(u == units - 1)
     def _():
         def pack(i, carry):
-            rows = [ref[:, pl.ds(i, 1)].astype(BF).reshape(parts * unit, -1) for ref in (dq, dk, dv)]
+            at = pl.ds(i, 1)
+            rows = [dq[:, at], (dk[:, at] * scale).astype(BF), dv[:, at].astype(BF)]
+            rows = [row.reshape(parts * unit, -1) for row in rows]
             packed = dot(jnp.concatenate(rows, axis=1), pick_ref[...]).astype(BF)
-            out_ref[:, pl.ds(i, 1)] = packed.reshape(parts, 1, unit, -1)
+            out_ref[:, at] = packed.reshape(parts, 1, unit, -1)
             return carry
 
         lax.fori_loop(0, units, pack, 0)
@@ -153,20 +196,28 @@
             num_scalar_prefetch=2,
             grid=(units,),
             in_specs=[whole(parts, units, unit, lanes), whole(heads * LANES, width)],
-            out_specs=pl.BlockSpec((parts, 1, unit, width), lambda u, *_: (0, u, 0, 0)),
+            out_specs=[
+                pl.BlockSpec((parts, 1, unit, width), lambda u, *_: (0, u, 0, 0)),
+                pl.BlockSpec((1, 8, parts * unit), lambda u, *_: (u, 0, 0)),
+            ],
         ),
-        out_shape=jax.ShapeDtypeStruct((parts, units, unit, width), BF),
+        out_shape=[
+            jax.ShapeDtypeStruct((parts, units, unit, width), BF),
+            jax.ShapeDtypeStruct((units, 8, parts * unit), F32),
+        ],
         compiler_params=pltpu.CompilerParams(vmem_limit_bytes=48 * 2**20),
         cost_estimate=pl.CostEstimate(flops=10 * 2**30, bytes_accessed=16 * 2**20, transcendentals=2**23),
         name="attend_forward",
     )(start, length, qkv, picker(heads, head_dim, BF))
 
 
-def attend_backward(start, length, qkv, grad, heads, head_dim):
+def attend_backward(start, length, qkv, norms, attended, grad, heads, head_dim):
     parts, units, unit, lanes = qkv.shape
     width = heads * head_dim
     whole = lambda *shape: pl.BlockSpec(shape, lambda u, *_: (0,) * len(shape))
+    one_unit = pl.BlockSpec((parts, 1, unit, width), lambda u, *_: (0, u, 0, 0))
     pick = picker(heads, head_dim, BF)
+    mark = (jnp.arange(8)[:, None] == jnp.arange(width)[None, :] // head_dim).astype(BF)
     return pl.pallas_call(
         partial(attend_backward_kernel, heads, 1.0 / math.sqrt(head_dim)),
         grid_spec=pltpu.PrefetchScalarGridSpec(
@@ -174,8 +225,11 @@
             grid=(units,),
             in_specs=[
                 whole(parts, units, unit, lanes),
-                pl.BlockSpec((parts, 1, unit, width), lambda u, *_: (0, u, 0, 0)),
+                pl.BlockSpec((1, 8, parts * unit), lambda u, *_: (u, 0, 0)),
+                one_unit,
+                one_unit,
                 whole(width, heads * LANES),
+                whole(8, width),
                 whole(3 * heads * LANES, whole_lanes(3 * width)),
             ],
             out_specs=whole(parts, units, unit, whole_lanes(3 * width)),
@@ -183,13 +237,14 @@
                 pltpu.VMEM((parts, units, unit, heads * LANES), BF),
                 pltpu.VMEM((parts, units, unit, heads * LANES), F32),
                 pltpu.VMEM((parts, units, unit, heads * LANES), F32),
+                pltpu.VMEM((units, heads, LANES, parts * unit), BF),
             ],
         ),
         out_shape=jax.ShapeDtypeStruct((parts, units, unit, whole_lanes(3 * width)), BF),
         compiler_params=pltpu.CompilerParams(vmem_limit_bytes=56 * 2**20),
         cost_estimate=pl.CostEstimate(flops=40 * 2**30, bytes_accessed=16 * 2**20, transcendentals=2**23),
         name="attend_backward",
-    )(start, length, qkv, grad, pick.T, picker(3 * heads, head_dim, BF, whole_lanes(3 * width)))
+    )(start, length, qkv, norms, attended, grad, pick.T, mark, picker(3 * heads, head_dim, BF, whole_lanes(3 * width)))
 
 
 MESH = pl.DeviceIdType.MESH
@@ -204,11 +259,11 @@
     return up if k % 2 == 0 else rows - up
 
 
-def reduce_kernel(chunks, tensors, *refs):
-    grads, outs, scratch = refs[:tensors], refs[tensors : 2 * tensors], list(refs[2 * tensors :])
-    own, local_sem, send_sem, recv_sem = scratch[:4]
-    bufs = scratch[4:]
-    per = 8
+def reduce_kernel(chunks, tensors, ring, *refs):
+    grads, slots, refs = refs[:tensors], refs[tensors], refs[tensors + 1 :]
+    outs, slots_out, scratch = refs[:tensors], refs[tensors], list(refs[tensors + 1 :])
+    own, local_sem, send_sem, recv_sem, credit, gathered_parts, slots_line, slots_send, slots_recv = scratch[:9]
+    rings = scratch[9:]
     place, z = lax.axis_index("img"), lax.axis_index("blk")
     y, x, c = lax.div(place, 4), lax.rem(lax.div(place, 2), 2), lax.rem(place, 2)
     pair, beside, across = place + 1 - 2 * c, place + 2 - 4 * x, place + 4 - 8 * y
@@ -217,11 +272,12 @@
     outside = (z == 0) | (z == 3)
 
     barrier = pltpu.get_barrier_semaphore()
-    for other in (pair, beside, across):
-        pl.semaphore_signal(barrier, inc=1, device_id={"img": other}, device_id_type=MESH)
     for step in (1, 2, 3):
         pl.semaphore_signal(barrier, inc=1, device_id={"blk": lax.rem(z + step, 4)}, device_id_type=MESH)
-    pl.semaphore_wait(barrier, 6)
+    others = [lax.rem(place + step, 8) for step in range(1, 8)]
+    for other in others:
+        pl.semaphore_signal(barrier, inc=1, device_id={"img": other}, device_id_type=MESH)
+    pl.semaphore_wait(barrier, 10)
 
     def send(k, which, source, target, where):
         return pltpu.make_async_remote_copy(
@@ -240,6 +296,23 @@
     def cut(k):
         return cut_rows(chunks[k][2], k)
 
+    def slot(k):
+        _, _, rows, _, cols, _ = chunks[k]
+        first = cut(k)
+        i = k % ring
+        wide = pl.ds(0, cols)
+        acc, rx, ry, rx2, ry2, from_near, from_far, total = rings
+        return (
+            acc.at[i, :, :, pl.ds(0, rows), wide],
+            rx.at[i, :, pl.ds(0, first), wide],
+            ry.at[i, :, pl.ds(0, rows - first), wide],
+            rx2.at[i, pl.ds(0, rows - first), wide],
+            ry2.at[i, pl.ds(0, first), wide],
+            from_near.at[i, pl.ds(0, rows), wide],
+            from_far.at[i, :, pl.ds(0, rows), wide],
+            total.at[i, pl.ds(0, rows), wide],
+        )
+
     copies = {}
 
     def begin(k, which, source, target, where):
@@ -255,15 +328,27 @@
         )
 
     count = len(chunks)
-    for k in range(count):
+
+    def stage_zero(k):
         grad, _, row, rows, col, cols, _ = parts_of(k)
-        begin(k, 0, grad.at[:, :, 1 - c, pl.ds(row, rows), pl.ds(col, cols)], bufs[per * k], {"img": pair})
+        if k >= ring:
+            pl.semaphore_wait(credit.at[k % ring], 5)
+        begin(k, 0, grad.at[:, :, 1 - c, pl.ds(row, rows), pl.ds(col, cols)], slot(k)[0], {"img": pair})
+
+    for k in range(min(ring, count)):
+        stage_zero(k)
     for k in range(min(2, count)):
         load(k).start()
 
+    wide_chunks = [k for k in range(count) if chunks[k][5]]
+
+    def wide_total(k):
+        _, _, rows, _, cols, _ = chunks[k]
+        return gathered_parts.at[wide_chunks.index(k), :, pl.ds(0, rows), pl.ds(0, cols)]
+
     def stage_one(k):
         _, _, _, rows, _, cols, _ = parts_of(k)
-        acc, rx, ry = bufs[per * k : per * k + 3]
+        acc, rx, ry = slot(k)[:3]
         load(k).wait()
         copies[k, 0].wait_recv()
         for i in range(2):
@@ -277,7 +362,7 @@
 
     def stage_two(k):
         rows = chunks[k][2]
-        acc, rx, ry, rx2, ry2 = bufs[per * k : per * k + 5]
+        acc, rx, ry, rx2, ry2 = slot(k)[:5]
         first = cut(k)
         copies[k, 1].wait_recv()
         copies[k, 2].wait_recv()
@@ -291,7 +376,9 @@
 
     def stage_three(k):
         _, out, row, rows, col, cols, gather = parts_of(k)
-        acc, _, _, rx2, ry2, from_near, from_far, total = bufs[per * k : per * (k + 1)]
+        acc, _, _, rx2, ry2, from_near, from_far, total = slot(k)
+        if gather:
+            total = wide_total(k)
         first = cut(k)
         copies[k, 3].wait_recv()
         copies[k, 4].wait_recv()
@@ -311,7 +398,7 @@
     def stage_four(k):
         if chunks[k][5]:
             return
-        from_near, from_far, total = bufs[per * k + 5 : per * k + 8]
+        from_near, from_far, total = slot(k)[5:]
         copies[k, 6] = send(k, 6, from_far.at[0], from_far.at[1], {"blk": far})
 
         @pl.when(inside)
@@ -323,7 +410,7 @@
     def stage_five(k):
         if chunks[k][5]:
             return
-        from_near, from_far, total = bufs[per * k + 5 : per * k + 8]
+        from_near, from_far, total = slot(k)[5:]
         copies[k, 7] = send(k, 7, total, total, {"blk": near})
 
         @pl.when(inside)
@@ -334,69 +421,132 @@
 
     def stage_six(k):
         _, out, row, rows, col, cols, gather = parts_of(k)
-        total = bufs[per * k + 7]
+        total = wide_total(k) if gather else slot(k)[7]
         if gather:
             for step in (1, 2, 3):
                 copies[k, 4 + step].wait()
             out[:, row : row + rows, col : col + cols] = total[...]
-            return
-        pl.when(outside)(copies[k, 7].wait_recv)
-        out[row : row + rows, col : col + cols] = total[...]
-
+        else:
+            pl.when(outside)(copies[k, 7].wait_recv)
+            out[row : row + rows, col : col + cols] = total[...]
+            pl.when(outside)(copies[k, 5].wait_send)
+            pl.when(inside)(copies[k, 6].wait_send)
+            pl.when(inside)(copies[k, 7].wait_send)
+        for which in (0, 3, 4):
+            copies[k, which].wait_send()
+        if k + ring < count:
+            for other in (pair, beside, across):
+                pl.semaphore_signal(credit.at[k % ring], inc=1, device_id={"img": other}, device_id_type=MESH)
+            for other in (near, far):
+                pl.semaphore_signal(credit.at[k % ring], inc=1, device_id={"blk": other}, device_id_type=MESH)
+
+    def slots_copy(which, source, target, where):
+        return pltpu.make_async_remote_copy(
+            src_ref=source,
+            dst_ref=target,
+            send_sem=slots_send.at[which],
+            recv_sem=slots_recv.at[which],
+            device_id=where,
+            device_id_type=MESH,
+        )
+
+    slots_near = slots_copy(0, slots, slots_line.at[0], {"blk": near})
+    slots_far = slots_copy(8, slots_line.at[1], slots_line.at[2], {"blk": far})
+    slots_back = slots_copy(9, slots_out.at[place], slots_out.at[place], {"blk": near})
+    slots_round = [
+        slots_copy(1 + i, slots_out.at[place], slots_out.at[place], {"img": other}) for i, other in enumerate(others)
+    ]
+
+    def slots_one():
+        pl.when(outside)(slots_near.start)
+
+    def slots_two():
+        @pl.when(inside)
+        def _():
+            slots_near.wait_recv()
+            slots_line[1] = slots_line[0] + slots[...]
+            slots_far.start()
+
+    def slots_three():
+        @pl.when(inside)
+        def _():
+            slots_far.wait_recv()
+            slots_out[place] = slots_line[1] + slots_line[2]
+            slots_back.start()
+
+    def slots_four():
+        pl.when(outside)(slots_back.wait_recv)
+        for copy in slots_round:
+            copy.start()
+
+    def slots_five():
+        for copy in slots_round:
+            copy.wait()
+        pl.when(outside)(slots_near.wait_send)
+        pl.when(inside)(slots_far.wait_send)
+        pl.when(inside)(slots_back.wait_send)
+
+    slots_stages = {0: slots_one, 2: slots_two, 4: slots_three, 6: slots_four, 9: slots_five}
     stages = ((stage_one, 0), (stage_two, 2), (stage_three, 4), (stage_four, 5), (stage_five, 6), (stage_six, 7))
-    for step in range(count + 7):
+    for step in range(max(count + 7, 10)):
         for stage, behind in stages:
             if 0 <= step - behind < count:
                 stage(step - behind)
-    for k in range(count):
-        copies[k, 0].wait_send()
-        copies[k, 3].wait_send()
-        copies[k, 4].wait_send()
-        if not chunks[k][5]:
-            pl.when(outside)(copies[k, 5].wait_send)
-            pl.when(inside)(copies[k, 6].wait_send)
-            pl.when(inside)(copies[k, 7].wait_send)
-
-
-def reduce_call(grads, gathered, depth, width, collective_id):
+        if step - 8 >= 0 and step - 8 + ring < count:
+            stage_zero(step - 8 + ring)
+        if step in slots_stages:
+            slots_stages[step]()
+
+
+def reduce_call(grads, gathered, slots, width, collective_id):
     chunks, shapes = [], []
     for t, grad in enumerate(grads):
         rows, cols = grad.shape[0] // 8, grad.shape[1]
+        depth = 144 if rows % 144 == 0 else 128
         for row in range(0, rows, depth):
             for col in range(0, cols, width):
                 chunks.append((t, row, min(depth, rows - row), col, min(width, cols - col), gathered[t]))
         shapes.append(jax.ShapeDtypeStruct((4, rows, cols) if gathered[t] else (rows, cols), BF))
+    shapes.append(jax.ShapeDtypeStruct((8, *slots.shape), F32))
+    n, ring = len(chunks), 12
+    deep = max(rows for _, _, rows, _, _, _ in chunks)
+    half = (deep // 2 + 15) // 16 * 16
+    dma = pltpu.SemaphoreType.DMA
     scratch = [
-        pltpu.VMEM((2, 2, 2, depth, width), BF),
-        pltpu.SemaphoreType.DMA((2,)),
-        pltpu.SemaphoreType.DMA((len(chunks), 8)),
-        pltpu.SemaphoreType.DMA((len(chunks), 8)),
+        pltpu.VMEM((2, 2, 2, deep, width), BF),
+        dma((2,)),
+        dma((n, 8)),
+        dma((n, 8)),
+        pltpu.SemaphoreType.REGULAR((ring,)),
+        pltpu.VMEM((max(1, sum(g for *_, g in chunks)), 4, deep, width), BF),
+        pltpu.VMEM((3, *slots.shape), F32),
+        dma((10,)),
+        dma((10,)),
     ]
-    for k, (_, _, rows, _, cols, gather) in enumerate(chunks):
-        first = cut_rows(rows, k)
-        for shape in (
-            (2, 2, rows, cols),
-            (2, first, cols),
-            (2, rows - first, cols),
-            (rows - first, cols),
-            (first, cols),
-            (16, cols) if gather else (rows, cols),
-            (1, 16, cols) if gather else (2, rows, cols),
-            (4, rows, cols) if gather else (rows, cols),
-        ):
-            scratch.append(pltpu.VMEM(shape, BF))
+    for shape in (
+        (2, 2, deep, width),
+        (2, half, width),
+        (2, half, width),
+        (half, width),
+        (half, width),
+        (deep, width),
+        (2, deep, width),
+        (deep, width),
+    ):
+        scratch.append(pltpu.VMEM((ring, *shape), BF))
+    vmem, anywhere = pl.BlockSpec(memory_space=pltpu.VMEM), pl.BlockSpec(memory_space=pl.ANY)
     return pl.pallas_call(
-        partial(reduce_kernel, chunks, len(grads)),
+        partial(reduce_kernel, chunks, len(grads), ring),
         out_shape=shapes,
-        in_specs=[pl.BlockSpec(memory_space=pl.ANY)] * len(grads),
-        out_specs=[pl.BlockSpec(memory_space=pltpu.VMEM)] * len(grads),
+        in_specs=[anywhere] * len(grads) + [vmem],
+        out_specs=[vmem] * (len(grads) + 1),
         scratch_shapes=scratch,
         compiler_params=pltpu.CompilerParams(
             collective_id=collective_id, has_side_effects=True, vmem_limit_bytes=56 * 2**20
         ),
         cost_estimate=pl.CostEstimate(flops=0, bytes_accessed=500 * 2**20, transcendentals=0),
         name=f"reduce_{collective_id}",
-    )(*(g.reshape(2, 2, 2, g.shape[0] // 8, g.shape[1]) for g in grads))
+    )(*(g.reshape(2, 2, 2, g.shape[0] // 8, g.shape[1]) for g in grads), slots)
 
 
 def gather_kernel(chunks, tensors, early, hot_ref, x_ref, share_ref, bias_ref, start_ref, *refs):
@@ -818,9 +968,12 @@
 
     bias_mine = lax.dynamic_slice_in_dim(attend_bias_full.reshape(2, parts, mine), place_blk, 1, axis=1)
     bias_mine = jnp.concatenate([bias_mine[0, 0], jnp.zeros((mine,), F32), bias_mine[1, 0]])
-    projected = dot(modulated_group, pad_heads(attend_full[:, : 3 * mine])) + pad_heads(bias_mine)[None, :]
+    is_value = jnp.arange(3 * heads * LANES) >= 2 * heads * LANES
+    is_last = jnp.arange(3 * heads * LANES) % LANES == LANES - 1
+    padded_bias = jnp.where(is_value & is_last, 1.0, pad_heads(bias_mine))
+    projected = dot(modulated_group, pad_heads(attend_full[:, : 3 * mine])) + padded_bias[None, :]
     qkv = projected.astype(BF).reshape(parts, units, unit, 3 * heads * LANES)
-    attended_heads = attend_forward(start, length, qkv, heads, head_dim)
+    attended_heads, norms = attend_forward(start, length, qkv, heads, head_dim)
     attended = lax.all_to_all(
         attended_heads.reshape(parts, count, mine), "blk", split_axis=0, concat_axis=0, tiled=True
     )
@@ -858,10 +1011,10 @@
     def scatter(values):
         return lax.psum_scatter(values, "img", scatter_dimension=0, tiled=True)
 
-    outer_part = scatter(left_product(second, grad_aligned))
+    grad_outer = left_product(second, grad_aligned)
     grad_outer_bias = column_sum(grad_aligned)
     grad_pre_two = local_back(jax.nn.silu, pre_two, right_product(grad_aligned, outer_full)).astype(BF)
-    middle_part = scatter(left_product(first, grad_pre_two))
+    grad_middle_weight = left_product(first, grad_pre_two)
     grad_middle_bias = column_sum(grad_pre_two)
     grad_pre_one = local_back(jax.nn.silu, pre_one, right_product(grad_pre_two, middle_full)).astype(BF)
     grad_inner = left_product(whole_low, grad_pre_one)
@@ -886,33 +1039,38 @@
         rows = jnp.concatenate([jnp.sum(v, axis=1) for v in values], axis=1)
         return jnp.dot(unit_hot.T, rows, precision=HIGH)
 
-    early_slots = lax.psum(slot_sum(grad_gate_one, grad_mod_two, grad_scale_two, grad_gate_two), "blk")
+    early_slots = slot_sum(grad_gate_one, grad_mod_two, grad_scale_two, grad_gate_two)
     grad_attended = jnp.einsum("to,pio->pti", grad_branch_one, output_heads, preferred_element_type=F32)
     grad_heads = lax.all_to_all(grad_attended.astype(BF), "blk", split_axis=0, concat_axis=0, tiled=True)
-    grad_heads, outer_part, early_slots = lax.optimization_barrier((grad_heads, outer_part, early_slots))
-    early_grad = lax.all_gather(early_slots, "img", axis=0, tiled=True)
-    grad_qkv = attend_backward(
-        start, length, qkv, grad_heads.reshape(parts, units, unit, mine), heads, head_dim
-    ).reshape(parts * count, -1)
-    grad_qkv, middle_part, early_grad = lax.optimization_barrier((grad_qkv, middle_part, early_grad))
-    outer_sum, middle_sum = lax.psum((outer_part, middle_part), "blk")
+    grad_heads = grad_heads.reshape(parts, units, unit, mine)
+    grad_qkv = attend_backward(start, length, qkv, norms, attended_heads, grad_heads, heads, head_dim).reshape(parts * count, -1)
     grad_attend = left_product(modulated_group, grad_qkv)
     partial_mod_one = right_product(grad_qkv, attend_full).astype(BF)
-    late_grads = (grad_inner, grad_shrink, grad_attend, grad_output, grad_expand)
+    grads = (
+        grad_outer,
+        grad_middle_weight,
+        grad_inner,
+        grad_attend,
+        grad_output,
+        grad_shrink,
+        grad_expand,
+    )
+    gathered = (False, False, False, True, False, False, False)
     if (devices, parts) == (8, 4):
-        inner_sum, shrink_sum, attend_parts, output_sum, expand_sum = reduce_call(
-            late_grads, (False, False, True, False, False), width // devices, 640, 1
-        )
+        *sums, early_grad = reduce_call(grads, gathered, early_slots, 640, 1)
     else:
-        inner_sum, shrink_sum, attend_part, output_sum, expand_sum = (scatter(g) for g in late_grads)
-        sums = lax.psum((inner_sum, shrink_sum, output_sum, expand_sum), "blk")
-        inner_sum, shrink_sum, output_sum, expand_sum = sums
-        attend_parts = lax.all_gather(attend_part, "blk", axis=0, tiled=False)
+        sums = [scatter(grad) for grad in grads]
+        attend_part = lax.all_gather(sums[3], "blk", axis=0, tiled=False)
+        sums = list(lax.psum(tuple(sums[:3] + sums[4:]), "blk"))
+        sums.insert(3, attend_part)
+        early_grad = lax.all_gather(lax.psum(early_slots, "blk"), "img", axis=0, tiled=False)
+    outer_sum, middle_sum, inner_sum, attend_parts, output_sum, shrink_sum, expand_sum = sums
+    early_grad = early_grad.reshape(devices * slots, -1)
     attend_parts = attend_parts[:, :, : 3 * mine].reshape(parts, -1, 3, mine)
     attend_sum = jnp.transpose(attend_parts, (1, 2, 0, 3)).reshape(-1, 3 * width)
-    grad_mod_one = by_unit(
-        lax.psum_scatter(partial_mod_one, "blk", scatter_dimension=0, tiled=True).astype(F32)
-    )
+    grad_mod_one = lax.psum_scatter(partial_mod_one, "blk", scatter_dimension=0, tiled=True)
+    grad_mod_one, early_grad = lax.optimization_barrier((grad_mod_one, early_grad))
+    grad_mod_one = by_unit(grad_mod_one.astype(F32))
     grad_scale_one = grad_mod_one * normal_one
     grad_source = grad_middle + norm_back(grad_mod_one * (1.0 + scale_one), normal_one, inverse_one)
 

time: 925 us -> 817 us (0.88)
  waiting for transfers between devices: 127 us -> 42.1 us
  matrix products: 195 us -> 182 us
  local copies, waits for them, and re-layouts: 53 us -> 41.6 us
    reduce_scatter x2 -> x0, waiting for transfers between devices: 74.3 us -> none  [scatter(): return lax.psum_scatter(values, 'img', scatter_dimension=0, tiled=True)]
    pallas_call x1, Pallas kernels: 216 us -> 254 us  [reduce_call(): pl.pallas_call(partial(reduce_kernel, chunks, len(grads), ring), out_shap...]
    pallas_call x1, Pallas kernels: 57.1 us -> 28 us  [attend_backward(): pl.pallas_call(partial(attend_backward_kernel, heads, 1.0 / math.sqrt(hea...]
    psum x2 -> x0, waiting for transfers between devices: 27.6 us -> none  [the longest x1 27.6 us: per_device(): lax.psum(slot_sum(grad_gate_one, grad_mod_two, grad_scale_two, grad_gate_...]
    all_to_all x1, waiting for transfers between devices: 0.01 us -> 17.4 us  [per_device(): lax.all_to_all(grad_attended.astype(BF), 'blk', split_axis=0, concat_axis...]
    pallas_call x1, Pallas kernels: 27.5 us -> 12.6 us  [attend_forward(): pl.pallas_call(partial(attend_forward_kernel, heads, 1.0 / math.sqrt(head...]
  transfers between devices with their start and end apart: 10 -> 5, of which waited for: 4 -> 2; matrix products, arithmetic and copies ran while one was open for 20% -> 19% of each run, Pallas kernels for 33% -> 33%
where the time goes in v3:
time: 817 us; the launch traced here: 807 us
  Pallas kernels  467 us (57%)
  matrix products  182 us (22%)
  other arithmetic  45.1 us (6%)
  waiting for transfers between devices  42.1 us (5%)
  local copies, waits for them, and re-layouts  41.6 us (5%)
  between operations  15.2 us (2%)
  starting transfers between devices  13.1 us (2%)
    pallas_call x1, Pallas kernels, reduce_call(): pl.pallas_call(partial(reduce_kernel, chunks, len(grads), ring), out_shap...  254 us
    pallas_call x1, Pallas kernels, gather_call(): pl.pallas_call(partial(gather_kernel, chunks, len(shards), 2 * rows.shape...  141 us
    dot_general x6, matrix products, right_product(): return jnp.einsum('to,io->ti', grad, weight, preferred_element_type=F32)  59.3 us
    dot_general x8, matrix products, dot(): return jnp.dot(left, right, preferred_element_type=F32)  57.3 us
    dot_general x6, matrix products, left_product(): jnp.einsum('ti,to->io', left, right, preferred_element_type=F32).astype(BF)  43 us
    pallas_call x1, Pallas kernels, total_call(): pl.pallas_call(total_kernel, out_shape=jax.ShapeDtypeStruct((devices, *mi...  32.3 us
    pallas_call x1, Pallas kernels, attend_backward(): pl.pallas_call(partial(attend_backward_kernel, heads, 1.0 / math.sqrt(hea...  28 us
    all_to_all x1, waiting for transfers between devices, per_device(): lax.all_to_all(attended_heads.reshape(parts, count, mine), 'blk', split_a...  24.1 us
  transfers between devices with their start and end apart: 5, of which 2 were waited for; matrix products, arithmetic and copies ran while one was open for 19% of the time, Pallas kernels for 33%

profile of v3, /device:TPU:9, one launch (start us, length us, event | category | flops | bytes accessed | tf_op | source)
XLA Modules:
  0.0 806.8 jit_solution(795838655678565259)
XLA Ops:
  7.4 2.9 reshape.527
  10.3 3.6 dynamic-slice_reduce_fusion
  15.3 1.5 convolution_add_fusion.3
  17.4 1.6 convolution_bitcast_fusion.share_ref
  19.1 141.0 %gather_3.1 = (bf16[8,144,896]{2,1,0:T(8,128)(2,1)}, bf16[8,144,1152]{2,1,0:T(8,128)(2,1)}, bf16[8,144,4608]{2,1,0:T(8,128)(2,1)}, bf16[8,256,768]{2,1,0:T(8,128...) custom-call(f32[8,8]{1,0:T(8,128)S(1)} %fusion.76.hot_ref, ...), custom_call_target="tpu_custom_call" | custom-call | bytes 471859200 | tf_op jit(solution)/shard_map/gather_3/pallas_call | solution.py:750
  161.2 4.1 copy.57
  165.2 2.2 pad.23
  168.8 10.2 %add_convert_fusion = bf16[2048,1536]{1,0:T(8,128)(2,1)} fusion(bf16[2048,1152]{1,0:T(8,128)(2,1)S(1)} %bitcast.181, bf16[1152,1536]{0,1:T(8,128)(2,1)S(1)} %bitcast.161, f32[1536]{0:T(1024)S(1)} %bitcast_select_fusion), kind=kOutput, calls=%fused_computation.4 | convolution fusion | flops 7254048768 | bytes 14555136 | tf_op jit(solution)/shard_map/dot_general | solution.py:53
  179.0 12.6 %attend_forward.1 = (bf16[4,8,64,288]{3,2,1,0:T(8,128)(2,1)S(1)}, f32[8,8,256]{2,1,0:T(8,128)S(1)}) custom-call(s32[8]{0:T(128)S(1)} %get-tuple-element.44.start_ref, s32[8]{0:T(128)S(1)} %fusion.65.length_ref, bf16[4,8,64,1536]{3,2,1,0:T(8,128)(2,1)} %bitcast.187, bf16[512,288]{1,0:T(8,128)(2,1)S(1)} %and_convert_fusion.1.pick_ref), custom_call_target="tpu_custom_call" | custom-call | flops 10737418240 | bytes 16777216 | tf_op jit(solution)/shard_map/attend_forward/pallas_call | solution.py:193
  191.6 1.1 copy-done.2
  193.3 2.5 copy.52
  195.8 6.5 all-to-all-start
  203.8 24.1 %all-to-all-done = bf16[4,512,288]{1,2,0:T(8,128)(2,1)} async-done(((bf16[4,512,288]{1,2,0:T(8,128)(2,1)}), bf16[4,512,288]{1,2,0:T(8,128)(2,1)}, u32[]{:S(2)}, u32[]{:S(2)}) %all-to-all-start) | async-done | bytes 1179680 | tf_op jit(solution)/shard_map/all_to_all | solution.py:977
  227.9 6.7 convert_reduce_fusion.6
  234.7 2.8 multiply_reduce_fusion.4
  237.5 2.4 fusion.17
  239.9 13.5 %fusion.107 = f32[512,4608]{1,0:T(8,128)} fusion(bf16[512,1152]{1,0:T(8,128)(2,1)S(1)} %fusion.17, bf16[1152,4608]{1,0:T(8,128)(2,1)} %bitcast.179), kind=kOutput, calls=%fused_computation.225 | convolution fusion | flops 5435817984 | bytes 21233664 | tf_op jit(solution)/shard_map/dot_general | solution.py:53
  253.5 11.4 %fusion.15 = (bf16[512,1152]{1,0:T(8,128)(2,1)}, f32[512,1152]{1,0:T(8,128)}) fusion(f32[8,1152]{1,0:T(8,128)S(1)} %get-tuple-element.104, f32[512,1152]{1,0:T(8,128)S(1)} %copy-done.10, f32[8,1152]{1,0:T(8,128)S(1)} %get-tuple-element.105, bf16[512,1152]{1,0:T(8,128)(2,1)S(1)} %copy-done.1, f32[1152]{0:T(1024)S(1)} %add.338, ...), kind=kOutput, calls=%fused_computation.47 | convolution fusion | flops 5463539712 | bytes 27228672 | tf_op jit(solution)/shard_map/dot_general | solution.py:53
  264.8 7.6 fusion.108
  272.4 8.8 %fusion.97 = f32[512,2048]{1,0:T(8,128)S(1)} fusion(bf16[2048,2048]{1,0:T(8,128)(2,1)} %all-gather.5.cloned.1.call-done, f32[512,2048]{1,0:T(8,128)} %fusion.108, f32[2048]{0:T(1024)S(1)} %bitcast.173), kind=kOutput, calls=%fused_computation.220 | convolution fusion | flops 4301258752 | bytes 16785408 | tf_op jit(solution)/shard_map/dot_general | solution.py:53
  281.3 2.7 multiply_reduce_fusion.8
  284.4 4.0 convert_reduce_fusion.2
  288.5 9.7 %convert_reduce_fusion.3 = (f32[2048]{0:T(1024)S(1)}, bf16[512,2048]{1,0:T(8,128)(2,1)S(1)}) fusion(f32[512,2048]{1,0:T(8,128)S(1)} %copy-done.52, f32[2048]{0:T(1024)S(1)} %bitcast.174, bf16[512,2048]{1,0:T(8,128)(2,1)} %get-tuple-element.89, bf16[2048,2048]{1,0:T(8,128)(2,1)} %all-gather.5.cloned.1.call-done), kind=kOutput, calls=%fused_computation.29 | convolution fusion | flops 4308596736 | bytes 16793600 | tf_op jit(solution)/shard_map/to,io->ti/dot_general | solution.py:45
  298.3 4.4 convert_reduce_fusion.4
  302.7 17.6 %convert_reduce_fusion = (f32[4608]{0:T(1024)S(1)}, bf16[512,4608]{1,0:T(8,128)(2,1)}) fusion(f32[512,4608]{1,0:T(8,128)} %fusion.107, f32[4608]{0:T(1024)S(1)} %add.333, bf16[512,1152]{1,0:T(8,128)(2,1)S(1)} %get-tuple-element.93, bf16[4608,1152]{1,0:T(8,128)(2,1)} %bitcast.142), kind=kOutput, calls=%fused_computation.12 | convolution fusion | flops 5490077184 | bytes 25989120 | tf_op jit(solution)/shard_map/to,io->ti/dot_general | solution.py:45
  320.3 13.6 %multiply_reduce_fusion.2 = (f32[8,1152]{1,0:T(8,128)S(1)}, f32[8,64]{1,0:T(8,128)S(1)}, f32[8,64]{1,0:T(8,128)S(1)}, f32[8,1152]{1,0:T(8,128)S(1)}, f32[8,64,11...) fusion(f32[8,1152]{1,0:T(8,128)S(1)} %get-tuple-element.103, f32[8,64]{1,0:T(8,128)S(1)} %rsqrt.47, ...), kind=kOutput, calls=%fused_computation.64 | convolution fusion | flops 5442876416 | bytes 26107904 | tf_op jit(solution)/shard_map/to,io->ti/dot_general | solution.py:45
  334.0 5.6 convert_reduce_fusion.5
  339.6 1.0 copy-done.25
  340.6 2.7 fusion.26
  343.3 6.3 all-to-all-start.1
  350.4 0.9 and_convert_fusion.2.spread_ref
  351.2 2.5 and_convert_fusion.pick_ref
  354.3 2.7 multiply_reduce_fusion.3
  357.0 17.4 %all-to-all-done.1 = bf16[4,512,288]{1,2,0:T(8,128)(2,1)} async-done(((bf16[4,512,288]{1,2,0:T(8,128)(2,1)}), bf16[4,512,288]{1,2,0:T(8,128)(2,1)}, u32[]{:S(2)}, u32[]{:S(2)}) %all-to-all-start.1) | async-done | bytes 1179680 | tf_op jit(solution)/shard_map/all_to_all | solution.py:1044
  374.4 2.5 copy.53
  376.9 28.0 %attend_backward.1 = bf16[4,8,64,896]{3,2,1,0:T(8,128)(2,1)} custom-call(s32[8]{0:T(128)} %copy-done.7, s32[8]{0:T(128)} %copy-done.8, bf16[4,8,64,1536]{3,2,1,0:T(8,128)(2,1)} %bitcast.188, f32[8,8,256]{2,1,0:T(8,128)} %copy-done.9, bf16[4,8,64,288]{3,2,1,0:T(8,128)(2,1)} %copy-done.2, bf16[4,8,64,288]{3,2,1,0:T(8,128)(2,1)} %bitcast.169, ...), custom_call_target="tpu_custom_call" | custom-call | flops 42949672960 | bytes 16777216 | tf_op jit(solution)/shard_map/attend_backward/pallas_call | solution.py:221
  404.9 9.9 %convolution_convert_fusion.2 = bf16[2048,1152]{1,0:T(8,128)(2,1)} fusion(bf16[2048,896]{1,0:T(8,128)(2,1)} %bitcast.158, bf16[1152,896]{1,0:T(8,128)(2,1)S(1)} %bitcast.168), kind=kOutput, calls=%fused_computation.15 | convolution fusion | flops 4230217728 | bytes 10452992 | tf_op jit(solution)/shard_map/to,io->ti/dot_general | solution.py:45
  414.8 2.8 multiply_reduce_fusion.1
  417.6 1.0 fusion.31.refs_7_
  418.6 4.6 convolution_convert_fusion.5
  423.3 4.7 convolution_convert_fusion.3
  428.0 3.7 convolution_convert_fusion.7
  431.7 8.5 %convolution_convert_fusion = bf16[1152,4608]{1,0:T(8,128)(2,1)} fusion(bf16[512,1152]{1,0:T(8,128)(2,1)S(1)} %copy-done.24, bf16[512,4608]{1,0:T(8,128)(2,1)S(1)} %bitcast.191), kind=kOutput, calls=%fused_computation | convolution fusion | flops 5441126400 | bytes 16515072 | tf_op jit(solution)/shard_map/ti,to->io/dot_general | solution.py:41
  440.2 9.4 %convolution_convert_fusion.4 = bf16[2048,2048]{1,0:T(8,128)(2,1)} fusion(bf16[512,2048]{1,0:T(8,128)(2,1)S(1)} %copy-done.55, f32[512,2048]{1,0:T(8,128)} %fusion.108, f32[2048]{0:T(1024)S(1)} %bitcast.175), kind=kOutput, calls=%fused_computation.17 | convolution fusion | flops 4305453056 | bytes 14688256 | tf_op jit(solution)/shard_map/ti,to->io/dot_general | solution.py:41
  449.7 10.5 %convolution_convert_fusion.1 = bf16[4608,1152]{1,0:T(8,128)(2,1)} fusion(bf16[512,1152]{1,0:T(8,128)(2,1)S(1)} %copy-done.22, f32[512,4608]{1,0:T(8,128)S(1)} %bitcast.152, f32[4608]{0:T(1024)S(1)} %add.333), kind=kOutput, calls=%fused_computation.1 | convolution fusion | flops 5464719360 | bytes 21252096 | tf_op jit(solution)/shard_map/ti,to->io/dot_general | solution.py:41
  460.2 6.3 convolution_convert_fusion.6
  466.4 253.6 %reduce_1.1 = (bf16[256,768]{1,0:T(8,128)(2,1)}, bf16[256,2048]{1,0:T(8,128)(2,1)}, bf16[144,2048]{1,0:T(8,128)(2,1)}, bf16[4,144,896]{2,1,0:T(8,128)(2,1)}, bf1...) custom-call(bf16[2,2,2,256,768]{4,3,2,1,0:T(8,128)(2,1)} %bitcast.162, ...), custom_call_target="tpu_custom_call" | custom-call | bytes 524288000 | tf_op jit(solution)/shard_map/reduce_1/pallas_call | solution.py:538
  720.1 2.7 slice_convert_fusion
  722.7 5.2 reshape.563
  728.0 5.2 copy.54
  733.2 3.6 reshape.562
  736.8 2.6 convert_reduce_fusion.1
  739.5 3.2 convert_element_type.242
  742.7 1.7 convert_element_type.243
  744.4 1.6 convert_element_type.245
  746.0 1.1 convert_element_type.244
  747.1 0.9 convert_element_type.246
  748.1 0.9 convert_element_type.241
  749.1 2.1 fusion.20
  751.4 4.8 bitcast_reduce_fusion
  756.5 32.3 %total_2.1 = f32[8,16,2304]{2,1,0:T(8,128)S(1)} custom-call(f32[16,2304]{1,0:T(8,128)S(1)} %select_maximum_fusion.mine_ref), custom_call_target="tpu_custom_call" | custom-call | tf_op jit(solution)/shard_map/total_2/pallas_call | solution.py:834
  789.6 3.7 fusion.28
  793.3 2.1 fusion.29
  798.5 1.3 fusion.30
  (229 shorter events, 13.0 us)
Async XLA Ops:
  7.2 10.2 %copy-start = (bf16[144,6912]{1,0:T(8,128)(2,1)S(1)}, bf16[144,6912]{1,0:T(8,128)(2,1)}, u32[]{:S(2)}) copy-start(bf16[144,6912]{1,0:T(8,128)(2,1)} %param.30) | copy-start | bytes 5971972
  7.2 7.0 copy-start.51
  7.2 7.8 copy-start.41
  7.2 7.8 copy-start.44
  7.2 7.8 copy-start.40
  7.2 7.8 copy-start.45
  7.3 7.8 copy-start.46
  7.3 7.8 copy-start.47
  7.3 7.8 copy-start.48
  7.3 8.0 copy-start.42
  7.3 257.5 %all-gather.3.cloned.1.call-start = ((), (), s32[]{:S(2)}) async-start(), calls=%async_computation.3 | async-start | bytes 5308416 | tf_op jit(solution)/shard_map/all_gather | solution.py:919
  15.0 187.9 %copy-start.37 = (s32[8]{0:T(128)}, s32[8]{0:T(128)S(1)}, u32[]{:S(2)}) copy-start(s32[8]{0:T(128)S(1)} %slice.75) | copy-start | bytes 100
  15.2 3.9 copy-start.39
  15.2 3.9 copy-start.6
  15.3 3.8 copy-start.1
  15.3 3.8 copy-start.3
  15.3 3.8 copy-start.4
  15.3 3.8 copy-start.5
  160.2 112.2 %all-gather.5.cloned.1.call-start = ((), (), s32[]{:S(2)}) async-start(), calls=%async_computation.4 | async-start | bytes 9437184 | tf_op jit(solution)/shard_map/all_gather | solution.py:919
  165.2 3.5 copy-start.49
  167.8 11.1 %copy-start.8 = (s32[8]{0:T(128)}, s32[8]{0:T(128)S(1)}, u32[]{:S(2)}) copy-start(s32[8]{0:T(128)S(1)} %fusion.65.length_ref) | copy-start | bytes 100
  168.5 10.4 %copy-start.7 = (s32[8]{0:T(128)}, s32[8]{0:T(128)S(1)}, u32[]{:S(2)}) copy-start(s32[8]{0:T(128)S(1)} %get-tuple-element.44.start_ref) | copy-start | bytes 100
  195.8 32.1 %all-to-all-start = ((bf16[4,512,288]{1,2,0:T(8,128)(2,1)}), bf16[4,512,288]{1,2,0:T(8,128)(2,1)}, u32[]{:S(2)}, u32[]{:S(2)}) async-start(bf16[4,512,288]{1,2,0:T(8,128)(2,1)} %copy.52), calls=%async_computation | async-start | bytes 2359296 | tf_op jit(solution)/shard_map/all_to_all | solution.py:977
  239.9 13.6 %copy-start.23 = (bf16[512,1152]{1,0:T(8,128)(2,1)}, bf16[512,1152]{1,0:T(8,128)(2,1)S(1)}, u32[]{:S(2)}) copy-start(bf16[512,1152]{1,0:T(8,128)(2,1)S(1)} %fusion.17) | copy-start | bytes 3538948
  239.9 13.6 %slice-start = ((s8[10616832]{0:T(1024)(128)(4,1)}), s8[4194304]{0:T(1024)(128)(4,1)S(1)}, s32[]{:S(2)}) async-start(s8[10616832]{0:T(1024)(128)(4,1)} %bitcast.143), calls=%async_computation.6 | async-start | bytes 8388608
  239.9 13.5 %copy-start.10 = (f32[512,1152]{1,0:T(8,128)S(1)}, f32[512,1152]{1,0:T(8,128)}, u32[]{:S(2)}) copy-start(f32[512,1152]{1,0:T(8,128)} %get-tuple-element.117) | copy-start | bytes 7077892
  239.9 13.5 %slice-start.1 = ((s8[10616832]{0:T(1024)(128)(4,1)}), s8[4194304]{0:T(1024)(128)(4,1)S(1)}, s32[]{:S(2)}) async-start(s8[10616832]{0:T(1024)(128)(4,1)} %bitcast.143), calls=%async_computation.7 | async-start | bytes 8388608
  239.9 13.5 %slice-start.2 = ((s8[10616832]{0:T(1024)(128)(4,1)}), s8[2228224]{0:T(1024)(128)(4,1)S(1)}, s32[]{:S(2)}) async-start(s8[10616832]{0:T(1024)(128)(4,1)} %bitcast.143), calls=%async_computation.8 | async-start | bytes 4456448
  272.4 8.9 %copy-start.28 = (bf16[512,768]{1,0:T(8,128)(2,1)S(1)}, bf16[512,768]{1,0:T(8,128)(2,1)}, u32[]{:S(2)}) copy-start(bf16[512,768]{1,0:T(8,128)(2,1)} %param.27) | copy-start | bytes 2359300
  272.4 8.9 %copy-start.50 = (bf16[8,256,768]{2,1,0:T(8,128)(2,1)S(1)}, bf16[8,256,768]{2,1,0:T(8,128)(2,1)}, u32[]{:S(2)}) copy-start(bf16[8,256,768]{2,1,0:T(8,128)(2,1)} %get-tuple-element.55) | copy-start | bytes 9437188
  281.2 3.2 copy-start.53
  284.4 4.1 copy-start.29
  284.4 4.1 copy-start.52
  284.4 13.8 %slice-start.6 = ((s8[4718592]{0:T(1024)(128)(4,1)}), s8[4194304]{0:T(1024)(128)(4,1)S(1)}, s32[]{:S(2)}) async-start(s8[4718592]{0:T(1024)(128)(4,1)} %bitcast.156), calls=%async_computation.12 | async-start | bytes 8388608
  288.5 9.8 %slice-start.7 = ((s8[4718592]{0:T(1024)(128)(4,1)}), s8[524288]{0:T(1024)(128)(4,1)S(1)}, s32[]{:S(2)}) async-start(s8[4718592]{0:T(1024)(128)(4,1)} %bitcast.156), calls=%async_computation.13 | async-start | bytes 1048576
  288.5 9.8 %copy-start.19 = (bf16[512,1152]{1,0:T(8,128)(2,1)S(1)}, bf16[512,1152]{1,0:T(8,128)(2,1)}, u32[]{:S(2)}) copy-start(bf16[512,1152]{1,0:T(8,128)(2,1)} %param.28) | copy-start | bytes 3538948
  298.3 4.5 copy-start.15
  302.7 17.6 %copy-start.21 = (bf16[512,1152]{1,0:T(8,128)(2,1)}, bf16[512,1152]{1,0:T(8,128)(2,1)S(1)}, u32[]{:S(2)}) copy-start(bf16[512,1152]{1,0:T(8,128)(2,1)S(1)} %get-tuple-element.93) | copy-start | bytes 3538948
  302.7 17.6 %copy-start.11 = (f32[512,1152]{1,0:T(8,128)S(1)}, f32[512,1152]{1,0:T(8,128)}, u32[]{:S(2)}) copy-start(f32[512,1152]{1,0:T(8,128)} %get-tuple-element.117) | copy-start | bytes 7077892
  333.9 6.6 copy-start.14
  343.3 31.1 %all-to-all-start.1 = ((bf16[4,512,288]{1,2,0:T(8,128)(2,1)}), bf16[4,512,288]{1,2,0:T(8,128)(2,1)}, u32[]{:S(2)}, u32[]{:S(2)}) async-start(bf16[4,512,288]{1,2,0:T(8,128)(2,1)} %fusion.26), calls=%async_computation.1 | async-start | bytes 2359296 | tf_op jit(solution)/shard_map/all_to_all | solution.py:1044
  349.7 399.5 %reduce-scatter.2.cloned.1.call-start = ((), (), s32[]{:S(2)}) async-start(), calls=%async_computation.5 | async-start | bytes 5898240 | tf_op jit(solution)/shard_map/reduce_scatter | solution.py:1071
  376.9 28.0 %copy-start.17 = (bf16[8,144,896]{2,1,0:T(8,128)(2,1)S(1)}, bf16[8,144,896]{2,1,0:T(8,128)(2,1)}, u32[]{:S(2)}) copy-start(bf16[8,144,896]{2,1,0:T(8,128)(2,1)} %get-tuple-element.47) | copy-start | bytes 6193156
  414.8 3.8 copy-start.26
  418.6 4.6 copy-start.16
  418.6 4.6 copy-start.20
  423.2 4.8 copy-start.30
  423.2 4.8 copy-start.54
  423.3 8.4 %slice-start.10 = ((s8[4718592]{0:T(1024)(128)(4,1)}), s8[4194304]{0:T(1024)(128)(4,1)S(1)}, s32[]{:S(2)}) async-start(s8[4718592]{0:T(1024)(128)(4,1)} %bitcast.190), calls=%async_computation.16 | async-start | bytes 8388608
  428.0 3.7 copy-start.24
  428.0 3.7 slice-start.11
  431.7 8.5 %copy-start.55 = (bf16[512,2048]{1,0:T(8,128)(2,1)S(1)}, bf16[512,2048]{1,0:T(8,128)(2,1)}, u32[]{:S(2)}) copy-start(bf16[512,2048]{1,0:T(8,128)(2,1)} %get-tuple-element.89) | copy-start | bytes 6291460
  431.7 17.9 %slice-start.3 = ((s8[9437184]{0:T(1024)(128)(4,1)}), s8[4194304]{0:T(1024)(128)(4,1)S(1)}, s32[]{:S(2)}) async-start(s8[9437184]{0:T(1024)(128)(4,1)} %bitcast.151), calls=%async_computation.9 | async-start | bytes 8388608
  431.7 17.9 %slice-start.4 = ((s8[9437184]{0:T(1024)(128)(4,1)}), s8[4194304]{0:T(1024)(128)(4,1)S(1)}, s32[]{:S(2)}) async-start(s8[9437184]{0:T(1024)(128)(4,1)} %bitcast.151), calls=%async_computation.10 | async-start | bytes 8388608
  440.2 9.4 %slice-start.5 = ((s8[9437184]{0:T(1024)(128)(4,1)}), s8[1048576]{0:T(1024)(128)(4,1)S(1)}, s32[]{:S(2)}) async-start(s8[9437184]{0:T(1024)(128)(4,1)} %bitcast.151), calls=%async_computation.11 | async-start | bytes 2097152
  440.2 9.5 %copy-start.22 = (bf16[512,1152]{1,0:T(8,128)(2,1)S(1)}, bf16[512,1152]{1,0:T(8,128)(2,1)}, u32[]{:S(2)}) copy-start(bf16[512,1152]{1,0:T(8,128)(2,1)} %copy-done.21) | copy-start | bytes 3538948
  440.2 20.0 %slice-start.8 = ((s8[4718592]{0:T(1024)(128)(4,1)}), s8[4194304]{0:T(1024)(128)(4,1)S(1)}, s32[]{:S(2)}) async-start(s8[4718592]{0:T(1024)(128)(4,1)} %bitcast.182), calls=%async_computation.14 | async-start | bytes 8388608
  449.6 10.5 %copy-start.13 = (bf16[4,8,64,896]{3,2,1,0:T(8,128)(2,1)S(1)}, bf16[4,8,64,896]{3,2,1,0:T(8,128)(2,1)}, u32[]{:S(2)}) copy-start(bf16[4,8,64,896]{3,2,1,0:T(8,128)(2,1)} %attend_backward.1) | copy-start | bytes 11010052
  449.7 10.5 %slice-start.9 = ((s8[4718592]{0:T(1024)(128)(4,1)}), s8[524288]{0:T(1024)(128)(4,1)S(1)}, s32[]{:S(2)}) async-start(s8[4718592]{0:T(1024)(128)(4,1)} %bitcast.182), calls=%async_computation.15 | async-start | bytes 1048576
  739.5 3.2 copy-start.18
  744.4 3.6 copy-start.36
  756.2 32.7 %copy-start.12 = (f32[8,8,4608]{2,1,0:T(8,128)S(1)}, f32[8,8,4608]{2,1,0:T(8,128)}, u32[]{:S(2)}) copy-start(f32[8,8,4608]{2,1,0:T(8,128)} %get-tuple-element.57) | copy-start | bytes 3538948
  756.2 33.4 %copy-start.33 = (f32[64,144]{1,0:T(8,128)S(1)}, f32[64,144]{1,0:T(8,128)}, u32[]{:S(2)}) copy-start(f32[64,144]{1,0:T(8,128)} %copy-done.32) | copy-start | bytes 110596
  793.3 5.2 copy-start.43
  (9 other events, 15.3 us)
Sparse Core Ops, SparseCore 0:
  160.3 38.4 all-gather.2
  200.7 54.3 all-gather.4
  414.9 119.5 reduce-scatter.1

commit v4 on v3

--- a/solution.py
+++ b/solution.py
@@ -242,7 +242,7 @@
         ),
         out_shape=jax.ShapeDtypeStruct((parts, units, unit, whole_lanes(3 * width)), BF),
         compiler_params=pltpu.CompilerParams(vmem_limit_bytes=56 * 2**20),
-        cost_estimate=pl.CostEstimate(flops=40 * 2**30, bytes_accessed=16 * 2**20, transcendentals=2**23),
+        cost_estimate=pl.CostEstimate(flops=2**20, bytes_accessed=2**20, transcendentals=0),
         name="attend_backward",
     )(start, length, qkv, norms, attended, grad, pick.T, mark, picker(3 * heads, head_dim, BF, whole_lanes(3 * width)))
 
@@ -259,7 +259,7 @@
     return up if k % 2 == 0 else rows - up
 
 
-def reduce_kernel(chunks, tensors, ring, *refs):
+def reduce_kernel(chunks, tensors, ready, ring, *refs):
     grads, slots, refs = refs[:tensors], refs[tensors], refs[tensors + 1 :]
     outs, slots_out, scratch = refs[:tensors], refs[tensors], list(refs[tensors + 1 :])
     own, local_sem, send_sem, recv_sem, credit, gathered_parts, slots_line, slots_send, slots_recv = scratch[:9]
@@ -295,6 +295,9 @@
 
     def cut(k):
         return cut_rows(chunks[k][2], k)
+
+    def is_ready(k):
+        return chunks[k][0] in ready
 
     def slot(k):
         _, _, rows, _, cols, _ = chunks[k]
@@ -323,8 +326,8 @@
         grad, _, row, rows, col, cols, _ = parts_of(k)
         return pltpu.make_async_copy(
             grad.at[:, :, c, pl.ds(row, rows), pl.ds(col, cols)],
-            own.at[k % 2, :, :, pl.ds(0, rows), pl.ds(0, cols)],
-            local_sem.at[k % 2],
+            own.at[summed.index(k) % 2, :, :, pl.ds(0, rows), pl.ds(0, cols)],
+            local_sem.at[summed.index(k) % 2],
         )
 
     count = len(chunks)
@@ -333,11 +336,14 @@
         grad, _, row, rows, col, cols, _ = parts_of(k)
         if k >= ring:
             pl.semaphore_wait(credit.at[k % ring], 5)
+        if is_ready(k):
+            return
         begin(k, 0, grad.at[:, :, 1 - c, pl.ds(row, rows), pl.ds(col, cols)], slot(k)[0], {"img": pair})
 
     for k in range(min(ring, count)):
         stage_zero(k)
-    for k in range(min(2, count)):
+    summed = [k for k in range(count) if not is_ready(k)]
+    for k in summed[:2]:
         load(k).start()
 
     wide_chunks = [k for k in range(count) if chunks[k][5]]
@@ -348,19 +354,23 @@
 
     def stage_one(k):
         _, _, _, rows, _, cols, _ = parts_of(k)
+        if is_ready(k):
+            return
         acc, rx, ry = slot(k)[:3]
         load(k).wait()
         copies[k, 0].wait_recv()
         for i in range(2):
             for j in range(2):
-                add_into(acc, (i, j), own[k % 2, i, j, :rows, :cols])
-        if k + 2 < count:
-            load(k + 2).start()
+                add_into(acc, (i, j), own[summed.index(k) % 2, i, j, :rows, :cols])
+        for later in summed[summed.index(k) + 2 : summed.index(k) + 3]:
+            load(later).start()
         first = cut(k)
         begin(k, 1, acc.at[:, 1 - x, pl.ds(0, first)], rx, {"img": beside})
         begin(k, 2, acc.at[1 - y, :, pl.ds(first, rows - first)], ry, {"img": across})
 
     def stage_two(k):
+        if is_ready(k):
+            return
         rows = chunks[k][2]
         acc, rx, ry, rx2, ry2 = slot(k)[:5]
         first = cut(k)
@@ -379,6 +389,11 @@
         acc, _, _, rx2, ry2, from_near, from_far, total = slot(k)
         if gather:
             total = wide_total(k)
+        if is_ready(k):
+            from_far[0] = grads[chunks[k][0]][row : row + rows, col : col + cols]
+            copies[k, 5] = send(k, 5, from_far.at[0], from_near, {"blk": near})
+            pl.when(outside)(copies[k, 5].start)
+            return
         first = cut(k)
         copies[k, 3].wait_recv()
         copies[k, 4].wait_recv()
@@ -432,7 +447,7 @@
             pl.when(outside)(copies[k, 5].wait_send)
             pl.when(inside)(copies[k, 6].wait_send)
             pl.when(inside)(copies[k, 7].wait_send)
-        for which in (0, 3, 4):
+        for which in () if is_ready(k) else (0, 3, 4):
             copies[k, which].wait_send()
         if k + ring < count:
             for other in (pair, beside, across):
@@ -498,15 +513,15 @@
             slots_stages[step]()
 
 
-def reduce_call(grads, gathered, slots, width, collective_id):
+def reduce_call(grads, ready, gathered, slots, width, collective_id):
     chunks, shapes = [], []
     for t, grad in enumerate(grads):
-        rows, cols = grad.shape[0] // 8, grad.shape[1]
-        depth = 144 if rows % 144 == 0 else 128
+        rows, cols = grad.shape[0] // (1 if t in ready else 8), grad.shape[1]
+        depth = 144 if rows % 144 == 0 or t in ready else 128
         for row in range(0, rows, depth):
             for col in range(0, cols, width):
-                chunks.append((t, row, min(depth, rows - row), col, min(width, cols - col), gathered[t]))
-        shapes.append(jax.ShapeDtypeStruct((4, rows, cols) if gathered[t] else (rows, cols), BF))
+                chunks.append((t, row, min(depth, rows - row), col, min(width, cols - col), t == gathered))
+        shapes.append(jax.ShapeDtypeStruct((4, rows, cols) if t == gathered else (rows, cols), BF))
     shapes.append(jax.ShapeDtypeStruct((8, *slots.shape), F32))
     n, ring = len(chunks), 12
     deep = max(rows for _, _, rows, _, _, _ in chunks)
@@ -536,9 +551,9 @@
         scratch.append(pltpu.VMEM((ring, *shape), BF))
     vmem, anywhere = pl.BlockSpec(memory_space=pltpu.VMEM), pl.BlockSpec(memory_space=pl.ANY)
     return pl.pallas_call(
-        partial(reduce_kernel, chunks, len(grads), ring),
+        partial(reduce_kernel, chunks, len(grads), ready, ring),
         out_shape=shapes,
-        in_specs=[anywhere] * len(grads) + [vmem],
+        in_specs=[vmem if t in ready else anywhere for t in range(len(grads))] + [vmem],
         out_specs=[vmem] * (len(grads) + 1),
         scratch_shapes=scratch,
         compiler_params=pltpu.CompilerParams(
@@ -546,7 +561,10 @@
         ),
         cost_estimate=pl.CostEstimate(flops=0, bytes_accessed=500 * 2**20, transcendentals=0),
         name=f"reduce_{collective_id}",
-    )(*(g.reshape(2, 2, 2, g.shape[0] // 8, g.shape[1]) for g in grads), slots)
+    )(
+        *(g if t in ready else g.reshape(2, 2, 2, g.shape[0] // 8, g.shape[1]) for t, g in enumerate(grads)),
+        slots,
+    )
 
 
 def gather_kernel(chunks, tensors, early, hot_ref, x_ref, share_ref, bias_ref, start_ref, *refs):
@@ -781,6 +799,24 @@
     )(unit_hot, rows, shares, bias_row, first_modulation, *shards)
 
 
+def assemble_kernel(mine, parts_ref, out_ref):
+    pieces = [
+        parts_ref[part, :, which * mine : (which + 1) * mine].astype(F32)
+        for which in range(3)
+        for part in range(parts_ref.shape[0])
+    ]
+    out_ref[...] = jnp.concatenate(pieces, axis=1)
+
+
+def assemble(parts, mine):
+    return pl.pallas_call(
+        partial(assemble_kernel, mine),
+        out_shape=jax.ShapeDtypeStruct((parts.shape[1], 3 * mine * parts.shape[0]), F32),
+        compiler_params=pltpu.CompilerParams(vmem_limit_bytes=32 * 2**20),
+        name="assemble",
+    )(parts)
+
+
 def total_kernel(mine_ref, out_ref, lines, line_send, line_recv, send_sem, recv_sem):
     place, z = lax.axis_index("img"), lax.axis_index("blk")
     parts, devices = lines.shape[0], out_ref.shape[0]
@@ -895,8 +931,9 @@
     silu_condition = jax.nn.silu(condition).astype(BF)
     shares = dot(silu_condition, modulate_weight)
     biases = (attend_bias, output_bias, expand_bias, shrink_bias, inner_bias, middle_bias, outer_bias)
-    bias_row = jnp.concatenate(biases).astype(F32)
-    bias_row = jnp.pad(bias_row, (0, whole_lanes(bias_row.shape[0]) - bias_row.shape[0]))[None, :]
+    longest = whole_lanes(max(bias.shape[0] for bias in biases))
+    bias_row = jnp.stack([jnp.pad(bias.astype(F32), (0, longest - bias.shape[0])) for bias in biases])
+    bias_row = jnp.pad(bias_row, ((0, 8 - len(biases)), (0, 0)))
     shares = shares.reshape(devices, slots, -1)
 
     labels = token_image[::unit]
@@ -941,11 +978,7 @@
         (inner_weight, middle_weight, modulated_group)
     )
     inner_full, middle_full = gather(inner_shard), gather(middle_shard)
-    full_biases = []
-    at = 0
-    for bias in biases:
-        full_biases.append(got_bias[:, 0, at : at + bias.shape[0]].reshape(-1))
-        at += bias.shape[0]
+    full_biases = [got_bias[:, i, : bias.shape[0]].reshape(-1) for i, bias in enumerate(biases)]
     (
         attend_bias_full,
         output_bias_full,
@@ -1019,6 +1052,10 @@
     grad_pre_one = local_back(jax.nn.silu, pre_one, right_product(grad_pre_two, middle_full)).astype(BF)
     grad_inner = left_product(whole_low, grad_pre_one)
     grad_inner_bias = column_sum(grad_pre_one)
+    early_weights = jnp.concatenate(
+        [g.reshape(devices, -1, g.shape[1]) for g in (grad_inner, grad_middle_weight)], axis=1
+    )
+    early_part = scatter(early_weights.reshape(-1, early_weights.shape[2]))
     grad_whole = by_unit(cotangent.astype(F32)) + by_unit(right_product(grad_pre_one, inner_full))
     grad_gate_two = grad_whole * branch_two
     grad_branch_two = by_row((grad_whole * gate_two).astype(BF))
@@ -1042,32 +1079,25 @@
     early_slots = slot_sum(grad_gate_one, grad_mod_two, grad_scale_two, grad_gate_two)
     grad_attended = jnp.einsum("to,pio->pti", grad_branch_one, output_heads, preferred_element_type=F32)
     grad_heads = lax.all_to_all(grad_attended.astype(BF), "blk", split_axis=0, concat_axis=0, tiled=True)
+    grad_heads, grad_shrink, grad_expand = lax.optimization_barrier((grad_heads, grad_shrink, grad_expand))
     grad_heads = grad_heads.reshape(parts, units, unit, mine)
     grad_qkv = attend_backward(start, length, qkv, norms, attended_heads, grad_heads, heads, head_dim).reshape(parts * count, -1)
-    grad_attend = left_product(modulated_group, grad_qkv)
+    grad_tied, early_sum = lax.optimization_barrier((grad_qkv, lax.psum(early_part, "blk")))
+    grad_attend = left_product(modulated_group, grad_tied)
     partial_mod_one = right_product(grad_qkv, attend_full).astype(BF)
-    grads = (
-        grad_outer,
-        grad_middle_weight,
-        grad_inner,
-        grad_attend,
-        grad_output,
-        grad_shrink,
-        grad_expand,
-    )
-    gathered = (False, False, False, True, False, False, False)
+    grads = (grad_outer, grad_attend, grad_output, grad_shrink, grad_expand)
     if (devices, parts) == (8, 4):
-        *sums, early_grad = reduce_call(grads, gathered, early_slots, 640, 1)
+        *sums, early_grad = reduce_call(grads, (), 1, early_slots, 640, 1)
     else:
         sums = [scatter(grad) for grad in grads]
-        attend_part = lax.all_gather(sums[3], "blk", axis=0, tiled=False)
-        sums = list(lax.psum(tuple(sums[:3] + sums[4:]), "blk"))
-        sums.insert(3, attend_part)
+        attend_part = lax.all_gather(sums[1], "blk", axis=0, tiled=False)
+        sums = list(lax.psum(tuple(sums[:1] + sums[2:]), "blk"))
+        sums.insert(1, attend_part)
         early_grad = lax.all_gather(lax.psum(early_slots, "blk"), "img", axis=0, tiled=False)
-    outer_sum, middle_sum, inner_sum, attend_parts, output_sum, shrink_sum, expand_sum = sums
+    outer_sum, attend_parts, output_sum, shrink_sum, expand_sum = sums
+    inner_sum, middle_sum = early_sum[: inner_weight.shape[0]], early_sum[inner_weight.shape[0] :]
     early_grad = early_grad.reshape(devices * slots, -1)
-    attend_parts = attend_parts[:, :, : 3 * mine].reshape(parts, -1, 3, mine)
-    attend_sum = jnp.transpose(attend_parts, (1, 2, 0, 3)).reshape(-1, 3 * width)
+    attend_sum = assemble(attend_parts, mine)
     grad_mod_one = lax.psum_scatter(partial_mod_one, "blk", scatter_dimension=0, tiled=True)
     grad_mod_one, early_grad = lax.optimization_barrier((grad_mod_one, early_grad))
     grad_mod_one = by_unit(grad_mod_one.astype(F32))

time: 817 us -> 782 us (0.957)
  Pallas kernels: 467 us -> 441 us
    pallas_call x1 -> x2, Pallas kernels: 254 us -> 194 us  [the longest x1 192 us: reduce_call(): pl.pallas_call(partial(reduce_kernel, chunks, len(grads), ready, ring), o...]
    pallas_call x1, Pallas kernels: 28 us -> 50 us  [attend_backward(): pl.pallas_call(partial(attend_backward_kernel, heads, 1.0 / math.sqrt(hea...]
    reduce_scatter x0 -> x1, waiting for transfers between devices: none -> 19.3 us  [scatter(): return lax.psum_scatter(values, 'img', scatter_dimension=0, tiled=True)]
    all_to_all x1, waiting for transfers between devices: 17.4 us -> 0.01 us  [per_device(): lax.all_to_all(grad_attended.astype(BF), 'blk', split_axis=0, concat_axis...]
    convert_element_type x3 -> x0, local copies, waits for them, and re-layouts: 14 us -> none  [per_device(): attend_sum.astype(F32)]
    concatenate x0 -> x1, other arithmetic: none -> 10 us  [per_device(): jnp.concatenate([g.reshape(devices, -1, g.shape[1]) for g in (grad_inner,...]
    pallas_call x1, Pallas kernels: 12.6 us -> 22.2 us  [attend_forward(): pl.pallas_call(partial(attend_forward_kernel, heads, 1.0 / math.sqrt(head...]
  transfers between devices with their start and end apart: 5 -> 7, of which waited for: 2 -> 2; matrix products, arithmetic and copies ran while one was open for 19% -> 23% of each run, Pallas kernels for 33% -> 34%
where the time goes in v4:
time: 782 us; the launch traced here: 778 us
  Pallas kernels  441 us (56%)
  matrix products  189 us (24%)
  other arithmetic  44 us (6%)
  waiting for transfers between devices  40.5 us (5%)
  local copies, waits for them, and re-layouts  35 us (4%)
  between operations  15 us (2%)
  starting transfers between devices  13.2 us (2%)
    pallas_call x1, Pallas kernels, reduce_call(): pl.pallas_call(partial(reduce_kernel, chunks, len(grads), ready, ring), o...  192 us
    pallas_call x1, Pallas kernels, gather_call(): pl.pallas_call(partial(gather_kernel, chunks, len(shards), 2 * rows.shape...  142 us
    dot_general x6, matrix products, right_product(): return jnp.einsum('to,io->ti', grad, weight, preferred_element_type=F32)  65.1 us
    dot_general x8, matrix products, dot(): return jnp.dot(left, right, preferred_element_type=F32)  57.7 us
    pallas_call x1, Pallas kernels, attend_backward(): pl.pallas_call(partial(attend_backward_kernel, heads, 1.0 / math.sqrt(hea...  50 us
    dot_general x6, matrix products, left_product(): jnp.einsum('ti,to->io', left, right, preferred_element_type=F32).astype(BF)  45.7 us
    pallas_call x1, Pallas kernels, total_call(): pl.pallas_call(total_kernel, out_shape=jax.ShapeDtypeStruct((devices, *mi...  32.6 us
    pallas_call x1, Pallas kernels, attend_forward(): pl.pallas_call(partial(attend_forward_kernel, heads, 1.0 / math.sqrt(head...  22.2 us
  transfers between devices with their start and end apart: 7, of which 2 were waited for; matrix products, arithmetic and copies ran while one was open for 23% of the time, Pallas kernels for 34%

profile of v4, /device:TPU:9, one launch (start us, length us, event | category | flops | bytes accessed | tf_op | source)
XLA Modules:
  0.0 777.7 jit_solution(2803315905991268547)
XLA Ops:
  7.4 2.9 reshape.524
  10.3 3.6 dynamic-slice_reduce_fusion
  15.4 1.5 convolution_add_fusion.3
  17.6 1.6 convolution_bitcast_fusion.share_ref
  19.3 142.2 %gather_3.1 = (bf16[8,144,896]{2,1,0:T(8,128)(2,1)}, bf16[8,144,1152]{2,1,0:T(8,128)(2,1)}, bf16[8,144,4608]{2,1,0:T(8,128)(2,1)}, bf16[8,256,768]{2,1,0:T(8,128...) custom-call(f32[8,8]{1,0:T(8,128)S(1)} %fusion.76.hot_ref, ...), custom_call_target="tpu_custom_call" | custom-call | bytes 471859200 | tf_op jit(solution)/shard_map/gather_3/pallas_call | solution.py:768
  163.6 0.9 slice_reduce_fusion.1
  164.8 4.1 copy.51
  168.8 2.3 pad.65
  172.4 10.5 %add_convert_fusion = bf16[2048,1536]{1,0:T(8,128)(2,1)} fusion(bf16[2048,1152]{1,0:T(8,128)(2,1)S(1)} %bitcast.180, bf16[1152,1536]{0,1:T(8,128)(2,1)S(1)} %bitcast.160, f32[1536]{0:T(1024)S(1)} %bitcast_select_fusion), kind=kOutput, calls=%fused_computation.5 | convolution fusion | flops 7254048768 | bytes 14555136 | tf_op jit(solution)/shard_map/dot_general | solution.py:53
  182.9 22.2 %attend_forward.1 = (bf16[4,8,64,288]{3,2,1,0:T(8,128)(2,1)S(1)}, f32[8,8,256]{2,1,0:T(8,128)S(1)}) custom-call(s32[8]{0:T(128)S(1)} %get-tuple-element.47.start_ref, s32[8]{0:T(128)S(1)} %fusion.65.length_ref, bf16[4,8,64,1536]{3,2,1,0:T(8,128)(2,1)} %bitcast.156, bf16[512,288]{1,0:T(8,128)(2,1)S(1)} %and_convert_fusion.1.pick_ref), custom_call_target="tpu_custom_call" | custom-call | flops 10737418240 | bytes 16777216 | tf_op jit(solution)/shard_map/attend_forward/pallas_call | solution.py:193
  205.1 1.1 copy-done.2
  206.9 2.5 copy.47
  209.4 5.4 all-to-all-start
  214.8 1.0 slice_reduce_fusion.3
  215.8 1.0 slice_reduce_fusion
  216.9 0.8 slice_reduce_fusion.4
  217.8 0.9 fusion.103
  219.7 20.6 %all-to-all-done = bf16[4,512,288]{1,2,0:T(8,128)(2,1)} async-done(((bf16[4,512,288]{1,2,0:T(8,128)(2,1)}), bf16[4,512,288]{1,2,0:T(8,128)(2,1)}, u32[]{:S(2)}, u32[]{:S(2)}) %all-to-all-start) | async-done | bytes 1179680 | tf_op jit(solution)/shard_map/all_to_all | solution.py:1010
  240.3 4.5 convert_reduce_fusion.6
  244.8 1.6 multiply_reduce_fusion.4
  247.2 14.0 %fusion.107 = f32[512,4608]{1,0:T(8,128)} fusion(bf16[512,1152]{1,0:T(8,128)(2,1)S(1)} %fusion.17, bf16[1152,4608]{1,0:T(8,128)(2,1)} %bitcast.177), kind=kOutput, calls=%fused_computation.227 | convolution fusion | flops 5435817984 | bytes 21233664 | tf_op jit(solution)/shard_map/dot_general | solution.py:53
  261.2 11.4 %fusion.15 = (bf16[512,1152]{1,0:T(8,128)(2,1)}, f32[512,1152]{1,0:T(8,128)}) fusion(f32[8,1152]{1,0:T(8,128)S(1)} %get-tuple-element.110, f32[512,1152]{1,0:T(8,128)S(1)} %get-tuple-element.123, f32[8,1152]{1,0:T(8,128)S(1)} %get-tuple-element.111, bf16[512,1152]{1,0:T(8,128)(2,1)S(1)} %copy-done.1, f32[1152]{0:T(1024)S(1)} %add.356, ...), kind=kOutput, calls=%fused_computation.48 | convolution fusion | flops 5463539712 | bytes 27228672 | tf_op jit(solution)/shard_map/dot_general | solution.py:53
  272.6 7.6 fusion.108
  280.1 8.6 %fusion.97 = f32[512,2048]{1,0:T(8,128)S(1)} fusion(bf16[2048,2048]{1,0:T(8,128)(2,1)} %all-gather.5.cloned.1.call-done, f32[512,2048]{1,0:T(8,128)} %fusion.108, f32[2048]{0:T(1024)S(1)} %bitcast.174), kind=kOutput, calls=%fused_computation.222 | convolution fusion | flops 4301258752 | bytes 16785408 | tf_op jit(solution)/shard_map/dot_general | solution.py:53
  288.7 2.6 multiply_reduce_fusion.8
  291.9 3.1 convert_reduce_fusion.2
  295.0 5.0 convolution_convert_fusion.3
  299.9 10.2 %convert_reduce_fusion.3 = (f32[2048]{0:T(1024)S(1)}, bf16[512,2048]{1,0:T(8,128)(2,1)S(1)}) fusion(f32[512,2048]{1,0:T(8,128)} %fusion.108, f32[2048]{0:T(1024)S(1)} %bitcast.176, bf16[512,2048]{1,0:T(8,128)(2,1)S(1)} %get-tuple-element.95, bf16[2048,2048]{1,0:T(8,128)(2,1)} %all-gather.5.cloned.1.call-done), kind=kOutput, calls=%fused_computation.30 | convolution fusion | flops 4308596736 | bytes 16793600 | tf_op jit(solution)/shard_map/to,io->ti/dot_general | solution.py:45
  310.2 2.9 convolution_convert_fusion.4
  313.1 10.0 %pad_maximum_fusion = bf16[8,400,2048]{2,1,0:T(8,128)(2,1)} fusion(bf16[8,256,2048]{2,1,0:T(8,128)(2,1)S(1)} %bitcast.154, bf16[8,144,2048]{2,1,0:T(8,128)(2,1)S(1)} %bitcast.159), kind=kLoop, calls=%fused_computation.4 | loop fusion | flops 26214400 | bytes 26214400 | tf_op jit(solution)/shard_map/concatenate | solution.py:1055
  323.8 0.9 and_convert_fusion.2.spread_ref
  324.7 2.3 and_convert_fusion.pick_ref
  327.1 8.3 %convert_reduce_fusion.4 = (f32[1152]{0:T(1024)S(1)}, bf16[512,1152]{1,0:T(8,128)(2,1)S(1)}, f32[512,1152]{1,0:T(8,128)}) fusion(f32[8,1152]{1,0:T(8,128)S(1)} %get-tuple-element.110, bf16[512,2048]{1,0:T(8,128)(2,1)} %copy-done.21, bf16[1152,2048]{1,0:T(8,128)(2,1)} %all-gather.3.cloned.1.call-done, bf16[512,1152]{1,0:T(8,128)(2,1)} %param.28), kind=kOutput, calls=%fused_computation.59 | convolution fusion | flops 2419457024 | bytes 11575808 | tf_op jit(solution)/shard_map/to,io->ti/dot_general | solution.py:45
  335.4 19.6 %convert_reduce_fusion = (f32[4608]{0:T(1024)S(1)}, bf16[512,4608]{1,0:T(8,128)(2,1)}) fusion(f32[512,4608]{1,0:T(8,128)} %fusion.107, f32[4608]{0:T(1024)S(1)} %add.351, bf16[512,1152]{1,0:T(8,128)(2,1)S(1)} %get-tuple-element.99, bf16[4608,1152]{1,0:T(8,128)(2,1)} %bitcast.147), kind=kOutput, calls=%fused_computation.13 | convolution fusion | flops 5490077184 | bytes 25989120 | tf_op jit(solution)/shard_map/to,io->ti/dot_general | solution.py:45
  355.0 13.6 %multiply_reduce_fusion.2 = (f32[8,1152]{1,0:T(8,128)S(1)}, f32[8,64]{1,0:T(8,128)S(1)}, f32[8,64]{1,0:T(8,128)S(1)}, f32[8,1152]{1,0:T(8,128)S(1)}, f32[8,64,11...) fusion(f32[8,1152]{1,0:T(8,128)S(1)} %get-tuple-element.109, f32[8,64]{1,0:T(8,128)S(1)} %rsqrt.47, ...), kind=kOutput, calls=%fused_computation.65 | convolution fusion | flops 5442876416 | bytes 26107904 | tf_op jit(solution)/shard_map/to,io->ti/dot_general | solution.py:45
  368.6 6.0 convert_reduce_fusion.5
  374.7 1.0 copy-done.29
  375.7 2.7 fusion.26
  378.4 7.5 all-to-all-start.1
  385.9 13.7 %convolution_convert_fusion.1 = bf16[4608,1152]{1,0:T(8,128)(2,1)} fusion(bf16[512,1152]{1,0:T(8,128)(2,1)} %copy-done.27, f32[512,4608]{1,0:T(8,128)} %fusion.107, f32[4608]{0:T(1024)S(1)} %add.351), kind=kOutput, calls=%fused_computation.1 | convolution fusion | flops 5464719360 | bytes 21252096 | tf_op jit(solution)/shard_map/ti,to->io/dot_general | solution.py:41
  399.6 19.3 %reduce-scatter.5.cloned.1.call-done = bf16[400,2048]{1,0:T(8,128)(2,1)} async-done(((bf16[3200,2048]{1,0:T(8,128)(2,1)}), bf16[400,2048]{1,0:T(8,128)(2,1)}) %reduce-scatter.5.cloned.1.call-update) | async-done | bytes 1638416 | tf_op jit(solution)/shard_map/reduce_scatter | solution.py:1045
  419.0 10.5 %convolution_convert_fusion = bf16[1152,4608]{1,0:T(8,128)(2,1)} fusion(bf16[512,1152]{1,0:T(8,128)(2,1)} %copy-done.28, bf16[512,4608]{1,0:T(8,128)(2,1)} %get-tuple-element.101), kind=kOutput, calls=%fused_computation | convolution fusion | flops 5441126400 | bytes 16515072 | tf_op jit(solution)/shard_map/ti,to->io/dot_general | solution.py:41
  429.4 2.5 copy.48
  432.0 50.0 %attend_backward.1 = bf16[4,8,64,896]{3,2,1,0:T(8,128)(2,1)} custom-call(s32[8]{0:T(128)} %copy-done.12, s32[8]{0:T(128)} %copy-done.13, bf16[4,8,64,1536]{3,2,1,0:T(8,128)(2,1)} %bitcast.157, f32[8,8,256]{2,1,0:T(8,128)} %copy-done.10, bf16[4,8,64,288]{3,2,1,0:T(8,128)(2,1)} %copy-done.2, bf16[4,8,64,288]{3,2,1,0:T(8,128)(2,1)} %bitcast.158, ...), custom_call_target="tpu_custom_call" | custom-call | flops 1048576 | bytes 1048576 | tf_op jit(solution)/shard_map/attend_backward/pallas_call | solution.py:221
  482.0 10.3 %convolution_convert_fusion.2 = bf16[2048,1152]{1,0:T(8,128)(2,1)} fusion(bf16[2048,896]{1,0:T(8,128)(2,1)} %bitcast.142, bf16[1152,896]{1,0:T(8,128)(2,1)S(1)} %bitcast.167), kind=kOutput, calls=%fused_computation.16 | convolution fusion | flops 4230217728 | bytes 10452992 | tf_op jit(solution)/shard_map/to,io->ti/dot_general | solution.py:45
  493.5 2.8 multiply_reduce_fusion.3
  497.9 1.0 fusion.31.refs_5_
  498.9 4.7 convolution_convert_fusion.5
  503.6 3.7 convolution_convert_fusion.7
  508.2 10.0 %convolution_convert_fusion.6 = bf16[1152,896]{1,0:T(8,128)(2,1)} fusion(bf16[2048,1152]{1,0:T(8,128)(2,1)} %bitcast.179, bf16[2048,896]{1,0:T(8,128)(2,1)} %bitcast.143), kind=kOutput, calls=%fused_computation.36 | convolution fusion | flops 4228890624 | bytes 10452992 | tf_op jit(solution)/shard_map/ti,to->io/dot_general | solution.py:41
  518.2 192.2 %reduce_1.1 = (bf16[256,768]{1,0:T(8,128)(2,1)}, bf16[4,144,896]{2,1,0:T(8,128)(2,1)}, bf16[144,1152]{1,0:T(8,128)(2,1)}, bf16[576,1152]{1,0:T(8,128)(2,1)}, bf1...) custom-call(bf16[2,2,2,256,768]{4,3,2,1,0:T(8,128)(2,1)} %bitcast.161, bf16[2,2,2,144,896]{4,3,2,1,0:T(8,128)(2,1)} %bitcast.165, ...), custom_call_target="tpu_custom_call" | custom-call | bytes 524288000 | tf_op jit(solution)/shard_map/reduce_1/pallas_call | solution.py:553
  710.5 2.1 fusion.20
  712.8 4.7 bitcast_reduce_fusion
  717.8 32.6 %total_2.1 = f32[8,16,2304]{2,1,0:T(8,128)S(1)} custom-call(f32[16,2304]{1,0:T(8,128)S(1)} %select_maximum_fusion.mine_ref), custom_call_target="tpu_custom_call" | custom-call | tf_op jit(solution)/shard_map/total_2/pallas_call | solution.py:870
  751.2 3.7 fusion.28
  754.9 2.1 fusion.29
  760.1 1.5 slice_convert_fusion
  761.6 1.1 slice_convert_fusion.1
  762.8 1.3 fusion.30
  764.1 1.8 convert_element_type.244
  765.8 1.7 convert_element_type.245
  767.5 1.6 assemble.1
  769.2 0.9 convert_element_type.248
  770.1 0.9 convert_element_type.243
  (232 shorter events, 17.5 us)
Async XLA Ops:
  7.2 10.4 %copy-start = (bf16[144,6912]{1,0:T(8,128)(2,1)S(1)}, bf16[144,6912]{1,0:T(8,128)(2,1)}, u32[]{:S(2)}) copy-start(bf16[144,6912]{1,0:T(8,128)(2,1)} %param.30) | copy-start | bytes 5971972
  7.2 7.0 copy-start.56
  7.2 7.8 %copy-start.46 = (bf16[288]{0:T(512)(128)(2,1)S(1)}, bf16[288]{0:T(512)(128)(2,1)}, u32[]{:S(2)}) copy-start(bf16[288]{0:T(512)(128)(2,1)} %param.33) | copy-start | bytes 1732
  7.2 7.9 %copy-start.49 = (bf16[144]{0:T(256)(128)(2,1)S(1)}, bf16[144]{0:T(256)(128)(2,1)}, u32[]{:S(2)}) copy-start(bf16[144]{0:T(256)(128)(2,1)} %param.35) | copy-start | bytes 868
  7.2 7.9 %copy-start.45 = (bf16[576]{0:T(1024)(128)(2,1)S(1)}, bf16[576]{0:T(1024)(128)(2,1)}, u32[]{:S(2)}) copy-start(bf16[576]{0:T(1024)(128)(2,1)} %param.37) | copy-start | bytes 3460
  7.2 7.9 %copy-start.50 = (bf16[144]{0:T(256)(128)(2,1)S(1)}, bf16[144]{0:T(256)(128)(2,1)}, u32[]{:S(2)}) copy-start(bf16[144]{0:T(256)(128)(2,1)} %param.39) | copy-start | bytes 868
  7.3 8.0 %copy-start.51 = (bf16[256]{0:T(256)(128)(2,1)S(1)}, bf16[256]{0:T(256)(128)(2,1)}, u32[]{:S(2)}) copy-start(bf16[256]{0:T(256)(128)(2,1)} %param.41) | copy-start | bytes 1540
  7.3 8.0 %copy-start.52 = (bf16[256]{0:T(256)(128)(2,1)S(1)}, bf16[256]{0:T(256)(128)(2,1)}, u32[]{:S(2)}) copy-start(bf16[256]{0:T(256)(128)(2,1)} %param.43) | copy-start | bytes 1540
  7.3 265.3 %all-gather.3.cloned.1.call-start = ((), (), s32[]{:S(2)}) async-start(), calls=%async_computation.4 | async-start | bytes 5308416 | tf_op jit(solution)/shard_map/all_gather | solution.py:956
  7.3 8.0 %copy-start.53 = (bf16[96]{0:T(256)(128)(2,1)S(1)}, bf16[96]{0:T(256)(128)(2,1)}, u32[]{:S(2)}) copy-start(bf16[96]{0:T(256)(128)(2,1)} %param.45) | copy-start | bytes 580
  7.4 8.0 %copy-start.47 = (s32[64]{0:T(128)S(1)}, s32[64]{0:T(128)}, u32[]{:S(2)}) copy-start(s32[64]{0:T(128)} %param.26) | copy-start | bytes 772
  15.0 203.8 %copy-start.41 = (s32[8]{0:T(128)}, s32[8]{0:T(128)S(1)}, u32[]{:S(2)}) copy-start(s32[8]{0:T(128)S(1)} %slice.78) | copy-start | bytes 100
  15.0 4.2 copy-start.43
  15.1 4.1 copy-start.1
  15.4 3.9 copy-start.3
  15.4 3.9 copy-start.4
  15.4 3.9 copy-start.6
  15.4 3.9 copy-start.7
  162.9 117.3 %all-gather.5.cloned.1.call-start = ((), (), s32[]{:S(2)}) async-start(), calls=%async_computation.5 | async-start | bytes 9437184 | tf_op jit(solution)/shard_map/all_gather | solution.py:956
  168.8 3.6 copy-start.54
  171.5 11.4 %copy-start.13 = (s32[8]{0:T(128)}, s32[8]{0:T(128)S(1)}, u32[]{:S(2)}) copy-start(s32[8]{0:T(128)S(1)} %fusion.65.length_ref) | copy-start | bytes 100
  172.2 10.7 %copy-start.12 = (s32[8]{0:T(128)}, s32[8]{0:T(128)S(1)}, u32[]{:S(2)}) copy-start(s32[8]{0:T(128)S(1)} %get-tuple-element.47.start_ref) | copy-start | bytes 100
  205.1 1.1 copy-start.2
  206.8 11.9 %copy-start.9 = (f32[8,6912]{1,0:T(8,128)S(1)}, f32[8,6912]{1,0:T(8,128)}, u32[]{:S(2)}) copy-start(f32[8,6912]{1,0:T(8,128)} %copy-done.8) | copy-start | bytes 663556
  209.4 30.9 %all-to-all-start = ((bf16[4,512,288]{1,2,0:T(8,128)(2,1)}), bf16[4,512,288]{1,2,0:T(8,128)(2,1)}, u32[]{:S(2)}, u32[]{:S(2)}) async-start(bf16[4,512,288]{1,2,0:T(8,128)(2,1)} %copy.47), calls=%async_computation | async-start | bytes 2359296 | tf_op jit(solution)/shard_map/all_to_all | solution.py:1010
  214.7 204.1 %reduce-scatter.5.cloned.1.call-start = ((), (), s32[]{:S(2)}) async-start(), calls=%async_computation.7 | async-start | bytes 14745600 | tf_op jit(solution)/shard_map/reduce_scatter | solution.py:1045
  244.8 16.4 %copy-start.14 = (f32[512,1152]{1,0:T(8,128)}, f32[512,1152]{1,0:T(8,128)S(1)}, u32[]{:S(2)}) copy-start(f32[512,1152]{1,0:T(8,128)S(1)} %get-tuple-element.123) | copy-start | bytes 7077892
  244.8 2.4 copy-start.39
  247.2 14.0 %copy-start.28 = (bf16[512,1152]{1,0:T(8,128)(2,1)}, bf16[512,1152]{1,0:T(8,128)(2,1)S(1)}, u32[]{:S(2)}) copy-start(bf16[512,1152]{1,0:T(8,128)(2,1)S(1)} %fusion.17) | copy-start | bytes 3538948
  247.2 14.0 %slice-start = ((s8[10616832]{0:T(1024)(128)(4,1)}), s8[4194304]{0:T(1024)(128)(4,1)S(1)}, s32[]{:S(2)}) async-start(s8[10616832]{0:T(1024)(128)(4,1)} %bitcast.148), calls=%async_computation.9 | async-start | bytes 8388608
  247.2 14.0 %slice-start.1 = ((s8[10616832]{0:T(1024)(128)(4,1)}), s8[4194304]{0:T(1024)(128)(4,1)S(1)}, s32[]{:S(2)}) async-start(s8[10616832]{0:T(1024)(128)(4,1)} %bitcast.148), calls=%async_computation.10 | async-start | bytes 8388608
  247.2 14.0 %slice-start.2 = ((s8[10616832]{0:T(1024)(128)(4,1)}), s8[2228224]{0:T(1024)(128)(4,1)S(1)}, s32[]{:S(2)}) async-start(s8[10616832]{0:T(1024)(128)(4,1)} %bitcast.148), calls=%async_computation.11 | async-start | bytes 4456448
  280.1 8.6 %copy-start.31 = (bf16[512,768]{1,0:T(8,128)(2,1)S(1)}, bf16[512,768]{1,0:T(8,128)(2,1)}, u32[]{:S(2)}) copy-start(bf16[512,768]{1,0:T(8,128)(2,1)} %param.27) | copy-start | bytes 2359300
  280.1 8.6 %copy-start.55 = (bf16[8,256,768]{2,1,0:T(8,128)(2,1)S(1)}, bf16[8,256,768]{2,1,0:T(8,128)(2,1)}, u32[]{:S(2)}) copy-start(bf16[8,256,768]{2,1,0:T(8,128)(2,1)} %get-tuple-element.58) | copy-start | bytes 9437188
  288.7 3.1 copy-start.58
  291.8 3.1 copy-start.32
  291.9 3.1 copy-start.57
  299.9 10.3 %copy-start.26 = (bf16[512,1152]{1,0:T(8,128)(2,1)S(1)}, bf16[512,1152]{1,0:T(8,128)(2,1)}, u32[]{:S(2)}) copy-start(bf16[512,1152]{1,0:T(8,128)(2,1)} %get-tuple-element.124) | copy-start | bytes 3538948
  310.2 2.9 copy-start.21
  335.4 19.6 %copy-start.27 = (bf16[512,1152]{1,0:T(8,128)(2,1)}, bf16[512,1152]{1,0:T(8,128)(2,1)S(1)}, u32[]{:S(2)}) copy-start(bf16[512,1152]{1,0:T(8,128)(2,1)S(1)} %get-tuple-element.99) | copy-start | bytes 3538948
  335.4 19.6 %copy-start.15 = (f32[512,1152]{1,0:T(8,128)S(1)}, f32[512,1152]{1,0:T(8,128)}, u32[]{:S(2)}) copy-start(f32[512,1152]{1,0:T(8,128)} %copy-done.14) | copy-start | bytes 7077892
  368.6 7.1 copy-start.20
  374.7 1.0 copy-start.29
  378.4 51.0 %all-to-all-start.1 = ((bf16[4,512,288]{1,2,0:T(8,128)(2,1)}), bf16[4,512,288]{1,2,0:T(8,128)(2,1)}, u32[]{:S(2)}, u32[]{:S(2)}) async-start(bf16[4,512,288]{1,2,0:T(8,128)(2,1)} %fusion.26), calls=%async_computation.1 | async-start | bytes 2359296 | tf_op jit(solution)/shard_map/all_to_all | solution.py:1081
  385.9 122.3 %all-reduce.14.cloned.1.call-start = ((), (), s32[]{:S(2)}) async-start(), calls=%async_computation.8 | async-start | bytes 3276800 | tf_op jit(solution)/shard_map/psum | solution.py:1085
  418.9 291.6 %reduce-scatter.3.cloned.1.call-start = ((), (), s32[]{:S(2)}) async-start(), calls=%async_computation.6 | async-start | bytes 5898240 | tf_op jit(solution)/shard_map/reduce_scatter | solution.py:1101
  432.0 50.0 %copy-start.22 = (bf16[8,144,896]{2,1,0:T(8,128)(2,1)S(1)}, bf16[8,144,896]{2,1,0:T(8,128)(2,1)}, u32[]{:S(2)}) copy-start(bf16[8,144,896]{2,1,0:T(8,128)(2,1)} %get-tuple-element.50) | copy-start | bytes 6193156
  492.3 0.8 copy-start.44
  493.5 3.1 copy-start.16
  493.5 3.8 copy-start.19
  497.3 1.6 copy-start.30
  498.9 4.7 copy-start.33
  498.9 4.7 copy-start.59
  503.6 3.7 copy-start.17
  518.2 192.3 %copy-start.37 = (f32[8,1152]{1,0:T(8,128)S(1)}, f32[8,1152]{1,0:T(8,128)}, u32[]{:S(2)}) copy-start(f32[8,1152]{1,0:T(8,128)} %get-tuple-element.107) | copy-start | bytes 110596
  717.5 33.0 %copy-start.18 = (f32[8,8,4608]{2,1,0:T(8,128)S(1)}, f32[8,8,4608]{2,1,0:T(8,128)}, u32[]{:S(2)}) copy-start(f32[8,8,4608]{2,1,0:T(8,128)} %get-tuple-element.64) | copy-start | bytes 3538948
  717.5 33.7 %copy-start.35 = (f32[64,144]{1,0:T(8,128)S(1)}, f32[64,144]{1,0:T(8,128)}, u32[]{:S(2)}) copy-start(f32[64,144]{1,0:T(8,128)} %copy-done.34) | copy-start | bytes 110596
  754.9 5.2 copy-start.23
  760.1 2.7 copy-start.48
  760.1 4.0 copy-start.25
  762.8 3.1 copy-start.24
  765.8 1.7 copy-start.5
  767.5 1.6 copy-start.36
  767.5 2.5 copy-start.38
  (6 other events, 3.9 us)
Sparse Core Ops, SparseCore 0:
  163.0 38.4 all-gather.2
  203.4 54.3 all-gather.4
  323.3 95.5 reduce-scatter.4
  421.1 70.1 all-reduce.13
  493.5 111.6 reduce-scatter.2

commit v5 on v4

--- a/solution.py
+++ b/solution.py
@@ -1079,31 +1079,14 @@
     early_slots = slot_sum(grad_gate_one, grad_mod_two, grad_scale_two, grad_gate_two)
     grad_attended = jnp.einsum("to,pio->pti", grad_branch_one, output_heads, preferred_element_type=F32)
     grad_heads = lax.all_to_all(grad_attended.astype(BF), "blk", split_axis=0, concat_axis=0, tiled=True)
-    grad_heads, grad_shrink, grad_expand = lax.optimization_barrier((grad_heads, grad_shrink, grad_expand))
+    grad_heads, grad_shrink, grad_expand, grad_output, grad_outer = lax.optimization_barrier(
+        (grad_heads, grad_shrink, grad_expand, grad_output, grad_outer)
+    )
     grad_heads = grad_heads.reshape(parts, units, unit, mine)
     grad_qkv = attend_backward(start, length, qkv, norms, attended_heads, grad_heads, heads, head_dim).reshape(parts * count, -1)
     grad_tied, early_sum = lax.optimization_barrier((grad_qkv, lax.psum(early_part, "blk")))
     grad_attend = left_product(modulated_group, grad_tied)
     partial_mod_one = right_product(grad_qkv, attend_full).astype(BF)
-    grads = (grad_outer, grad_attend, grad_output, grad_shrink, grad_expand)
-    if (devices, parts) == (8, 4):
-        *sums, early_grad = reduce_call(grads, (), 1, early_slots, 640, 1)
-    else:
-        sums = [scatter(grad) for grad in grads]
-        attend_part = lax.all_gather(sums[1], "blk", axis=0, tiled=False)
-        sums = list(lax.psum(tuple(sums[:1] + sums[2:]), "blk"))
-        sums.insert(1, attend_part)
-        early_grad = lax.all_gather(lax.psum(early_slots, "blk"), "img", axis=0, tiled=False)
-    outer_sum, attend_parts, output_sum, shrink_sum, expand_sum = sums
-    inner_sum, middle_sum = early_sum[: inner_weight.shape[0]], early_sum[inner_weight.shape[0] :]
-    early_grad = early_grad.reshape(devices * slots, -1)
-    attend_sum = assemble(attend_parts, mine)
-    grad_mod_one = lax.psum_scatter(partial_mod_one, "blk", scatter_dimension=0, tiled=True)
-    grad_mod_one, early_grad = lax.optimization_barrier((grad_mod_one, early_grad))
-    grad_mod_one = by_unit(grad_mod_one.astype(F32))
-    grad_scale_one = grad_mod_one * normal_one
-    grad_source = grad_middle + norm_back(grad_mod_one * (1.0 + scale_one), normal_one, inverse_one)
-
     qkv_bias = column_sum(grad_qkv[:, : 3 * mine]).reshape(3, 1, mine)
     spread = (jnp.arange(parts) == place_blk).astype(F32)[None, :, None]
     attend_bias_rows = jnp.concatenate([qkv_bias[:1], qkv_bias[2:]]) * spread
@@ -1117,13 +1100,37 @@
         grad_outer_bias,
     )
     bias_rows = jnp.concatenate([b.reshape(devices, -1) for b in bias_grads], axis=1)
+    early_width = early_slots.shape[1]
+    deep = max(slots, devices)
+    early_rows = jnp.concatenate(
+        [
+            jnp.pad(early_slots, ((0, deep - slots), (0, 0))),
+            jnp.pad(bias_rows, ((0, deep - devices), (0, whole_lanes(bias_rows.shape[1]) - bias_rows.shape[1]))),
+        ],
+        axis=1,
+    )
+    grads = (grad_outer, grad_attend, grad_output, grad_shrink, grad_expand)
+    if (devices, parts) == (8, 4):
+        *sums, early = reduce_call(grads, (), 1, early_rows, 640, 1)
+    else:
+        sums = [scatter(grad) for grad in grads]
+        attend_part = lax.all_gather(sums[1], "blk", axis=0, tiled=False)
+        sums = list(lax.psum(tuple(sums[:1] + sums[2:]), "blk"))
+        sums.insert(1, attend_part)
+        early = lax.all_gather(lax.psum(early_rows, "blk"), "img", axis=0, tiled=False)
+    outer_sum, attend_parts, output_sum, shrink_sum, expand_sum = sums
+    inner_sum, middle_sum = early_sum[: inner_weight.shape[0]], early_sum[inner_weight.shape[0] :]
+    attend_sum = assemble(attend_parts, mine)
+    grad_mod_one = lax.psum_scatter(partial_mod_one, "blk", scatter_dimension=0, tiled=True)
+    grad_mod_one, early = lax.optimization_barrier((grad_mod_one, early))
+    early_grad = early[:, :slots, :early_width].reshape(devices * slots, -1)
+    grad_mod_one = by_unit(grad_mod_one.astype(F32))
+    grad_scale_one = grad_mod_one * normal_one
+    grad_source = grad_middle + norm_back(grad_mod_one * (1.0 + scale_one), normal_one, inverse_one)
+
     late_slots = slot_sum(grad_mod_one, grad_scale_one)
-    late_rows = jnp.concatenate(
-        [late_slots, jnp.pad(bias_rows, ((0, 0), (0, late_slots.shape[1] - bias_rows.shape[1])))], axis=0
-    )
-    late = total_call(late_rows, devices, parts, 2)
-    late_grad = late[:, :slots].reshape(devices * slots, 2 * width)
-    bias_sum = jnp.sum(lax.dynamic_index_in_dim(late, slots + place_img, axis=1, keepdims=False), axis=0)
+    late_grad = total_call(late_slots, devices, parts, 2).reshape(devices * slots, 2 * width)
+    bias_sum = jnp.sum(lax.dynamic_index_in_dim(early, place_img, axis=1, keepdims=False)[:, early_width:], axis=0)
     bias_sums = []
     at = 0
     for bias in biases:

time: 782 us -> 768 us (0.982)
  Pallas kernels: 441 us -> 430 us
    pallas_call x1, Pallas kernels: 192 us -> 205 us  [reduce_call(): pl.pallas_call(partial(reduce_kernel, chunks, len(grads), ready, ring), o...]
    pallas_call x1, Pallas kernels: 50 us -> 39 us  [attend_backward(): pl.pallas_call(partial(attend_backward_kernel, heads, 1.0 / math.sqrt(hea...]
    reduce_scatter x1, waiting for transfers between devices: 19.3 us -> 8.47 us  [scatter(): return lax.psum_scatter(values, 'img', scatter_dimension=0, tiled=True)]
    psum x1, waiting for transfers between devices: 0.02 us -> 8.22 us  [per_device(): lax.psum(early_part, 'blk')]
    pallas_call x1, Pallas kernels: 32.6 us -> 24.4 us  [total_call(): pl.pallas_call(total_kernel, out_shape=jax.ShapeDtypeStruct((devices, *mi...]
  transfers between devices with their start and end apart: 7 -> 7, of which waited for: 2 -> 3; matrix products, arithmetic and copies ran while one was open for 23% -> 24% of each run, Pallas kernels for 34% -> 34%
where the time goes in v5:
time: 768 us; the launch traced here: 762 us
  Pallas kernels  430 us (56%)
  matrix products  189 us (25%)
  other arithmetic  42.5 us (6%)
  local copies, waits for them, and re-layouts  35.7 us (5%)
  waiting for transfers between devices  35.1 us (5%)
  between operations  15.4 us (2%)
  starting transfers between devices  14.6 us (2%)
    pallas_call x1, Pallas kernels, reduce_call(): pl.pallas_call(partial(reduce_kernel, chunks, len(grads), ready, ring), o...  205 us
    pallas_call x1, Pallas kernels, gather_call(): pl.pallas_call(partial(gather_kernel, chunks, len(shards), 2 * rows.shape...  142 us
    dot_general x6, matrix products, right_product(): return jnp.einsum('to,io->ti', grad, weight, preferred_element_type=F32)  65.9 us
    dot_general x8, matrix products, dot(): return jnp.dot(left, right, preferred_element_type=F32)  57.6 us
    dot_general x6, matrix products, left_product(): jnp.einsum('ti,to->io', left, right, preferred_element_type=F32).astype(BF)  45 us
    pallas_call x1, Pallas kernels, attend_backward(): pl.pallas_call(partial(attend_backward_kernel, heads, 1.0 / math.sqrt(hea...  39 us
    pallas_call x1, Pallas kernels, total_call(): pl.pallas_call(total_kernel, out_shape=jax.ShapeDtypeStruct((devices, *mi...  24.4 us
    all_to_all x1, waiting for transfers between devices, per_device(): lax.all_to_all(attended_heads.reshape(parts, count, mine), 'blk', split_a...  17.9 us
  transfers between devices with their start and end apart: 7, of which 3 were waited for; matrix products, arithmetic and copies ran while one was open for 24% of the time, Pallas kernels for 34%

profile of v5, /device:TPU:9, one launch (start us, length us, event | category | flops | bytes accessed | tf_op | source)
XLA Modules:
  0.0 761.6 jit_solution(3938420576005513319)
XLA Ops:
  7.4 2.9 reshape.530
  10.3 3.6 dynamic-slice_reduce_fusion
  15.4 1.5 convolution_add_fusion.3
  17.6 1.6 convolution_bitcast_fusion.share_ref
  19.3 142.2 %gather_3.1 = (bf16[8,144,896]{2,1,0:T(8,128)(2,1)}, bf16[8,144,1152]{2,1,0:T(8,128)(2,1)}, bf16[8,144,4608]{2,1,0:T(8,128)(2,1)}, bf16[8,256,768]{2,1,0:T(8,128...) custom-call(f32[8,8]{1,0:T(8,128)S(1)} %fusion.76.hot_ref, ...), custom_call_target="tpu_custom_call" | custom-call | bytes 471859200 | tf_op jit(solution)/shard_map/gather_3/pallas_call | solution.py:768
  163.6 0.9 slice_reduce_fusion.2
  164.8 4.1 copy.52
  168.8 2.3 pad.65
  172.4 10.5 %add_convert_fusion = bf16[2048,1536]{1,0:T(8,128)(2,1)} fusion(bf16[2048,1152]{1,0:T(8,128)(2,1)S(1)} %bitcast.185, bf16[1152,1536]{0,1:T(8,128)(2,1)S(1)} %bitcast.164, f32[1536]{0:T(1024)S(1)} %bitcast_select_fusion), kind=kOutput, calls=%fused_computation.5 | convolution fusion | flops 7254048768 | bytes 14555136 | tf_op jit(solution)/shard_map/dot_general | solution.py:53
  182.9 17.7 %attend_forward.1 = (bf16[4,8,64,288]{3,2,1,0:T(8,128)(2,1)S(1)}, f32[8,8,256]{2,1,0:T(8,128)S(1)}) custom-call(s32[8]{0:T(128)S(1)} %get-tuple-element.49.start_ref, s32[8]{0:T(128)S(1)} %fusion.65.length_ref, bf16[4,8,64,1536]{3,2,1,0:T(8,128)(2,1)} %bitcast.160, bf16[512,288]{1,0:T(8,128)(2,1)S(1)} %and_convert_fusion.1.pick_ref), custom_call_target="tpu_custom_call" | custom-call | flops 10737418240 | bytes 16777216 | tf_op jit(solution)/shard_map/attend_forward/pallas_call | solution.py:193
  200.7 1.1 copy-done.2
  202.4 2.5 copy.47
  204.9 5.4 all-to-all-start
  210.3 1.0 slice_reduce_fusion.4
  211.3 1.0 slice_reduce_fusion.1
  213.3 0.9 fusion.103
  215.2 17.9 %all-to-all-done = bf16[4,512,288]{1,2,0:T(8,128)(2,1)} async-done(((bf16[4,512,288]{1,2,0:T(8,128)(2,1)}), bf16[4,512,288]{1,2,0:T(8,128)(2,1)}, u32[]{:S(2)}, u32[]{:S(2)}) %all-to-all-start) | async-done | bytes 1179680 | tf_op jit(solution)/shard_map/all_to_all | solution.py:1010
  233.1 4.5 convert_reduce_fusion.6
  237.7 1.6 multiply_reduce_fusion.4
  240.0 13.9 %fusion.107 = f32[512,4608]{1,0:T(8,128)} fusion(bf16[512,1152]{1,0:T(8,128)(2,1)S(1)} %fusion.17, bf16[1152,4608]{1,0:T(8,128)(2,1)} %bitcast.182), kind=kOutput, calls=%fused_computation.229 | convolution fusion | flops 5435817984 | bytes 21233664 | tf_op jit(solution)/shard_map/dot_general | solution.py:53
  254.0 11.3 %fusion.15 = (bf16[512,1152]{1,0:T(8,128)(2,1)}, f32[512,1152]{1,0:T(8,128)}) fusion(f32[8,1152]{1,0:T(8,128)S(1)} %get-tuple-element.115, f32[512,1152]{1,0:T(8,128)S(1)} %get-tuple-element.128, f32[8,1152]{1,0:T(8,128)S(1)} %get-tuple-element.116, bf16[512,1152]{1,0:T(8,128)(2,1)S(1)} %copy-done.1, f32[1152]{0:T(1024)S(1)} %add.354, ...), kind=kOutput, calls=%fused_computation.48 | convolution fusion | flops 5463539712 | bytes 27228672 | tf_op jit(solution)/shard_map/dot_general | solution.py:53
  265.3 7.6 fusion.108
  272.9 8.6 %fusion.97 = f32[512,2048]{1,0:T(8,128)S(1)} fusion(bf16[2048,2048]{1,0:T(8,128)(2,1)} %all-gather.5.cloned.1.call-done, f32[512,2048]{1,0:T(8,128)} %fusion.108, f32[2048]{0:T(1024)S(1)} %bitcast.179), kind=kOutput, calls=%fused_computation.224 | convolution fusion | flops 4301258752 | bytes 16785408 | tf_op jit(solution)/shard_map/dot_general | solution.py:53
  281.5 2.6 multiply_reduce_fusion.8
  284.6 3.1 convert_reduce_fusion.2
  287.7 5.0 convolution_convert_fusion.3
  292.6 10.2 %convert_reduce_fusion.3 = (f32[2048]{0:T(1024)S(1)}, bf16[512,2048]{1,0:T(8,128)(2,1)S(1)}) fusion(f32[512,2048]{1,0:T(8,128)} %fusion.108, f32[2048]{0:T(1024)S(1)} %bitcast.181, bf16[512,2048]{1,0:T(8,128)(2,1)S(1)} %get-tuple-element.101, bf16[2048,2048]{1,0:T(8,128)(2,1)} %all-gather.5.cloned.1.call-done), kind=kOutput, calls=%fused_computation.30 | convolution fusion | flops 4308596736 | bytes 16793600 | tf_op jit(solution)/shard_map/to,io->ti/dot_general | solution.py:45
  302.9 2.9 convolution_convert_fusion.4
  305.8 9.8 %pad_maximum_fusion = bf16[8,400,2048]{2,1,0:T(8,128)(2,1)} fusion(bf16[8,256,2048]{2,1,0:T(8,128)(2,1)S(1)} %bitcast.158, bf16[8,144,2048]{2,1,0:T(8,128)(2,1)S(1)} %bitcast.163), kind=kLoop, calls=%fused_computation.4 | loop fusion | flops 26214400 | bytes 26214400 | tf_op jit(solution)/shard_map/concatenate | solution.py:1055
  316.3 0.9 and_convert_fusion.2.spread_ref
  317.2 2.3 and_convert_fusion.pick_ref
  319.6 7.7 %convert_reduce_fusion.4 = (f32[1152]{0:T(1024)S(1)}, bf16[512,1152]{1,0:T(8,128)(2,1)S(1)}, f32[512,1152]{1,0:T(8,128)}) fusion(f32[8,1152]{1,0:T(8,128)S(1)} %get-tuple-element.115, bf16[512,2048]{1,0:T(8,128)(2,1)} %copy-done.19, bf16[1152,2048]{1,0:T(8,128)(2,1)} %all-gather.3.cloned.1.call-done, bf16[512,1152]{1,0:T(8,128)(2,1)} %param.28), kind=kOutput, calls=%fused_computation.62 | convolution fusion | flops 2419457024 | bytes 11575808 | tf_op jit(solution)/shard_map/to,io->ti/dot_general | solution.py:45
  327.3 19.7 %convert_reduce_fusion = (f32[4608]{0:T(1024)S(1)}, bf16[512,4608]{1,0:T(8,128)(2,1)}) fusion(f32[512,4608]{1,0:T(8,128)} %fusion.107, f32[4608]{0:T(1024)S(1)} %add.349, bf16[512,1152]{1,0:T(8,128)(2,1)S(1)} %get-tuple-element.105, bf16[4608,1152]{1,0:T(8,128)(2,1)} %bitcast.152), kind=kOutput, calls=%fused_computation.13 | convolution fusion | flops 5490077184 | bytes 25989120 | tf_op jit(solution)/shard_map/to,io->ti/dot_general | solution.py:45
  347.0 15.0 %multiply_reduce_fusion.2 = (f32[8,1152]{1,0:T(8,128)S(1)}, f32[8,64]{1,0:T(8,128)S(1)}, f32[8,64]{1,0:T(8,128)S(1)}, f32[8,1152]{1,0:T(8,128)S(1)}, f32[8,64,11...) fusion(f32[8,1152]{1,0:T(8,128)S(1)} %get-tuple-element.114, f32[8,64]{1,0:T(8,128)S(1)} %rsqrt.47, ...), kind=kOutput, calls=%fused_computation.65 | convolution fusion | flops 5442876416 | bytes 26107904 | tf_op jit(solution)/shard_map/to,io->ti/dot_general | solution.py:45
  362.0 4.1 multiply_reduce_fusion.3
  366.1 1.4 copy-done.16
  367.8 1.0 copy-done.29
  368.8 2.7 fusion.26
  371.6 8.8 %all-to-all-start.1 = ((bf16[4,512,288]{1,2,0:T(8,128)(2,1)}), bf16[4,512,288]{1,2,0:T(8,128)(2,1)}, u32[]{:S(2)}, u32[]{:S(2)}) async-start(bf16[4,512,288]{1,2,0:T(8,128)(2,1)} %fusion.26), calls=%async_computation.1 | async-start | bytes 2359296 | tf_op jit(solution)/shard_map/all_to_all | solution.py:1081
  380.4 5.0 convolution_convert_fusion.5
  385.3 12.9 %convolution_convert_fusion.1 = bf16[4608,1152]{1,0:T(8,128)(2,1)} fusion(bf16[512,1152]{1,0:T(8,128)(2,1)S(1)} %copy-done.26, f32[512,4608]{1,0:T(8,128)} %fusion.107, f32[4608]{0:T(1024)S(1)} %add.349), kind=kOutput, calls=%fused_computation.1 | convolution fusion | flops 5464719360 | bytes 21252096 | tf_op jit(solution)/shard_map/ti,to->io/dot_general | solution.py:41
  398.3 8.3 %convolution_convert_fusion = bf16[1152,4608]{1,0:T(8,128)(2,1)} fusion(bf16[512,1152]{1,0:T(8,128)(2,1)S(1)} %copy-done.28, bf16[512,4608]{1,0:T(8,128)(2,1)S(1)} %bitcast.190), kind=kOutput, calls=%fused_computation | convolution fusion | flops 5441126400 | bytes 16515072 | tf_op jit(solution)/shard_map/ti,to->io/dot_general | solution.py:41
  406.6 8.5 %reduce-scatter.5.cloned.1.call-done = bf16[400,2048]{1,0:T(8,128)(2,1)} async-done(((bf16[3200,2048]{1,0:T(8,128)(2,1)}), bf16[400,2048]{1,0:T(8,128)(2,1)}) %reduce-scatter.5.cloned.1.call-update) | async-done | bytes 1638416 | tf_op jit(solution)/shard_map/reduce_scatter | solution.py:1045
  415.3 6.0 convolution_convert_fusion.7
  421.3 2.5 copy.48
  423.8 39.0 %attend_backward.1 = bf16[4,8,64,896]{3,2,1,0:T(8,128)(2,1)} custom-call(s32[8]{0:T(128)} %copy-done.12, s32[8]{0:T(128)} %copy-done.13, bf16[4,8,64,1536]{3,2,1,0:T(8,128)(2,1)} %bitcast.161, f32[8,8,256]{2,1,0:T(8,128)} %copy-done.10, bf16[4,8,64,288]{3,2,1,0:T(8,128)(2,1)} %copy-done.2, bf16[4,8,64,288]{3,2,1,0:T(8,128)(2,1)} %bitcast.162, ...), custom_call_target="tpu_custom_call" | custom-call | flops 1048576 | bytes 1048576 | tf_op jit(solution)/shard_map/attend_backward/pallas_call | solution.py:221
  462.8 10.2 %convolution_convert_fusion.2 = bf16[2048,1152]{1,0:T(8,128)(2,1)} fusion(bf16[2048,896]{1,0:T(8,128)(2,1)} %bitcast.149, bf16[1152,896]{1,0:T(8,128)(2,1)S(1)} %bitcast.170), kind=kOutput, calls=%fused_computation.16 | convolution fusion | flops 4230217728 | bytes 10452992 | tf_op jit(solution)/shard_map/to,io->ti/dot_general | solution.py:45
  474.2 2.9 multiply_reduce_fusion.1
  479.3 8.2 %all-reduce.14.cloned.1.call-done = bf16[400,2048]{1,0:T(8,128)(2,1)} async-done(((bf16[400,2048]{1,0:T(8,128)(2,1)}), bf16[400,2048]{1,0:T(8,128)(2,1)}) %all-reduce.14.cloned.1.call-update) | async-done | bytes 1638416 | tf_op jit(solution)/shard_map/psum | solution.py:1087
  487.5 9.9 %convolution_convert_fusion.6 = bf16[1152,896]{1,0:T(8,128)(2,1)} fusion(bf16[2048,1152]{1,0:T(8,128)(2,1)} %bitcast.184, bf16[2048,896]{1,0:T(8,128)(2,1)} %bitcast.150), kind=kOutput, calls=%fused_computation.36 | convolution fusion | flops 4228890624 | bytes 10452992 | tf_op jit(solution)/shard_map/ti,to->io/dot_general | solution.py:41
  497.4 204.7 %reduce_1.1 = (bf16[256,768]{1,0:T(8,128)(2,1)}, bf16[4,144,896]{2,1,0:T(8,128)(2,1)}, bf16[144,1152]{1,0:T(8,128)(2,1)}, bf16[576,1152]{1,0:T(8,128)(2,1)}, bf1...) custom-call(bf16[2,2,2,256,768]{4,3,2,1,0:T(8,128)(2,1)} %bitcast.165, bf16[2,2,2,144,896]{4,3,2,1,0:T(8,128)(2,1)} %bitcast.171, ...), custom_call_target="tpu_custom_call" | custom-call | bytes 524288000 | tf_op jit(solution)/shard_map/reduce_1/pallas_call | solution.py:553
  702.1 2.1 fusion.20
  704.4 4.8 bitcast_reduce_fusion
  709.5 24.4 %total_2.1 = f32[8,8,2304]{2,1,0:T(8,128)S(1)} custom-call(f32[8,2304]{1,0:T(8,128)S(1)} %fusion.41.mine_ref), custom_call_target="tpu_custom_call" | custom-call | tf_op jit(solution)/shard_map/total_2/pallas_call | solution.py:870
  734.7 3.7 fusion.28
  738.5 2.1 fusion.29
  743.7 1.5 slice_convert_fusion
  745.3 1.1 slice_convert_fusion.1
  746.4 1.3 fusion.30
  747.7 1.8 convert_element_type.244
  749.5 1.7 convert_element_type.245
  751.2 1.6 assemble.1
  752.8 0.9 convert_element_type.248
  753.7 0.9 convert_element_type.243
  (235 shorter events, 18.6 us)
Async XLA Ops:
  7.2 10.4 %copy-start = (bf16[144,6912]{1,0:T(8,128)(2,1)S(1)}, bf16[144,6912]{1,0:T(8,128)(2,1)}, u32[]{:S(2)}) copy-start(bf16[144,6912]{1,0:T(8,128)(2,1)} %param.30) | copy-start | bytes 5971972
  7.2 7.0 copy-start.55
  7.2 7.8 %copy-start.45 = (bf16[288]{0:T(512)(128)(2,1)S(1)}, bf16[288]{0:T(512)(128)(2,1)}, u32[]{:S(2)}) copy-start(bf16[288]{0:T(512)(128)(2,1)} %param.33) | copy-start | bytes 1732
  7.2 7.9 %copy-start.48 = (bf16[144]{0:T(256)(128)(2,1)S(1)}, bf16[144]{0:T(256)(128)(2,1)}, u32[]{:S(2)}) copy-start(bf16[144]{0:T(256)(128)(2,1)} %param.35) | copy-start | bytes 868
  7.2 7.9 %copy-start.44 = (bf16[576]{0:T(1024)(128)(2,1)S(1)}, bf16[576]{0:T(1024)(128)(2,1)}, u32[]{:S(2)}) copy-start(bf16[576]{0:T(1024)(128)(2,1)} %param.37) | copy-start | bytes 3460
  7.2 7.9 %copy-start.49 = (bf16[144]{0:T(256)(128)(2,1)S(1)}, bf16[144]{0:T(256)(128)(2,1)}, u32[]{:S(2)}) copy-start(bf16[144]{0:T(256)(128)(2,1)} %param.39) | copy-start | bytes 868
  7.3 8.0 %copy-start.50 = (bf16[256]{0:T(256)(128)(2,1)S(1)}, bf16[256]{0:T(256)(128)(2,1)}, u32[]{:S(2)}) copy-start(bf16[256]{0:T(256)(128)(2,1)} %param.41) | copy-start | bytes 1540
  7.3 8.0 %copy-start.51 = (bf16[256]{0:T(256)(128)(2,1)S(1)}, bf16[256]{0:T(256)(128)(2,1)}, u32[]{:S(2)}) copy-start(bf16[256]{0:T(256)(128)(2,1)} %param.43) | copy-start | bytes 1540
  7.3 258.0 %all-gather.3.cloned.1.call-start = ((), (), s32[]{:S(2)}) async-start(), calls=%async_computation.4 | async-start | bytes 5308416 | tf_op jit(solution)/shard_map/all_gather | solution.py:956
  7.3 8.0 %copy-start.52 = (bf16[96]{0:T(256)(128)(2,1)S(1)}, bf16[96]{0:T(256)(128)(2,1)}, u32[]{:S(2)}) copy-start(bf16[96]{0:T(256)(128)(2,1)} %param.45) | copy-start | bytes 580
  7.4 8.0 %copy-start.46 = (s32[64]{0:T(128)S(1)}, s32[64]{0:T(128)}, u32[]{:S(2)}) copy-start(s32[64]{0:T(128)} %param.26) | copy-start | bytes 772
  15.0 199.3 %copy-start.40 = (s32[8]{0:T(128)}, s32[8]{0:T(128)S(1)}, u32[]{:S(2)}) copy-start(s32[8]{0:T(128)S(1)} %slice.81) | copy-start | bytes 100
  15.0 4.2 copy-start.42
  15.1 4.1 copy-start.1
  15.4 3.9 copy-start.3
  15.4 3.9 copy-start.4
  15.4 3.8 copy-start.6
  15.4 3.8 copy-start.7
  162.9 110.0 %all-gather.5.cloned.1.call-start = ((), (), s32[]{:S(2)}) async-start(), calls=%async_computation.5 | async-start | bytes 9437184 | tf_op jit(solution)/shard_map/all_gather | solution.py:956
  168.8 3.6 copy-start.53
  171.5 11.4 %copy-start.13 = (s32[8]{0:T(128)}, s32[8]{0:T(128)S(1)}, u32[]{:S(2)}) copy-start(s32[8]{0:T(128)S(1)} %fusion.65.length_ref) | copy-start | bytes 100
  172.2 10.7 %copy-start.12 = (s32[8]{0:T(128)}, s32[8]{0:T(128)S(1)}, u32[]{:S(2)}) copy-start(s32[8]{0:T(128)S(1)} %get-tuple-element.49.start_ref) | copy-start | bytes 100
  200.6 1.1 copy-start.2
  202.4 11.9 %copy-start.9 = (f32[8,6912]{1,0:T(8,128)S(1)}, f32[8,6912]{1,0:T(8,128)}, u32[]{:S(2)}) copy-start(f32[8,6912]{1,0:T(8,128)} %copy-done.8) | copy-start | bytes 663556
  204.9 28.2 %all-to-all-start = ((bf16[4,512,288]{1,2,0:T(8,128)(2,1)}), bf16[4,512,288]{1,2,0:T(8,128)(2,1)}, u32[]{:S(2)}, u32[]{:S(2)}) async-start(bf16[4,512,288]{1,2,0:T(8,128)(2,1)} %copy.47), calls=%async_computation | async-start | bytes 2359296 | tf_op jit(solution)/shard_map/all_to_all | solution.py:1010
  210.3 204.8 %reduce-scatter.5.cloned.1.call-start = ((), (), s32[]{:S(2)}) async-start(), calls=%async_computation.7 | async-start | bytes 14745600 | tf_op jit(solution)/shard_map/reduce_scatter | solution.py:1045
  237.6 16.3 %copy-start.14 = (f32[512,1152]{1,0:T(8,128)}, f32[512,1152]{1,0:T(8,128)S(1)}, u32[]{:S(2)}) copy-start(f32[512,1152]{1,0:T(8,128)S(1)} %get-tuple-element.128) | copy-start | bytes 7077892
  237.6 2.4 copy-start.38
  240.0 13.9 %copy-start.27 = (bf16[512,1152]{1,0:T(8,128)(2,1)}, bf16[512,1152]{1,0:T(8,128)(2,1)S(1)}, u32[]{:S(2)}) copy-start(bf16[512,1152]{1,0:T(8,128)(2,1)S(1)} %fusion.17) | copy-start | bytes 3538948
  240.0 13.9 %slice-start = ((s8[10616832]{0:T(1024)(128)(4,1)}), s8[4194304]{0:T(1024)(128)(4,1)S(1)}, s32[]{:S(2)}) async-start(s8[10616832]{0:T(1024)(128)(4,1)} %bitcast.153), calls=%async_computation.9 | async-start | bytes 8388608
  240.0 13.9 %slice-start.1 = ((s8[10616832]{0:T(1024)(128)(4,1)}), s8[4194304]{0:T(1024)(128)(4,1)S(1)}, s32[]{:S(2)}) async-start(s8[10616832]{0:T(1024)(128)(4,1)} %bitcast.153), calls=%async_computation.10 | async-start | bytes 8388608
  240.0 13.9 %slice-start.2 = ((s8[10616832]{0:T(1024)(128)(4,1)}), s8[2228224]{0:T(1024)(128)(4,1)S(1)}, s32[]{:S(2)}) async-start(s8[10616832]{0:T(1024)(128)(4,1)} %bitcast.153), calls=%async_computation.11 | async-start | bytes 4456448
  272.9 8.6 %copy-start.31 = (bf16[512,768]{1,0:T(8,128)(2,1)S(1)}, bf16[512,768]{1,0:T(8,128)(2,1)}, u32[]{:S(2)}) copy-start(bf16[512,768]{1,0:T(8,128)(2,1)} %param.27) | copy-start | bytes 2359300
  272.9 8.6 %copy-start.54 = (bf16[8,256,768]{2,1,0:T(8,128)(2,1)S(1)}, bf16[8,256,768]{2,1,0:T(8,128)(2,1)}, u32[]{:S(2)}) copy-start(bf16[8,256,768]{2,1,0:T(8,128)(2,1)} %get-tuple-element.60) | copy-start | bytes 9437188
  281.4 3.1 copy-start.57
  284.5 3.1 copy-start.32
  284.6 3.1 copy-start.56
  292.6 10.3 %copy-start.24 = (bf16[512,1152]{1,0:T(8,128)(2,1)S(1)}, bf16[512,1152]{1,0:T(8,128)(2,1)}, u32[]{:S(2)}) copy-start(bf16[512,1152]{1,0:T(8,128)(2,1)} %get-tuple-element.129) | copy-start | bytes 3538948
  302.9 2.9 copy-start.19
  327.3 19.7 %copy-start.25 = (bf16[512,1152]{1,0:T(8,128)(2,1)}, bf16[512,1152]{1,0:T(8,128)(2,1)S(1)}, u32[]{:S(2)}) copy-start(bf16[512,1152]{1,0:T(8,128)(2,1)S(1)} %get-tuple-element.105) | copy-start | bytes 3538948
  327.3 19.7 %copy-start.15 = (f32[512,1152]{1,0:T(8,128)S(1)}, f32[512,1152]{1,0:T(8,128)}, u32[]{:S(2)}) copy-start(f32[512,1152]{1,0:T(8,128)} %copy-done.14) | copy-start | bytes 7077892
  366.1 1.4 copy-start.16
  366.1 2.7 copy-start.18
  367.8 1.0 copy-start.29
  371.6 49.8 %all-to-all-start.1 = ((bf16[4,512,288]{1,2,0:T(8,128)(2,1)}), bf16[4,512,288]{1,2,0:T(8,128)(2,1)}, u32[]{:S(2)}, u32[]{:S(2)}) async-start(bf16[4,512,288]{1,2,0:T(8,128)(2,1)} %fusion.26), calls=%async_computation.1 | async-start | bytes 2359296 | tf_op jit(solution)/shard_map/all_to_all | solution.py:1081
  380.4 107.1 %all-reduce.14.cloned.1.call-start = ((), (), s32[]{:S(2)}) async-start(), calls=%async_computation.8 | async-start | bytes 3276800 | tf_op jit(solution)/shard_map/psum | solution.py:1087
  380.4 5.0 copy-start.26
  380.4 17.9 %slice-start.3 = ((s8[4718592]{0:T(1024)(128)(4,1)}), s8[4194304]{0:T(1024)(128)(4,1)S(1)}, s32[]{:S(2)}) async-start(s8[4718592]{0:T(1024)(128)(4,1)} %bitcast.189), calls=%async_computation.12 | async-start | bytes 8388608
  385.3 12.9 %copy-start.28 = (bf16[512,1152]{1,0:T(8,128)(2,1)S(1)}, bf16[512,1152]{1,0:T(8,128)(2,1)}, u32[]{:S(2)}) copy-start(bf16[512,1152]{1,0:T(8,128)(2,1)} %copy-done.27) | copy-start | bytes 3538948
  385.3 12.9 %slice-start.4 = ((s8[4718592]{0:T(1024)(128)(4,1)}), s8[524288]{0:T(1024)(128)(4,1)S(1)}, s32[]{:S(2)}) async-start(s8[4718592]{0:T(1024)(128)(4,1)} %bitcast.189), calls=%async_computation.13 | async-start | bytes 1048576
  415.1 287.0 %reduce-scatter.3.cloned.1.call-start = ((), (), s32[]{:S(2)}) async-start(), calls=%async_computation.6 | async-start | bytes 5898240 | tf_op jit(solution)/shard_map/reduce_scatter | solution.py:1124
  423.8 39.0 %copy-start.20 = (bf16[8,144,896]{2,1,0:T(8,128)(2,1)S(1)}, bf16[8,144,896]{2,1,0:T(8,128)(2,1)}, u32[]{:S(2)}) copy-start(bf16[8,144,896]{2,1,0:T(8,128)(2,1)} %get-tuple-element.52) | copy-start | bytes 6193156
  474.2 2.9 copy-start.41
  474.2 3.5 copy-start.17
  497.4 204.7 %copy-start.36 = (f32[8,1152]{1,0:T(8,128)S(1)}, f32[8,1152]{1,0:T(8,128)}, u32[]{:S(2)}) copy-start(f32[8,1152]{1,0:T(8,128)} %get-tuple-element.112) | copy-start | bytes 110596
  704.4 29.5 %copy-start.30 = (f32[8,8,6400]{2,1,0:T(8,128)S(1)}, f32[8,8,6400]{2,1,0:T(8,128)}, u32[]{:S(2)}) copy-start(f32[8,8,6400]{2,1,0:T(8,128)} %get-tuple-element.70) | copy-start | bytes 4915204
  709.5 25.3 %copy-start.34 = (f32[64,144]{1,0:T(8,128)S(1)}, f32[64,144]{1,0:T(8,128)}, u32[]{:S(2)}) copy-start(f32[64,144]{1,0:T(8,128)} %copy-done.33) | copy-start | bytes 110596
  738.4 5.3 copy-start.21
  743.7 2.7 copy-start.47
  743.7 4.0 copy-start.23
  746.4 3.1 copy-start.22
  749.5 1.7 copy-start.5
  751.2 1.6 copy-start.35
  751.2 2.5 copy-start.37
  (6 other events, 4.0 us)
Sparse Core Ops, SparseCore 0:
  163.0 38.4 all-gather.2
  203.4 54.3 all-gather.4
  315.8 99.2 reduce-scatter.4
  417.3 70.1 all-reduce.13
  489.8 118.2 reduce-scatter.2

commit v6 on v5

--- a/solution.py
+++ b/solution.py
@@ -799,6 +799,29 @@
     )(unit_hot, rows, shares, bias_row, first_modulation, *shards)
 
 
+def pick_kernel(parts, mine, place_ref, weight_ref, out_ref):
+    width = parts * mine
+    padding = jnp.zeros((weight_ref.shape[0], out_ref.shape[1] - 3 * mine), BF)
+    for part in range(parts):
+
+        @pl.when(place_ref[0] == part)
+        def _():
+            starts = [which * width + part * mine for which in range(3)]
+            pieces = [weight_ref[:, start : start + mine] for start in starts]
+            out_ref[...] = jnp.concatenate(pieces + [padding], axis=1)
+
+
+def pick_heads(weight, place, parts, mine):
+    return pl.pallas_call(
+        partial(pick_kernel, parts, mine),
+        out_shape=jax.ShapeDtypeStruct((weight.shape[0], whole_lanes(3 * mine)), BF),
+        in_specs=[pl.BlockSpec(memory_space=pltpu.SMEM), pl.BlockSpec(memory_space=pltpu.VMEM)],
+        out_specs=pl.BlockSpec(memory_space=pltpu.VMEM),
+        compiler_params=pltpu.CompilerParams(vmem_limit_bytes=32 * 2**20),
+        name="pick_heads",
+    )(place.astype(jnp.int32).reshape(1), weight)
+
+
 def assemble_kernel(mine, parts_ref, out_ref):
     pieces = [
         parts_ref[part, :, which * mine : (which + 1) * mine].astype(F32)
@@ -947,10 +970,7 @@
     def by_row(values):
         return values.reshape(count, width)
 
-    attend_mine = lax.dynamic_slice_in_dim(
-        attend_weight.reshape(-1, 3, parts, mine), place_blk, 1, axis=2
-    ).reshape(-1, 3 * mine)
-    attend_mine = jnp.pad(attend_mine, ((0, 0), (0, whole_lanes(3 * mine) - 3 * mine)))
+    attend_mine = pick_heads(attend_weight, place_blk, parts, mine)
 
     def gather(shard):
         return lax.all_gather(shard, "img", axis=0, tiled=True)

time: 768 us -> 773 us (level)
  waiting for transfers between devices: 35.1 us -> 51.3 us
  Pallas kernels: 430 us -> 414 us
    pallas_call x1, Pallas kernels: 39 us -> 28 us  [attend_backward(): pl.pallas_call(partial(attend_backward_kernel, heads, 1.0 / math.sqrt(hea...]
    psum x1, waiting for transfers between devices: 8.22 us -> 19.1 us  [per_device(): lax.psum(early_part, 'blk')]
    reduce_scatter x1, waiting for transfers between devices: 8.47 us -> 18.1 us  [scatter(): return lax.psum_scatter(values, 'img', scatter_dimension=0, tiled=True)]
  transfers between devices with their start and end apart: 7 -> 7, of which waited for: 3 -> 3; matrix products, arithmetic and copies ran while one was open for 24% -> 24% of each run, Pallas kernels for 34% -> 32%
where the time goes in v6:
time: 773 us; the launch traced here: 769 us
  Pallas kernels  414 us (54%)
  matrix products  187 us (24%)
  waiting for transfers between devices  51.3 us (7%)
  other arithmetic  43.8 us (6%)
  local copies, waits for them, and re-layouts  42.5 us (5%)
  between operations  15.2 us (2%)
  starting transfers between devices  15 us (2%)
    pallas_call x1, Pallas kernels, reduce_call(): pl.pallas_call(partial(reduce_kernel, chunks, len(grads), ready, ring), o...  209 us
    pallas_call x1, Pallas kernels, gather_call(): pl.pallas_call(partial(gather_kernel, chunks, len(shards), 2 * rows.shape...  142 us
    dot_general x6, matrix products, right_product(): return jnp.einsum('to,io->ti', grad, weight, preferred_element_type=F32)  64 us
    dot_general x8, matrix products, dot(): return jnp.dot(left, right, preferred_element_type=F32)  56.7 us
    dot_general x6, matrix products, left_product(): jnp.einsum('ti,to->io', left, right, preferred_element_type=F32).astype(BF)  45.1 us
    pallas_call x1, Pallas kernels, attend_backward(): pl.pallas_call(partial(attend_backward_kernel, heads, 1.0 / math.sqrt(hea...  28 us
    pallas_call x1, Pallas kernels, total_call(): pl.pallas_call(total_kernel, out_shape=jax.ShapeDtypeStruct((devices, *mi...  21.3 us
    psum x1, waiting for transfers between devices, per_device(): lax.psum(early_part, 'blk')  19.1 us
  transfers between devices with their start and end apart: 7, of which 3 were waited for; matrix products, arithmetic and copies ran while one was open for 24% of the time, Pallas kernels for 32%

profile of v6, /device:TPU:9, one launch (start us, length us, event | category | flops | bytes accessed | tf_op | source)
XLA Modules:
  0.0 768.9 jit_solution(1697784414440727273)
XLA Ops:
  14.3 1.4 convolution_add_fusion.3
  15.9 1.6 convolution_bitcast_fusion.share_ref
  18.7 142.1 %gather_3.1 = (bf16[8,144,896]{2,1,0:T(8,128)(2,1)}, bf16[8,144,1152]{2,1,0:T(8,128)(2,1)}, bf16[8,144,4608]{2,1,0:T(8,128)(2,1)}, bf16[8,256,768]{2,1,0:T(8,128...) custom-call(f32[8,8]{1,0:T(8,128)S(1)} %copy-done.10, ...), custom_call_target="tpu_custom_call" | custom-call | bytes 471859200 | tf_op jit(solution)/shard_map/gather_3/pallas_call | solution.py:768
  162.2 1.3 reshape_reshape_squeeze.3
  163.6 1.3 dynamic-slice_reduce_fusion.1
  164.9 1.3 concatenate.29
  166.2 1.3 concatenate.30
  167.6 4.1 copy.49
  171.7 2.2 pad.60
  175.2 10.2 %add_convert_fusion = bf16[2048,1536]{1,0:T(8,128)(2,1)} fusion(bf16[2048,1152]{1,0:T(8,128)(2,1)S(1)} %bitcast.186, bf16[1152,1536]{0,1:T(8,128)(2,1)S(1)} %bitcast.165, f32[1536]{0:T(1024)S(1)} %bitcast_select_fusion), kind=kOutput, calls=%fused_computation.5 | convolution fusion | flops 7254048768 | bytes 14555136 | tf_op jit(solution)/shard_map/dot_general | solution.py:53
  185.5 12.6 %attend_forward.1 = (bf16[4,8,64,288]{3,2,1,0:T(8,128)(2,1)S(1)}, f32[8,8,256]{2,1,0:T(8,128)S(1)}) custom-call(s32[8]{0:T(128)S(1)} %get-tuple-element.49.start_ref, s32[8]{0:T(128)S(1)} %fusion.65.length_ref, bf16[4,8,64,1536]{3,2,1,0:T(8,128)(2,1)} %bitcast.161, bf16[512,288]{1,0:T(8,128)(2,1)S(1)} %and_convert_fusion.1.pick_ref), custom_call_target="tpu_custom_call" | custom-call | flops 10737418240 | bytes 16777216 | tf_op jit(solution)/shard_map/attend_forward/pallas_call | solution.py:193
  198.1 1.1 copy-done.2
  199.8 2.5 copy.45
  202.3 5.8 all-to-all-start
  208.8 1.4 add.337
  210.8 1.4 add.346
  212.2 1.4 add.351
  214.2 1.4 add.363
  216.2 0.9 fusion.75
  217.8 13.2 %all-to-all-done = bf16[4,512,288]{1,2,0:T(8,128)(2,1)} async-done(((bf16[4,512,288]{1,2,0:T(8,128)(2,1)}), bf16[4,512,288]{1,2,0:T(8,128)(2,1)}, u32[]{:S(2)}, u32[]{:S(2)}) %all-to-all-start) | async-done | bytes 1179680 | tf_op jit(solution)/shard_map/all_to_all | solution.py:1030
  231.0 4.4 convert_reduce_fusion.6
  235.4 1.6 multiply_reduce_fusion.4
  237.9 13.3 %fusion.107 = f32[512,4608]{1,0:T(8,128)} fusion(bf16[512,1152]{1,0:T(8,128)(2,1)S(1)} %fusion.17, bf16[1152,4608]{1,0:T(8,128)(2,1)} %bitcast.183), kind=kOutput, calls=%fused_computation.228 | convolution fusion | flops 5435817984 | bytes 21233664 | tf_op jit(solution)/shard_map/dot_general | solution.py:53
  251.2 11.4 %fusion.15 = (bf16[512,1152]{1,0:T(8,128)(2,1)}, f32[512,1152]{1,0:T(8,128)}) fusion(f32[8,1152]{1,0:T(8,128)S(1)} %get-tuple-element.115, f32[512,1152]{1,0:T(8,128)S(1)} %get-tuple-element.128, f32[8,1152]{1,0:T(8,128)S(1)} %get-tuple-element.116, bf16[512,1152]{1,0:T(8,128)(2,1)S(1)} %copy-done.1, f32[1152]{0:T(1024)S(1)} %copy-done.40, ...), kind=kOutput, calls=%fused_computation.48 | convolution fusion | flops 5463539712 | bytes 27228672 | tf_op jit(solution)/shard_map/dot_general | solution.py:53
  262.6 7.6 fusion.108
  270.2 8.6 %fusion.97 = f32[512,2048]{1,0:T(8,128)S(1)} fusion(bf16[2048,2048]{1,0:T(8,128)(2,1)} %all-gather.5.cloned.1.call-done, f32[512,2048]{1,0:T(8,128)} %fusion.108, f32[2048]{0:T(1024)S(1)} %bitcast.180), kind=kOutput, calls=%fused_computation.223 | convolution fusion | flops 4301258752 | bytes 16785408 | tf_op jit(solution)/shard_map/dot_general | solution.py:53
  278.8 2.6 multiply_reduce_fusion.8
  281.9 3.1 convert_reduce_fusion.2
  285.0 5.0 convolution_convert_fusion.3
  290.0 10.2 %convert_reduce_fusion.3 = (f32[2048]{0:T(1024)S(1)}, bf16[512,2048]{1,0:T(8,128)(2,1)S(1)}) fusion(f32[512,2048]{1,0:T(8,128)} %fusion.108, f32[2048]{0:T(1024)S(1)} %bitcast.182, bf16[512,2048]{1,0:T(8,128)(2,1)S(1)} %get-tuple-element.101, bf16[2048,2048]{1,0:T(8,128)(2,1)} %all-gather.5.cloned.1.call-done), kind=kOutput, calls=%fused_computation.30 | convolution fusion | flops 4308596736 | bytes 16793600 | tf_op jit(solution)/shard_map/to,io->ti/dot_general | solution.py:45
  300.3 2.9 convolution_convert_fusion.4
  303.2 9.8 %pad_maximum_fusion = bf16[8,400,2048]{2,1,0:T(8,128)(2,1)} fusion(bf16[8,256,2048]{2,1,0:T(8,128)(2,1)S(1)} %bitcast.159, bf16[8,144,2048]{2,1,0:T(8,128)(2,1)S(1)} %bitcast.164), kind=kLoop, calls=%fused_computation.4 | loop fusion | flops 26214400 | bytes 26214400 | tf_op jit(solution)/shard_map/concatenate | solution.py:1075
  315.1 2.3 and_convert_fusion.pick_ref
  317.6 7.7 %convert_reduce_fusion.4 = (f32[1152]{0:T(1024)S(1)}, bf16[512,1152]{1,0:T(8,128)(2,1)S(1)}, f32[512,1152]{1,0:T(8,128)}) fusion(f32[8,1152]{1,0:T(8,128)S(1)} %get-tuple-element.115, bf16[512,2048]{1,0:T(8,128)(2,1)} %copy-done.18, bf16[1152,2048]{1,0:T(8,128)(2,1)} %all-gather.3.cloned.1.call-done, bf16[512,1152]{1,0:T(8,128)(2,1)} %param.28), kind=kOutput, calls=%fused_computation.62 | convolution fusion | flops 2419457024 | bytes 11575808 | tf_op jit(solution)/shard_map/to,io->ti/dot_general | solution.py:45
  325.3 17.4 %convert_reduce_fusion = (f32[4608]{0:T(1024)S(1)}, bf16[512,4608]{1,0:T(8,128)(2,1)}) fusion(f32[512,4608]{1,0:T(8,128)} %fusion.107, f32[4608]{0:T(1024)S(1)} %copy-done.37, bf16[512,1152]{1,0:T(8,128)(2,1)S(1)} %get-tuple-element.105, bf16[4608,1152]{1,0:T(8,128)(2,1)} %bitcast.153), kind=kOutput, calls=%fused_computation.13 | convolution fusion | flops 5490077184 | bytes 25989120 | tf_op jit(solution)/shard_map/to,io->ti/dot_general | solution.py:45
  342.7 15.5 %multiply_reduce_fusion.2 = (f32[8,1152]{1,0:T(8,128)S(1)}, f32[8,64]{1,0:T(8,128)S(1)}, f32[8,64]{1,0:T(8,128)S(1)}, f32[8,1152]{1,0:T(8,128)S(1)}, f32[8,64,11...) fusion(f32[8,1152]{1,0:T(8,128)S(1)} %get-tuple-element.114, f32[8,64]{1,0:T(8,128)S(1)} %rsqrt.47, ...), kind=kOutput, calls=%fused_computation.65 | convolution fusion | flops 5442876416 | bytes 26107904 | tf_op jit(solution)/shard_map/to,io->ti/dot_general | solution.py:45
  358.2 4.0 multiply_reduce_fusion.3
  362.3 1.4 copy-done.15
  363.9 1.0 copy-done.28
  365.5 2.7 fusion.26
  368.2 8.9 %all-to-all-start.1 = ((bf16[4,512,288]{1,2,0:T(8,128)(2,1)}), bf16[4,512,288]{1,2,0:T(8,128)(2,1)}, u32[]{:S(2)}, u32[]{:S(2)}) async-start(bf16[4,512,288]{1,2,0:T(8,128)(2,1)} %fusion.26), calls=%async_computation.1 | async-start | bytes 2359296 | tf_op jit(solution)/shard_map/all_to_all | solution.py:1101
  377.1 5.0 convolution_convert_fusion.5
  382.1 12.9 %convolution_convert_fusion.1 = bf16[4608,1152]{1,0:T(8,128)(2,1)} fusion(bf16[512,1152]{1,0:T(8,128)(2,1)S(1)} %copy-done.25, f32[512,4608]{1,0:T(8,128)} %fusion.107, f32[4608]{0:T(1024)S(1)} %copy-done.37), kind=kOutput, calls=%fused_computation.1 | convolution fusion | flops 5464719360 | bytes 21252096 | tf_op jit(solution)/shard_map/ti,to->io/dot_general | solution.py:41
  395.0 8.4 %convolution_convert_fusion = bf16[1152,4608]{1,0:T(8,128)(2,1)} fusion(bf16[512,1152]{1,0:T(8,128)(2,1)S(1)} %copy-done.27, bf16[512,4608]{1,0:T(8,128)(2,1)S(1)} %bitcast.191), kind=kOutput, calls=%fused_computation | convolution fusion | flops 5441126400 | bytes 16515072 | tf_op jit(solution)/shard_map/ti,to->io/dot_general | solution.py:41
  403.3 18.1 %reduce-scatter.5.cloned.1.call-done = bf16[400,2048]{1,0:T(8,128)(2,1)} async-done(((bf16[3200,2048]{1,0:T(8,128)(2,1)}), bf16[400,2048]{1,0:T(8,128)(2,1)}) %reduce-scatter.5.cloned.1.call-update) | async-done | bytes 1638416 | tf_op jit(solution)/shard_map/reduce_scatter | solution.py:1065
  421.7 6.1 convolution_convert_fusion.7
  427.8 2.5 copy.46
  430.3 28.0 %attend_backward.1 = bf16[4,8,64,896]{3,2,1,0:T(8,128)(2,1)} custom-call(s32[8]{0:T(128)} %copy-done.11, s32[8]{0:T(128)} %copy-done.12, bf16[4,8,64,1536]{3,2,1,0:T(8,128)(2,1)} %bitcast.162, f32[8,8,256]{2,1,0:T(8,128)} %copy-done.9, bf16[4,8,64,288]{3,2,1,0:T(8,128)(2,1)} %copy-done.2, bf16[4,8,64,288]{3,2,1,0:T(8,128)(2,1)} %bitcast.163, ...), custom_call_target="tpu_custom_call" | custom-call | flops 1048576 | bytes 1048576 | tf_op jit(solution)/shard_map/attend_backward/pallas_call | solution.py:221
  458.3 10.1 %convolution_convert_fusion.2 = bf16[2048,1152]{1,0:T(8,128)(2,1)} fusion(bf16[2048,896]{1,0:T(8,128)(2,1)} %bitcast.150, bf16[1152,896]{1,0:T(8,128)(2,1)S(1)} %bitcast.171), kind=kOutput, calls=%fused_computation.16 | convolution fusion | flops 4230217728 | bytes 10452992 | tf_op jit(solution)/shard_map/to,io->ti/dot_general | solution.py:45
  469.6 2.9 multiply_reduce_fusion.1
  474.7 19.1 %all-reduce.13.cloned.1.call-done = bf16[400,2048]{1,0:T(8,128)(2,1)} async-done(((bf16[400,2048]{1,0:T(8,128)(2,1)}), bf16[400,2048]{1,0:T(8,128)(2,1)}) %all-reduce.13.cloned.1.call-update) | async-done | bytes 1638416 | tf_op jit(solution)/shard_map/psum | solution.py:1107
  493.8 9.9 %convolution_convert_fusion.6 = bf16[1152,896]{1,0:T(8,128)(2,1)} fusion(bf16[2048,1152]{1,0:T(8,128)(2,1)} %bitcast.185, bf16[2048,896]{1,0:T(8,128)(2,1)} %bitcast.151), kind=kOutput, calls=%fused_computation.36 | convolution fusion | flops 4228890624 | bytes 10452992 | tf_op jit(solution)/shard_map/ti,to->io/dot_general | solution.py:41
  503.7 208.7 %reduce_1.1 = (bf16[256,768]{1,0:T(8,128)(2,1)}, bf16[4,144,896]{2,1,0:T(8,128)(2,1)}, bf16[144,1152]{1,0:T(8,128)(2,1)}, bf16[576,1152]{1,0:T(8,128)(2,1)}, bf1...) custom-call(bf16[2,2,2,256,768]{4,3,2,1,0:T(8,128)(2,1)} %bitcast.166, bf16[2,2,2,144,896]{4,3,2,1,0:T(8,128)(2,1)} %bitcast.172, ...), custom_call_target="tpu_custom_call" | custom-call | bytes 524288000 | tf_op jit(solution)/shard_map/reduce_1/pallas_call | solution.py:553
  712.5 2.1 fusion.20
  714.8 4.8 bitcast_reduce_fusion
  719.9 21.3 %total_2.1 = f32[8,8,2304]{2,1,0:T(8,128)S(1)} custom-call(f32[8,2304]{1,0:T(8,128)S(1)} %fusion.41.mine_ref), custom_call_target="tpu_custom_call" | custom-call | tf_op jit(solution)/shard_map/total_2/pallas_call | solution.py:893
  742.0 3.7 fusion.28
  745.7 2.1 fusion.29
  751.0 1.5 slice_convert_fusion
  752.6 1.1 slice_convert_fusion.1
  753.7 1.3 fusion.30
  755.0 1.8 convert_element_type.242
  756.8 1.7 convert_element_type.243
  758.5 1.6 assemble.1
  (244 shorter events, 28.9 us)
Async XLA Ops:
  7.2 8.6 %copy-start = (bf16[144,6912]{1,0:T(8,128)(2,1)S(1)}, bf16[144,6912]{1,0:T(8,128)(2,1)}, u32[]{:S(2)}) copy-start(bf16[144,6912]{1,0:T(8,128)(2,1)} %param.30) | copy-start | bytes 5971972
  7.2 255.4 %all-gather.3.cloned.1.call-start = ((), (), s32[]{:S(2)}) async-start(), calls=%async_computation.4 | async-start | bytes 5308416 | tf_op jit(solution)/shard_map/all_gather | solution.py:976
  8.8 5.4 copy-start.49
  14.3 3.2 copy-start.6
  14.3 3.3 copy-start.52
  15.8 1.7 copy-start.32
  15.8 1.9 copy-start.1
  15.8 2.3 copy-start.3
  15.8 2.7 copy-start.4
  15.8 2.8 copy-start.7
  15.8 2.9 copy-start.8
  15.8 2.9 copy-start.10
  160.9 109.3 %all-gather.5.cloned.1.call-start = ((), (), s32[]{:S(2)}) async-start(), calls=%async_computation.5 | async-start | bytes 9437184 | tf_op jit(solution)/shard_map/all_gather | solution.py:976
  171.7 2.3 copy-start.54
  171.7 2.3 copy-start.55
  171.7 2.4 copy-start.50
  171.7 3.5 copy-start.60
  174.0 11.5 %copy-start.41 = (s32[288]{0:T(512)}, s32[288]{0:T(512)S(1)}, u32[]{:S(2)}) copy-start(s32[288]{0:T(512)S(1)} %get-tuple-element.135) | copy-start | bytes 3460
  174.0 11.5 %copy-start.43 = (s32[288]{0:T(512)}, s32[288]{0:T(512)S(1)}, u32[]{:S(2)}) copy-start(s32[288]{0:T(512)S(1)} %get-tuple-element.134) | copy-start | bytes 3460
  174.0 11.4 %copy-start.45 = (s32[512]{0:T(512)}, s32[512]{0:T(512)S(1)}, u32[]{:S(2)}) copy-start(s32[512]{0:T(512)S(1)} %get-tuple-element.136) | copy-start | bytes 6148
  174.0 11.4 %copy-start.47 = (s32[512]{0:T(512)}, s32[512]{0:T(512)S(1)}, u32[]{:S(2)}) copy-start(s32[512]{0:T(512)S(1)} %get-tuple-element.137) | copy-start | bytes 6148
  174.3 11.2 %copy-start.12 = (s32[8]{0:T(128)}, s32[8]{0:T(128)S(1)}, u32[]{:S(2)}) copy-start(s32[8]{0:T(128)S(1)} %fusion.65.length_ref) | copy-start | bytes 100
  175.0 10.5 %copy-start.11 = (s32[8]{0:T(128)}, s32[8]{0:T(128)S(1)}, u32[]{:S(2)}) copy-start(s32[8]{0:T(128)S(1)} %get-tuple-element.49.start_ref) | copy-start | bytes 100
  202.3 28.7 %all-to-all-start = ((bf16[4,512,288]{1,2,0:T(8,128)(2,1)}), bf16[4,512,288]{1,2,0:T(8,128)(2,1)}, u32[]{:S(2)}, u32[]{:S(2)}) async-start(bf16[4,512,288]{1,2,0:T(8,128)(2,1)} %copy.45), calls=%async_computation | async-start | bytes 2359296 | tf_op jit(solution)/shard_map/all_to_all | solution.py:1030
  208.1 213.4 %reduce-scatter.5.cloned.1.call-start = ((), (), s32[]{:S(2)}) async-start(), calls=%async_computation.7 | async-start | bytes 14745600 | tf_op jit(solution)/shard_map/reduce_scatter | solution.py:1065
  235.4 15.8 %copy-start.13 = (f32[512,1152]{1,0:T(8,128)}, f32[512,1152]{1,0:T(8,128)S(1)}, u32[]{:S(2)}) copy-start(f32[512,1152]{1,0:T(8,128)S(1)} %get-tuple-element.128) | copy-start | bytes 7077892
  235.4 2.4 copy-start.38
  237.8 13.4 %copy-start.26 = (bf16[512,1152]{1,0:T(8,128)(2,1)}, bf16[512,1152]{1,0:T(8,128)(2,1)S(1)}, u32[]{:S(2)}) copy-start(bf16[512,1152]{1,0:T(8,128)(2,1)S(1)} %fusion.17) | copy-start | bytes 3538948
  237.8 13.4 %slice-start = ((s8[10616832]{0:T(1024)(128)(4,1)}), s8[4194304]{0:T(1024)(128)(4,1)S(1)}, s32[]{:S(2)}) async-start(s8[10616832]{0:T(1024)(128)(4,1)} %bitcast.154), calls=%async_computation.9 | async-start | bytes 8388608
  237.8 13.4 %slice-start.1 = ((s8[10616832]{0:T(1024)(128)(4,1)}), s8[4194304]{0:T(1024)(128)(4,1)S(1)}, s32[]{:S(2)}) async-start(s8[10616832]{0:T(1024)(128)(4,1)} %bitcast.154), calls=%async_computation.10 | async-start | bytes 8388608
  237.8 13.4 %slice-start.2 = ((s8[10616832]{0:T(1024)(128)(4,1)}), s8[2228224]{0:T(1024)(128)(4,1)S(1)}, s32[]{:S(2)}) async-start(s8[10616832]{0:T(1024)(128)(4,1)} %bitcast.154), calls=%async_computation.11 | async-start | bytes 4456448
  237.8 13.4 %copy-start.37 = (f32[4608]{0:T(1024)S(1)}, f32[4608]{0:T(1024)}, u32[]{:S(2)}) copy-start(f32[4608]{0:T(1024)} %add.346) | copy-start | bytes 55300
  237.8 13.4 %copy-start.40 = (f32[1152]{0:T(1024)S(1)}, f32[1152]{0:T(1024)}, u32[]{:S(2)}) copy-start(f32[1152]{0:T(1024)} %add.351) | copy-start | bytes 13828
  262.6 7.6 copy-start.57
  270.2 8.6 %copy-start.30 = (bf16[512,768]{1,0:T(8,128)(2,1)S(1)}, bf16[512,768]{1,0:T(8,128)(2,1)}, u32[]{:S(2)}) copy-start(bf16[512,768]{1,0:T(8,128)(2,1)} %param.27) | copy-start | bytes 2359300
  270.2 8.6 %copy-start.56 = (f32[8,1,256]{2,1,0:T(1,128)S(1)}, f32[8,1,256]{2,1,0:T(1,128)}, u32[]{:S(2)}) copy-start(f32[8,1,256]{2,1,0:T(1,128)} %get-tuple-element.117) | copy-start | bytes 24580
  270.2 8.6 %copy-start.58 = (f32[768]{0:T(1024)S(1)}, f32[768]{0:T(1024)}, u32[]{:S(2)}) copy-start(f32[768]{0:T(1024)} %add.363) | copy-start | bytes 9220
  270.2 8.6 %copy-start.61 = (bf16[8,256,768]{2,1,0:T(8,128)(2,1)S(1)}, bf16[8,256,768]{2,1,0:T(8,128)(2,1)}, u32[]{:S(2)}) copy-start(bf16[8,256,768]{2,1,0:T(8,128)(2,1)} %get-tuple-element.60) | copy-start | bytes 9437188
  278.8 3.2 copy-start.63
  281.9 3.1 copy-start.31
  281.9 3.1 copy-start.62
  290.0 10.3 %copy-start.23 = (bf16[512,1152]{1,0:T(8,128)(2,1)S(1)}, bf16[512,1152]{1,0:T(8,128)(2,1)}, u32[]{:S(2)}) copy-start(bf16[512,1152]{1,0:T(8,128)(2,1)} %get-tuple-element.129) | copy-start | bytes 3538948
  300.2 2.9 copy-start.18
  325.3 17.4 %copy-start.24 = (bf16[512,1152]{1,0:T(8,128)(2,1)}, bf16[512,1152]{1,0:T(8,128)(2,1)S(1)}, u32[]{:S(2)}) copy-start(bf16[512,1152]{1,0:T(8,128)(2,1)S(1)} %get-tuple-element.105) | copy-start | bytes 3538948
  325.3 17.4 %copy-start.14 = (f32[512,1152]{1,0:T(8,128)S(1)}, f32[512,1152]{1,0:T(8,128)}, u32[]{:S(2)}) copy-start(f32[512,1152]{1,0:T(8,128)} %copy-done.13) | copy-start | bytes 7077892
  362.2 3.2 copy-start.17
  368.2 59.6 %all-to-all-start.1 = ((bf16[4,512,288]{1,2,0:T(8,128)(2,1)}), bf16[4,512,288]{1,2,0:T(8,128)(2,1)}, u32[]{:S(2)}, u32[]{:S(2)}) async-start(bf16[4,512,288]{1,2,0:T(8,128)(2,1)} %fusion.26), calls=%async_computation.1 | async-start | bytes 2359296 | tf_op jit(solution)/shard_map/all_to_all | solution.py:1101
  377.1 116.8 %all-reduce.13.cloned.1.call-start = ((), (), s32[]{:S(2)}) async-start(), calls=%async_computation.8 | async-start | bytes 3276800 | tf_op jit(solution)/shard_map/psum | solution.py:1107
  377.1 5.0 copy-start.25
  377.1 17.9 %slice-start.3 = ((s8[4718592]{0:T(1024)(128)(4,1)}), s8[4194304]{0:T(1024)(128)(4,1)S(1)}, s32[]{:S(2)}) async-start(s8[4718592]{0:T(1024)(128)(4,1)} %bitcast.190), calls=%async_computation.12 | async-start | bytes 8388608
  382.1 12.9 %copy-start.27 = (bf16[512,1152]{1,0:T(8,128)(2,1)S(1)}, bf16[512,1152]{1,0:T(8,128)(2,1)}, u32[]{:S(2)}) copy-start(bf16[512,1152]{1,0:T(8,128)(2,1)} %copy-done.26) | copy-start | bytes 3538948
  382.1 12.9 %slice-start.4 = ((s8[4718592]{0:T(1024)(128)(4,1)}), s8[524288]{0:T(1024)(128)(4,1)S(1)}, s32[]{:S(2)}) async-start(s8[4718592]{0:T(1024)(128)(4,1)} %bitcast.190), calls=%async_computation.13 | async-start | bytes 1048576
  421.5 290.9 %reduce-scatter.3.cloned.1.call-start = ((), (), s32[]{:S(2)}) async-start(), calls=%async_computation.6 | async-start | bytes 5898240 | tf_op jit(solution)/shard_map/reduce_scatter | solution.py:1144
  430.3 28.0 %copy-start.19 = (bf16[8,144,896]{2,1,0:T(8,128)(2,1)S(1)}, bf16[8,144,896]{2,1,0:T(8,128)(2,1)}, u32[]{:S(2)}) copy-start(bf16[8,144,896]{2,1,0:T(8,128)(2,1)} %get-tuple-element.52) | copy-start | bytes 6193156
  469.6 2.9 copy-start.51
  469.6 3.5 copy-start.16
  503.7 208.7 %copy-start.35 = (f32[8,1152]{1,0:T(8,128)S(1)}, f32[8,1152]{1,0:T(8,128)}, u32[]{:S(2)}) copy-start(f32[8,1152]{1,0:T(8,128)} %get-tuple-element.112) | copy-start | bytes 110596
  714.8 26.4 %copy-start.29 = (f32[8,8,6400]{2,1,0:T(8,128)S(1)}, f32[8,8,6400]{2,1,0:T(8,128)}, u32[]{:S(2)}) copy-start(f32[8,8,6400]{2,1,0:T(8,128)} %get-tuple-element.70) | copy-start | bytes 4915204
  719.9 22.2 %copy-start.33 = (f32[64,144]{1,0:T(8,128)S(1)}, f32[64,144]{1,0:T(8,128)}, u32[]{:S(2)}) copy-start(f32[64,144]{1,0:T(8,128)} %copy-done.32) | copy-start | bytes 110596
  745.7 5.3 copy-start.20
  751.0 2.7 copy-start.59
  751.0 4.0 copy-start.22
  753.7 3.1 copy-start.21
  758.5 2.5 copy-start.36
  (12 other events, 13.4 us)
Sparse Core Ops, SparseCore 0:
  161.0 38.4 all-gather.2
  201.4 54.3 all-gather.4
  313.2 108.2 reduce-scatter.4
  423.7 70.0 all-reduce.12
  496.1 119.7 reduce-scatter.2
